TPU v7x, 32 devices: a whole 2x2x4 slice. The times are simulated.
32 devices in a mesh: dp: 8 (over z, y), row: 2 (over x), col: 2 (over core).
Axes of the slice: x: 2, y: 2, z: 4, core: 2. Of those that a mesh axis runs over, the one named last changes fastest.
Arguments:
- tokens: bfloat16 [10240, 1536], P(('dp', 'row', 'col')), may hold values from -6 to 6
- attn_gain: float32 [1536], replicated, may hold values from 0.1 to 1.9
- query_weight: bfloat16 [1536, 1536], P(None, ('row', 'col')), may hold values from -0.15625 to 0.15625
- key_weight: bfloat16 [1536, 512], P(None, ('row', 'col')), may hold values from -0.15625 to 0.15625
- value_weight: bfloat16 [1536, 512], P(None, ('row', 'col')), may hold values from -0.15625 to 0.15625
- out_weight: bfloat16 [1536, 1536], P(('row', 'col')), may hold values from -2.5 to 2.5
- mlp_gain: float32 [1536], replicated, may hold values from 0.1 to 1.9
- router_weight: bfloat16 [1536, 16], replicated, may hold values from -0.078125 to 0.078125
- gate_weight: bfloat16 [16, 1536, 512], P('dp', None, ('row', 'col')), may hold values from -0.15625 to 0.15625
- up_weight: bfloat16 [16, 1536, 512], P('dp', None, ('row', 'col')), may hold values from -0.15625 to 0.15625
- down_weight: bfloat16 [16, 512, 1536], P('dp', ('row', 'col')), may hold values from -0.75 to 0.75
- output_grad: bfloat16 [10240, 1536], P(('dp', 'row', 'col')), may hold values from -6 to 6
- expert_ids: int32 [10240, 8], P(('dp', 'row', 'col')), may hold values from 0 to 15, all different within a row
- slot_rank: int32 [10240, 8], P(('dp', 'row', 'col')), may hold values from 0 to 2559, as said below
- segment_ids: int32 [10240], P(('dp', 'row', 'col')), may hold values from 0 to 12, as said below
- parent_ids: int32 [10240], P(('dp', 'row', 'col')), may hold values from 0 to 4, as said below
Outputs:
- output: bfloat16 [10240, 1536], P(('dp', 'row', 'col'))
- input_grad: float32 [10240, 1536], P(('dp', 'row', 'col'))
- attn_gain_grad: float32 [1536], replicated
- query_grad: float32 [1536, 1536], P(None, ('row', 'col'))
- key_grad: float32 [1536, 512], P(None, ('row', 'col'))
- value_grad: float32 [1536, 512], P(None, ('row', 'col'))
- out_grad: float32 [1536, 1536], P(('row', 'col'))
- mlp_gain_grad: float32 [1536], replicated
- router_grad: float32 [1536, 16], replicated
- gate_grad: float32 [16, 1536, 512], P('dp', None, ('row', 'col'))
- up_grad: float32 [16, 1536, 512], P('dp', None, ('row', 'col'))
- down_grad: float32 [16, 512, 1536], P('dp', ('row', 'col'))
Inputs may be any that keep to these rules, and one draw needn't show every extreme that they name: `segment_ids`: within each aligned block of 1280 tokens (one tree), segment 0 (the trunk) holds the first 512 tokens; segments 1 to 4 (branches) and 5 to 12 (leaves) hold 64 consecutive tokens each, in an order that varies. `parent_ids`: each token's segment's parent: 0 for the trunk and the branches, a branch for a leaf; each branch is the parent of two leaves; equal for all tokens of a segment. `slot_rank`: over the 320 rows of one device, a permutation of 0 to 2559.
All inputs are finite; a program needn't handle non-finite values.
Results may differ from a plain program's by a relative error of at most 0.019.
Values may be sent and summed in bfloat16 or wider, within the bound.
No kernel may reach another device: no remote copies, remote signals or barrier semaphores. Data moves between devices by JAX's collectives and lax.ppermute only.
A program may use at most 256 MiB of HBM per device.

v0:
```python
import math

import jax
import jax.numpy as jnp
from jax import lax
from jax.sharding import PartitionSpec as P

HD = 64
TOPK = 8


EPS = 1e-05
segment_count = 13


def rms_scale(values):
    return lax.rsqrt(jnp.mean(values * values, axis=-1, keepdims=True) + EPS)


def norm_back(grad_normed, values, scale_rows, gain):
    weighted = grad_normed * gain
    grad_gain = jnp.sum(grad_normed * values * scale_rows, axis=0)
    inner = jnp.mean(weighted * values, axis=-1, keepdims=True)
    return (
        scale_rows * weighted - values * scale_rows * scale_rows * scale_rows * inner,
        grad_gain,
    )


def grand_parents(segment, parent):
    labels = jnp.arange(segment_count, dtype=jnp.int32)
    parent_table = jnp.max(
        jnp.where(segment[None, :] == labels[:, None], parent[None, :], 0), axis=1
    )
    return jnp.sum(jnp.where(parent[:, None] == labels[None, :], parent_table[None, :], 0), axis=1)


def block_visible(segment, parent, grand, position, first_row, block_rows):
    query_segment = lax.dynamic_slice_in_dim(segment, first_row, block_rows, 0)[:, None]
    query_parent = lax.dynamic_slice_in_dim(parent, first_row, block_rows, 0)[:, None]
    query_grand = lax.dynamic_slice_in_dim(grand, first_row, block_rows, 0)[:, None]
    query_position = lax.dynamic_slice_in_dim(position, first_row, block_rows, 0)[:, None]
    key_segment = segment[None, :]
    same_segment = (key_segment == query_segment) & (position[None, :] <= query_position)
    from_parent = (key_segment == query_parent) & (key_segment != query_segment)
    from_grand = (
        (key_segment == query_grand)
        & (key_segment != query_segment)
        & (key_segment != query_parent)
    )
    return same_segment | from_parent | from_grand


def attend_forward(query_heads, key_heads, value_heads, segment, parent, grand, block_rows):
    total_rows = query_heads.shape[0]
    position = jnp.arange(total_rows, dtype=jnp.int32)
    score_scale = 1.0 / math.sqrt(HD)

    def one_block(block_index):
        first_row = block_index * block_rows
        query_block = lax.dynamic_slice_in_dim(query_heads, first_row, block_rows, 0)
        visible = block_visible(segment, parent, grand, position, first_row, block_rows)
        scores = (
            jnp.einsum("qgrd,kgd->grqk", query_block, key_heads, preferred_element_type=jnp.float32)
            * score_scale
        )
        scores = jnp.where(visible, scores, -jnp.inf)
        row_max = jnp.max(scores, axis=-1, keepdims=True)
        weights = jnp.exp(scores - row_max)
        row_total = jnp.sum(weights, axis=-1, keepdims=True)
        probabilities = (weights / row_total).astype(jnp.bfloat16)
        result = jnp.einsum(
            "grqk,kgd->qgrd", probabilities, value_heads, preferred_element_type=jnp.float32
        )
        return (result.astype(jnp.bfloat16), (row_max + jnp.log(row_total))[..., 0])

    outputs, log_total = lax.map(one_block, jnp.arange(total_rows // block_rows))
    return (outputs.reshape(query_heads.shape), log_total)


def attend_backward(
    query_heads, key_heads, value_heads, grad_heads, segment, parent, grand, log_total, block_rows
):
    total_rows = query_heads.shape[0]
    position = jnp.arange(total_rows, dtype=jnp.int32)
    score_scale = 1.0 / math.sqrt(HD)

    def one_block(running, block_index):
        grad_keys, grad_values = running
        first_row = block_index * block_rows
        query_block = lax.dynamic_slice_in_dim(query_heads, first_row, block_rows, 0)
        grad_block = lax.dynamic_slice_in_dim(grad_heads, first_row, block_rows, 0)
        visible = block_visible(segment, parent, grand, position, first_row, block_rows)
        scores = (
            jnp.einsum("qgrd,kgd->grqk", query_block, key_heads, preferred_element_type=jnp.float32)
            * score_scale
        )
        probabilities = jnp.where(visible, jnp.exp(scores - log_total[block_index][..., None]), 0.0)
        low_probs = probabilities.astype(jnp.bfloat16)
        grad_probs = jnp.einsum(
            "qgrd,kgd->grqk", grad_block, value_heads, preferred_element_type=jnp.float32
        )
        row_delta = jnp.sum(grad_probs * probabilities, axis=-1, keepdims=True)
        grad_scores = (probabilities * (grad_probs - row_delta)).astype(jnp.bfloat16)
        grad_query = (
            jnp.einsum("grqk,kgd->qgrd", grad_scores, key_heads, preferred_element_type=jnp.float32)
            * score_scale
        )
        grad_keys = (
            grad_keys
            + jnp.einsum(
                "grqk,qgrd->kgd", grad_scores, query_block, preferred_element_type=jnp.float32
            )
            * score_scale
        )
        grad_values = grad_values + jnp.einsum(
            "grqk,qgrd->kgd", low_probs, grad_block, preferred_element_type=jnp.float32
        )
        return ((grad_keys, grad_values), grad_query.astype(jnp.bfloat16))

    empty_grad = jnp.zeros(key_heads.shape, jnp.float32)
    sums, grad_query = lax.scan(
        one_block, (empty_grad, empty_grad), jnp.arange(total_rows // block_rows)
    )
    return (
        grad_query.reshape(query_heads.shape),
        sums[0].astype(jnp.bfloat16),
        sums[1].astype(jnp.bfloat16),
    )


def shards(
    tokens,
    attn_gain,
    query_weight,
    key_weight,
    value_weight,
    out_weight,
    mlp_gain,
    router_weight,
    gate_weight,
    up_weight,
    down_weight,
    output_grad,
    expert_ids,
    slot_rank,
    segment_ids,
    parent_ids,
):
    local_rows = tokens.shape[0]
    width = tokens.shape[1]
    group_size = lax.axis_size(("row", "col"))
    tree_rows = local_rows * group_size
    kv_local = key_weight.shape[1] // HD
    per_group = query_weight.shape[1] // key_weight.shape[1]
    experts_local = gate_weight.shape[0]
    experts_all = experts_local * lax.axis_size("dp")
    capacity = 5 * local_rows * TOPK // (4 * experts_all)
    block_rows = math.gcd(tree_rows, 512)
    full_gate, full_up, full_down = (
        lax.all_gather(gate_weight, ("row", "col"), axis=2, tiled=True),
        lax.all_gather(up_weight, ("row", "col"), axis=2, tiled=True),
        lax.all_gather(down_weight, ("row", "col"), axis=1, tiled=True),
    )
    token_values = tokens.astype(jnp.float32)
    scale_attn = rms_scale(token_values)
    normed = (token_values * scale_attn * attn_gain).astype(jnp.bfloat16)
    tree_normed, tree_segment, tree_parent = (
        lax.all_gather(normed, ("row", "col"), axis=0, tiled=True),
        lax.all_gather(segment_ids, ("row", "col"), axis=0, tiled=True),
        lax.all_gather(parent_ids, ("row", "col"), axis=0, tiled=True),
    )
    grand = grand_parents(tree_segment, tree_parent)
    queries = jnp.dot(tree_normed, query_weight, preferred_element_type=jnp.float32).astype(
        jnp.bfloat16
    )
    key_rows = jnp.dot(tree_normed, key_weight, preferred_element_type=jnp.float32).astype(
        jnp.bfloat16
    )
    value_rows = jnp.dot(tree_normed, value_weight, preferred_element_type=jnp.float32).astype(
        jnp.bfloat16
    )
    query_heads = queries.reshape(tree_rows, kv_local, per_group, HD)
    key_heads = key_rows.reshape(tree_rows, kv_local, HD)
    value_heads = value_rows.reshape(tree_rows, kv_local, HD)
    heads_out, log_total = attend_forward(
        query_heads, key_heads, value_heads, tree_segment, tree_parent, grand, block_rows
    )
    attn_heads = heads_out.reshape(tree_rows, -1)
    attn_result = lax.psum_scatter(
        jnp.dot(attn_heads, out_weight, preferred_element_type=jnp.float32),
        ("row", "col"),
        scatter_dimension=0,
        tiled=True,
    )
    hidden = token_values + attn_result
    scale_mlp = rms_scale(hidden)
    mlp_in = (hidden * scale_mlp * mlp_gain).astype(jnp.bfloat16)
    logits = jnp.dot(mlp_in, router_weight, preferred_element_type=jnp.float32)
    chosen = jnp.take_along_axis(logits, expert_ids, axis=1)
    chosen_max = jnp.max(chosen, axis=1, keepdims=True)
    chosen_exp = jnp.exp(chosen - chosen_max)
    gates = chosen_exp / jnp.sum(chosen_exp, axis=1, keepdims=True)
    flat_expert = expert_ids.reshape(-1)
    flat_rank = slot_rank.reshape(-1)
    earlier = (flat_expert[None, :] == flat_expert[:, None]) & (
        flat_rank[None, :] < flat_rank[:, None]
    )
    slot_number = jnp.sum(earlier.astype(jnp.int32), axis=1)
    kept_flat = slot_number < capacity
    target = jnp.where(kept_flat, flat_expert * capacity + slot_number, experts_all * capacity)
    safe_target = jnp.minimum(target, experts_all * capacity - 1)
    kept_pairs = kept_flat.reshape(local_rows, TOPK).astype(jnp.float32)
    source_rows = jnp.repeat(mlp_in, TOPK, axis=0)
    dispatch_rows = (
        jnp.zeros((experts_all * capacity, width), jnp.bfloat16)
        .at[target]
        .set(source_rows, mode="drop")
    )
    expert_rows = lax.all_to_all(
        dispatch_rows.reshape(experts_all, capacity, width),
        "dp",
        split_axis=0,
        concat_axis=1,
        tiled=True,
    )
    gate_pre = jnp.einsum(
        "erd,edf->erf", expert_rows, full_gate, preferred_element_type=jnp.float32
    )
    up_pre = jnp.einsum("erd,edf->erf", expert_rows, full_up, preferred_element_type=jnp.float32)
    sigmoid_gate = jax.nn.sigmoid(gate_pre)
    silu_gate = gate_pre * sigmoid_gate
    activated = (silu_gate * up_pre).astype(jnp.bfloat16)
    expert_out = jnp.einsum(
        "erf,efd->erd", activated, full_down, preferred_element_type=jnp.float32
    ).astype(jnp.bfloat16)
    returned = lax.all_to_all(expert_out, "dp", split_axis=1, concat_axis=0, tiled=True).reshape(
        experts_all * capacity, width
    )
    pair_out = returned[safe_target].reshape(local_rows, TOPK, width)
    pair_weight = gates * kept_pairs
    mixture = jnp.sum(pair_weight[..., None] * pair_out, axis=1)
    output = (hidden + mixture).astype(jnp.bfloat16)
    grad_top = output_grad.astype(jnp.float32)
    grad_gates = jnp.sum(grad_top[:, None, :] * pair_out, axis=2) * kept_pairs
    slot_grad = (
        (pair_weight[..., None] * grad_top[:, None, :]).astype(jnp.bfloat16).reshape(-1, width)
    )
    grad_dispatch = (
        jnp.zeros((experts_all * capacity, width), jnp.bfloat16)
        .at[target]
        .set(slot_grad, mode="drop")
    )
    grad_expert_out = lax.all_to_all(
        grad_dispatch.reshape(experts_all, capacity, width),
        "dp",
        split_axis=0,
        concat_axis=1,
        tiled=True,
    )
    grad_act = jnp.einsum(
        "erd,efd->erf", grad_expert_out, full_down, preferred_element_type=jnp.float32
    )
    down_full = jnp.einsum(
        "erf,erd->efd", activated, grad_expert_out, preferred_element_type=jnp.float32
    )
    grad_gate_pre = (
        grad_act * up_pre * sigmoid_gate * (1.0 + gate_pre * (1.0 - sigmoid_gate))
    ).astype(jnp.bfloat16)
    grad_up_pre = (grad_act * silu_gate).astype(jnp.bfloat16)
    grad_rows = jnp.einsum(
        "erf,edf->erd", grad_gate_pre, full_gate, preferred_element_type=jnp.float32
    )
    grad_rows = (
        grad_rows
        + jnp.einsum("erf,edf->erd", grad_up_pre, full_up, preferred_element_type=jnp.float32)
    ).astype(jnp.bfloat16)
    gate_full = jnp.einsum(
        "erd,erf->edf", expert_rows, grad_gate_pre, preferred_element_type=jnp.float32
    )
    up_full = jnp.einsum(
        "erd,erf->edf", expert_rows, grad_up_pre, preferred_element_type=jnp.float32
    )
    grad_back = lax.all_to_all(grad_rows, "dp", split_axis=1, concat_axis=0, tiled=True).reshape(
        experts_all * capacity, width
    )
    pair_back = grad_back[safe_target].reshape(local_rows, TOPK, width)
    grad_mlp_in = jnp.sum(pair_back * kept_pairs[..., None], axis=1)
    weighted_sum = jnp.sum(gates * grad_gates, axis=1, keepdims=True)
    grad_choice = gates * (grad_gates - weighted_sum)
    columns = jnp.arange(experts_all, dtype=jnp.int32)
    grad_logits = jnp.sum(
        jnp.where(expert_ids[..., None] == columns, grad_choice[..., None], 0.0), axis=1
    ).astype(jnp.bfloat16)
    grad_mlp_in = grad_mlp_in + jnp.dot(
        grad_logits, router_weight.T, preferred_element_type=jnp.float32
    )
    router_part = jnp.dot(mlp_in.T, grad_logits, preferred_element_type=jnp.float32)
    grad_hidden_norm, mlp_gain_part = norm_back(grad_mlp_in, hidden, scale_mlp, mlp_gain)
    grad_hidden = grad_top + grad_hidden_norm
    grad_attn = grad_hidden.astype(jnp.bfloat16)
    tree_grad_attn = lax.all_gather(grad_attn, ("row", "col"), axis=0, tiled=True)
    grad_heads = jnp.dot(tree_grad_attn, out_weight.T, preferred_element_type=jnp.float32).astype(
        jnp.bfloat16
    )
    out_part = jnp.dot(attn_heads.T, tree_grad_attn, preferred_element_type=jnp.float32)
    grad_query_heads, grad_key_heads, grad_value_heads = attend_backward(
        query_heads,
        key_heads,
        value_heads,
        grad_heads.reshape(query_heads.shape),
        tree_segment,
        tree_parent,
        grand,
        log_total,
        block_rows,
    )
    grad_queries = grad_query_heads.reshape(tree_rows, -1)
    grad_keys = grad_key_heads.reshape(tree_rows, -1)
    grad_values = grad_value_heads.reshape(tree_rows, -1)
    query_part = jnp.dot(tree_normed.T, grad_queries, preferred_element_type=jnp.float32)
    key_part = jnp.dot(tree_normed.T, grad_keys, preferred_element_type=jnp.float32)
    value_part = jnp.dot(tree_normed.T, grad_values, preferred_element_type=jnp.float32)
    summed = jnp.dot(grad_queries, query_weight.T, preferred_element_type=jnp.float32)
    summed = summed + jnp.dot(grad_keys, key_weight.T, preferred_element_type=jnp.float32)
    grad_normed = lax.psum_scatter(
        (summed + jnp.dot(grad_values, value_weight.T, preferred_element_type=jnp.float32)).astype(
            jnp.bfloat16
        ),
        ("row", "col"),
        scatter_dimension=0,
        tiled=True,
    ).astype(jnp.float32)
    grad_token_norm, attn_gain_part = norm_back(grad_normed, token_values, scale_attn, attn_gain)
    input_grad = grad_hidden + grad_token_norm
    query_grad, key_grad, value_grad, out_grad = (
        lax.psum(query_part.astype(jnp.bfloat16), "dp").astype(jnp.float32),
        lax.psum(key_part.astype(jnp.bfloat16), "dp").astype(jnp.float32),
        lax.psum(value_part.astype(jnp.bfloat16), "dp").astype(jnp.float32),
        lax.psum(out_part.astype(jnp.bfloat16), "dp").astype(jnp.float32),
    )
    gate_grad, up_grad, down_grad = (
        lax.psum_scatter(
            gate_full.astype(jnp.bfloat16), ("row", "col"), scatter_dimension=2, tiled=True
        ).astype(jnp.float32),
        lax.psum_scatter(
            up_full.astype(jnp.bfloat16), ("row", "col"), scatter_dimension=2, tiled=True
        ).astype(jnp.float32),
        lax.psum_scatter(
            down_full.astype(jnp.bfloat16), ("row", "col"), scatter_dimension=1, tiled=True
        ).astype(jnp.float32),
    )
    attn_gain_grad, mlp_gain_grad, router_grad = lax.psum(
        (attn_gain_part, mlp_gain_part, router_part), ("dp", "row", "col")
    )
    return (
        output,
        input_grad,
        attn_gain_grad,
        query_grad,
        key_grad,
        value_grad,
        out_grad,
        mlp_gain_grad,
        router_grad,
        gate_grad,
        up_grad,
        down_grad,
    )


def solution(mesh):
    return jax.shard_map(
        shards,
        mesh=mesh,
        in_specs=(
            P(("dp", "row", "col"), None),
            P(),
            P(None, ("row", "col")),
            P(None, ("row", "col")),
            P(None, ("row", "col")),
            P(("row", "col"), None),
            P(),
            P(),
            P("dp", None, ("row", "col")),
            P("dp", None, ("row", "col")),
            P("dp", ("row", "col"), None),
            P(("dp", "row", "col"), None),
            P(("dp", "row", "col"), None),
            P(("dp", "row", "col"), None),
            P(("dp", "row", "col")),
            P(("dp", "row", "col")),
        ),
        out_specs=(
            P(("dp", "row", "col"), None),
            P(("dp", "row", "col"), None),
            P(),
            P(None, ("row", "col")),
            P(None, ("row", "col")),
            P(None, ("row", "col")),
            P(("row", "col"), None),
            P(),
            P(),
            P("dp", None, ("row", "col")),
            P("dp", None, ("row", "col")),
            P("dp", ("row", "col"), None),
        ),
        check_vma=False,
    )
```

profile of v0, /device:TPU:0, one launch (start us, length us, event | category | flops | bytes accessed | tf_op | source)
XLA Modules:
  0.0 1771.1 jit_solution(17576297887361651493)
XLA Ops:
  13.8 13.1 all-reduce.2
  27.1 20.7 %all-gather.6.cloned.1.call-done = bf16[1280,1536]{1,0:T(8,128)(2,1)} async-done(((bf16[320,1536]{1,0:T(8,128)(2,1)}), bf16[1280,1536]{1,0:T(8,128)(2,1)}) %all-gather.6.cloned.1.call-update) | async-done | bytes 3932176 | tf_op jit(solution)/shard_map/all_gather | solution.py:169
  55.8 49.5 %while.29 = (s32[]{:T(128)}, bf16[5,256,2,3,64]{1,4,3,2,0:T(8,128)(2,1)}, f32[5,2,3,256]{3,2,1,0:T(4,128)}, s32[1280]{0:T(1024)S(1)}, s32[5]{0:T(128)S(1)}, /*in...) while((s32[]{:T(128)}, ...), condition=%wide.region_6.7_spmd.clone, body=%wide.region_3.6_spmd.clone.sunk | while | flops 530938368 | bytes 26026220 | solution.py:77
  123.8 59.8 %reduce-scatter.10.cloned.1.call-done = f32[320,1536]{1,0:T(8,128)} async-done(((f32[1280,1536]{1,0:T(8,128)}), f32[320,1536]{1,0:T(8,128)}) %reduce-scatter.10.cloned.1.call-update) | async-done | bytes 1966096 | tf_op jit(solution)/shard_map/reduce_scatter | solution.py:190
  188.4 20.9 %gather_fusion.2 = f32[2560]{0:T(1024)S(1)} fusion(f32[320,16]{0,1:T(8,128)S(1)} %fusion.87, s32[2560]{0:T(1024)S(1)} %reshape.308), kind=kCustom, calls=%fused_computation.2 | custom fusion | bytes 40960 | tf_op jit(solution)/shard_map/jit(take_along_axis)/gather | solution.py:200
  211.0 19.4 %scatter_custom_fusion.1 = bf16[3200,1536]{1,0:T(8,128)(2,1)} fusion(s32[2560]{0:T(1024)S(1)} %get-tuple-element.265, f32[320,1536]{1,0:T(8,128)S(1)} %copy-done.9, f32[2560]{0:T(1024)S(1)} %mul.282, bf16[]{:T(256)} %constant.49.clone.1), kind=kCustom, calls=%fused_computation.79 | custom fusion | flops 7864320 | bytes 11808770 | tf_op jit(solution)/shard_map/scatter | solution.py:252
  236.0 18.1 %scatter_custom_fusion = bf16[3200,1536]{1,0:T(8,128)(2,1)} fusion(s32[2560]{0:T(1024)S(1)} %get-tuple-element.265, bf16[]{:T(256)} %constant.49.clone.1, bf16[320,1536]{1,0:T(8,128)(2,1)} %copy-done.12), kind=kCustom, calls=%fused_computation.80 | custom fusion | bytes 10813442 | tf_op jit(solution)/shard_map/scatter | solution.py:218
  254.0 196.0 %all-to-all-done.2 = bf16[16,200,1536]{2,1,0:T(8,128)(2,1)} async-done(((bf16[16,200,1536]{2,1,0:T(8,128)(2,1)}), bf16[16,200,1536]{2,1,0:T(8,128)(2,1)}, u32[]{:S(2)}, u32[]{:S(2)}) %all-to-all-start.2) | async-done | bytes 9830432 | tf_op jit(solution)/shard_map/all_to_all | solution.py:254
  465.5 202.7 %all-to-all-done = bf16[16,200,1536]{2,1,0:T(8,128)(2,1)} async-done(((bf16[16,200,1536]{2,1,0:T(8,128)(2,1)}), bf16[16,200,1536]{2,1,0:T(8,128)(2,1)}, u32[]{:S(2)}, u32[]{:S(2)}) %all-to-all-start) | async-done | bytes 9830432 | tf_op jit(solution)/shard_map/all_to_all | solution.py:220
  697.7 15.5 multiply_convert_fusion
  720.5 31.2 %copy.109 = bf16[2,1600,1536]{2,0,1:T(2,128)(2,1)} copy(bf16[2,1600,1536]{2,1,0:T(8,128)(2,1)S(1)} %convolution_convert_fusion) | data formatting | bytes 19660800 | tf_op jit(solution)/shard_map/convert_element_type | solution.py:236
  757.0 11.7 fusion.90
  768.8 13.5 add_convert_fusion
  782.2 46.8 %copy.113 = bf16[2,1600,1536]{2,0,1:T(2,128)(2,1)} copy(bf16[2,1600,1536]{2,1,0:T(8,128)(2,1)} %add_convert_fusion) | data formatting | bytes 19660800 | tf_op jit(solution)/shard_map/convert_element_type | solution.py:277
  829.0 140.8 %all-to-all-done.1 = bf16[2,1600,1536]{2,0,1:T(2,128)(2,1)} async-done(((bf16[2,1600,1536]{2,0,1:T(2,128)(2,1)}), bf16[2,1600,1536]{2,0,1:T(2,128)(2,1)}, u32[]{:S(2)}, u32[]{:S(2)}) %all-to-all-start.1) | async-done | bytes 9830432 | tf_op jit(solution)/shard_map/all_to_all | solution.py:237
  985.4 21.5 %gather_fusion = bf16[2560,1536]{1,0:T(8,128)(2,1)} fusion(bf16[3200,1536]{1,0:T(8,128)(2,1)} %bitcast.252, s32[3072]{0:T(1024)S(1)} %pad_clamp_fusion), kind=kCustom, calls=%fused_computation | custom fusion | bytes 15738880 | tf_op jit(solution)/shard_map/gather | solution.py:240
  1016.3 171.7 %all-to-all-done.3 = bf16[2,1600,1536]{2,0,1:T(2,128)(2,1)} async-done(((bf16[2,1600,1536]{2,0,1:T(2,128)(2,1)}), bf16[2,1600,1536]{2,0,1:T(2,128)(2,1)}, u32[]{:S(2)}, u32[]{:S(2)}) %all-to-all-start.3) | async-done | bytes 9830432 | tf_op jit(solution)/shard_map/all_to_all | solution.py:284
  1197.5 21.6 %gather_fusion.1 = bf16[2560,1536]{1,0:T(8,128)(2,1)} fusion(bf16[3200,1536]{1,0:T(8,128)(2,1)} %bitcast.251, s32[3072]{0:T(1024)S(1)} %pad_clamp_fusion), kind=kCustom, calls=%fused_computation.1 | custom fusion | bytes 15738880 | tf_op jit(solution)/shard_map/gather | solution.py:287
  1284.3 12.1 convolution_convert_fusion.1
  1302.5 147.3 %while.30 = (s32[]{:T(128)}, f32[1280,2,64]{0,2,1:T(8,128)S(1)}, f32[1280,2,64]{0,2,1:T(8,128)S(1)}, bf16[5,256,2,3,64]{1,4,3,2,0:T(8,128)(2,1)}, s32[5]{0:T(128...) while((s32[]{:T(128)}, f32[1280,2,64]{0,2,1:T(8,128)S(1)}, ...), condition=%wide.region_22.23_spmd.clone.clone, body=%wide.region_20.22_spmd.clone.clone.sunk | while | flops 1280932352 | bytes 95736160 | solution.py:122
  1484.8 106.4 %all-reduce.10.cloned.1.call-done = (bf16[1536,384]{1,0:T(8,128)(2,1)}, bf16[1536,128]{1,0:T(8,128)(2,1)}, bf16[1536,128]{1,0:T(8,128)(2,1)}, bf16[384,1536]{1,0:T(8,128)(2,1)}) async-done(((bf16[1536,384]{1,0:T(8,128)(2,1)}, bf16[1536,128]{1,0:T(8,128)(2,1)}, bf16[1536,128]{1,0:T(8,128)(2,1)}, bf16[384,1536]{1,0:T(8,128)(2,1)}), (bf16[1536,384]{1,0:T(8,128)(2,1)}, bf16[1536,128]{1,0:T(8,128)(2,1)}, ...) | async-done | bytes 3145744 | tf_op jit(solution)/shard_map/psum | solution.py:337
  1599.9 35.9 %reduce-scatter.12.cloned.1.call-done = bf16[320,1536]{1,0:T(8,128)(2,1)} async-done(((bf16[1280,1536]{1,0:T(8,128)(2,1)}), bf16[320,1536]{1,0:T(8,128)(2,1)}) %reduce-scatter.12.cloned.1.call-update) | async-done | bytes 983056 | tf_op jit(solution)/shard_map/reduce_scatter | solution.py:326
  1643.9 39.5 %all-reduce.3 = (f32[1536]{0:T(1024)}, f32[1536]{0:T(1024)}) all-reduce(f32[1536]{0:T(1024)S(1)} %get-tuple-element.262, f32[1536]{0:T(1024)S(1)} %copy-done.55), channel_id=1, replica_groups=mesh['dp'=8,'row'=2,'col'=2] {'dp','row','col'}, use_global_device_ids=true, to_apply=%region_26.27 | all-reduce | flops 3072 | bytes 24576 | tf_op jit(solution)/shard_map/psum | solution.py:353
  1683.3 79.1 %all-reduce.8.cloned.1.call-done = f32[1536,16]{0,1:T(8,128)} async-done(((f32[1536,16]{0,1:T(8,128)}), f32[1536,16]{0,1:T(8,128)}) %all-reduce.8.cloned.1.call-update) | async-done | bytes 98320 | tf_op jit(solution)/shard_map/psum | solution.py:353
  (398 shorter events, 440.2 us)
Async XLA Ops:
  7.2 101.8 %copy-start = (bf16[384,1536]{1,0:T(8,128)(2,1)S(1)}, bf16[384,1536]{1,0:T(8,128)(2,1)}, u32[]{:S(2)}) copy-start(bf16[384,1536]{1,0:T(8,128)(2,1)} %param.25) | copy-start | bytes 3538948
  7.2 40.6 %all-gather.6.cloned.1.call-start = ((), (), s32[]{:S(2)}) async-start(), calls=%async_computation.9 | async-start | bytes 4915200 | tf_op jit(solution)/shard_map/all_gather | solution.py:169
  11.9 171.6 %reduce-scatter.10.cloned.1.call-start = ((), (), s32[]{:S(2)}) async-start(), calls=%async_computation.10 | async-start | bytes 9830400 | tf_op jit(solution)/shard_map/reduce_scatter | solution.py:190
  115.0 68.5 %copy-start.7 = (bf16[320,1536]{1,0:T(8,128)(2,1)S(1)}, bf16[320,1536]{1,0:T(8,128)(2,1)}, u32[]{:S(2)}) copy-start(bf16[320,1536]{1,0:T(8,128)(2,1)} %param.20) | copy-start | bytes 2949124
  121.6 88.0 %copy-start.52 = (pred[320,8]{0,1:T(8,128)(4,1)}, pred[320,8]{0,1:T(8,128)(4,1)S(1)}, u32[]{:S(2)}) copy-start(pred[320,8]{0,1:T(8,128)(4,1)S(1)} %copy.105) | copy-start | bytes 7684
  121.6 65.2 %copy-start.39 = (f32[1536]{0:T(1024)S(1)}, f32[1536]{0:T(1024)}, u32[]{:S(2)}) copy-start(f32[1536]{0:T(1024)} %param.26) | copy-start | bytes 18436
  123.8 64.2 %copy-start.38 = (bf16[1536,16]{0,1:T(8,128)(2,1)S(1)}, bf16[1536,16]{0,1:T(8,128)(2,1)}, u32[]{:S(2)}) copy-start(bf16[1536,16]{0,1:T(8,128)(2,1)} %param.27) | copy-start | bytes 147460
  230.4 219.6 %all-to-all-start.2 = ((bf16[16,200,1536]{2,1,0:T(8,128)(2,1)}), bf16[16,200,1536]{2,1,0:T(8,128)(2,1)}, u32[]{:S(2)}, u32[]{:S(2)}) async-start(bf16[16,200,1536]{2,1,0:T(8,128)(2,1)} %bitcast.255), calls=%async_computation.3 | async-start | bytes 19660800 | tf_op jit(solution)/shard_map/all_to_all | solution.py:254
  450.0 218.2 %all-to-all-start = ((bf16[16,200,1536]{2,1,0:T(8,128)(2,1)}), bf16[16,200,1536]{2,1,0:T(8,128)(2,1)}, u32[]{:S(2)}, u32[]{:S(2)}) async-start(bf16[16,200,1536]{2,1,0:T(8,128)(2,1)} %bitcast.254), calls=%async_computation.1 | async-start | bytes 19660800 | tf_op jit(solution)/shard_map/all_to_all | solution.py:220
  455.1 221.4 %all-gather.10.cloned.1.call-start = ((), (), s32[]{:S(2)}) async-start(), calls=%async_computation.12 | async-start | bytes 3932160 | tf_op jit(solution)/shard_map/all_gather | solution.py:162
  455.9 231.2 %all-gather.8.cloned.1.call-start = ((), (), s32[]{:S(2)}) async-start(), calls=%async_computation.11 | async-start | bytes 3932160 | tf_op jit(solution)/shard_map/all_gather | solution.py:161
  456.5 241.2 %all-gather.12.cloned.1.call-start = ((), (), s32[]{:S(2)}) async-start(), calls=%async_computation.13 | async-start | bytes 3932160 | tf_op jit(solution)/shard_map/all_gather | solution.py:163
  751.7 218.1 %all-to-all-start.1 = ((bf16[2,1600,1536]{2,0,1:T(2,128)(2,1)}), bf16[2,1600,1536]{2,0,1:T(2,128)(2,1)}, u32[]{:S(2)}, u32[]{:S(2)}) async-start(bf16[2,1600,1536]{2,0,1:T(2,128)(2,1)} %copy.109), calls=%async_computation.2 | async-start | bytes 19660800 | tf_op jit(solution)/shard_map/all_to_all | solution.py:237
  829.0 146.3 %copy-start.33 = (pred[320,8]{1,0:T(8,128)(4,1)S(1)}, pred[320,8]{1,0:T(8,128)(4,1)}, u32[]{:S(2)}) copy-start(pred[320,8]{1,0:T(8,128)(4,1)} %copy-done.32) | copy-start | bytes 7684
  829.0 147.0 %copy-start.51 = (s32[2560]{0:T(1024)S(1)}, s32[2560]{0:T(1024)}, u32[]{:S(2)}) copy-start(s32[2560]{0:T(1024)} %get-tuple-element.264) | copy-start | bytes 30724
  969.8 218.3 %all-to-all-start.3 = ((bf16[2,1600,1536]{2,0,1:T(2,128)(2,1)}), bf16[2,1600,1536]{2,0,1:T(2,128)(2,1)}, u32[]{:S(2)}, u32[]{:S(2)}) async-start(bf16[2,1600,1536]{2,0,1:T(2,128)(2,1)} %copy.113), calls=%async_computation.4 | async-start | bytes 19660800 | tf_op jit(solution)/shard_map/all_to_all | solution.py:284
  974.9 321.7 %all-gather.14.cloned.1.call-start = ((), (), s32[]{:S(2)}) async-start(), calls=%async_computation.14 | async-start | bytes 4915200 | tf_op jit(solution)/shard_map/all_gather | solution.py:302
  1016.3 213.9 %copy-start.42 = (bf16[320,16]{0,1:T(8,128)(2,1)}, bf16[320,16]{0,1:T(8,128)(2,1)S(1)}, u32[]{:S(2)}) copy-start(bf16[320,16]{0,1:T(8,128)(2,1)S(1)} %select_reduce_fusion) | copy-start | bytes 30724
  1235.6 234.0 %reduce-scatter.18.cloned.1.call-start = ((), (), s32[]{:S(2)}) async-start(), calls=%async_computation.19 | async-start | bytes 3932160
  1260.0 213.3 %reduce-scatter.16.cloned.1.call-start = ((), (), s32[]{:S(2)}) async-start(), calls=%async_computation.18 | async-start | bytes 3932160
  1284.3 197.2 %reduce-scatter.14.cloned.1.call-start = ((), (), s32[]{:S(2)}) async-start(), calls=%async_computation.17 | async-start | bytes 3932160 | tf_op jit(solution)/shard_map/reduce_scatter | solution.py:349
  1296.5 294.7 %all-reduce.10.cloned.1.call-start = ((), (), s32[]{:S(2)}) async-start(), calls=%async_computation.20 | async-start | bytes 6291456 | tf_op jit(solution)/shard_map/psum | solution.py:337
  1462.8 173.0 %reduce-scatter.12.cloned.1.call-start = ((), (), s32[]{:S(2)}) async-start(), calls=%async_computation.15 | async-start | bytes 4915200 | tf_op jit(solution)/shard_map/reduce_scatter | solution.py:326
  1469.6 292.9 %all-reduce.8.cloned.1.call-start = ((), (), s32[]{:S(2)}) async-start(), calls=%async_computation.16 | async-start | bytes 196608 | tf_op jit(solution)/shard_map/psum | solution.py:353
  (64 other events, 766.0 us)
Sparse Core Ops, SparseCore 0:
  12.1 35.7 all-gather.5
  114.5 69.0 reduce-scatter.9
  457.6 29.2 all-gather.9
  488.4 28.9 all-gather.7
  518.9 28.5 all-gather.11
  1235.7 31.4 all-gather.13
  1270.0 37.9 reduce-scatter.17
  1310.5 37.9 reduce-scatter.15
  1351.1 37.9 reduce-scatter.13
  1462.9 128.2 all-reduce.9
  1593.9 41.8 reduce-scatter.11
  1641.8 120.6 all-reduce.7
where the time goes:
time: 1780 us; the launch traced here: 1770 us
  waiting for transfers between devices  1010 us (57%)
  local copies, waits for them, and re-layouts  269 us (15%)
  matrix products  246 us (14%)
  other arithmetic  134 us (8%)
  blocking collectives  52.5 us (3%)
  starting transfers between devices  22.1 us (1%)
    all_to_all x1, waiting for transfers between devices, shards(): lax.all_to_all(dispatch_rows.reshape(experts_all, capacity, width), 'dp',...  203 us
    all_to_all x1, waiting for transfers between devices, shards(): lax.all_to_all(grad_dispatch.reshape(experts_all, capacity, width), 'dp',...  196 us
    all_to_all x1, waiting for transfers between devices, shards(): lax.all_to_all(grad_rows, 'dp', split_axis=1, concat_axis=0, tiled=True)  172 us
    all_to_all x1, waiting for transfers between devices, shards(): lax.all_to_all(expert_out, 'dp', split_axis=1, concat_axis=0, tiled=True)  141 us
    psum x1, waiting for transfers between devices, shards(): lax.psum(query_part.astype(jnp.bfloat16), 'dp').astype(jnp.float32)  106 us
    psum x1, waiting for transfers between devices, shards(): lax.psum((attn_gain_part, mlp_gain_part, router_part), ('dp', 'row', 'col'))  79.1 us
    reduce_scatter x1, waiting for transfers between devices, shards(): lax.psum_scatter(jnp.dot(attn_heads, out_weight, preferred_element_type=j...  59.8 us
    convert_element_type x1, local copies, waits for them, and re-layouts, shards(): grad_rows = (grad_rows + jnp.einsum('erf,edf->erd', grad_up_pre, full_up,...  46.8 us
  transfers between devices with their start and end apart: 16, of which 9 were waited for; matrix products, arithmetic and copies ran while one was open for 24% of the time, Pallas kernels for 0%

commit v1 on v0

v1 whole, which is shorter than its diff:
```python
import functools
import math

import jax
import jax.numpy as jnp
from jax import lax
from jax.experimental import pallas as pl
from jax.experimental.pallas import tpu as pltpu
from jax.sharding import PartitionSpec as P

HD = 64
TOPK = 8
QT = 128
EPS = 1e-05
NEG = -1e30
MIB = 2**20
BF = jnp.bfloat16
F32 = jnp.float32
VMEM = pl.BlockSpec(memory_space=pltpu.VMEM)
SMEM = pl.BlockSpec(memory_space=pltpu.SMEM)


def dot(a, b, ca, cb):
    return lax.dot_general(a, b, (((ca,), (cb,)), ((), ())), preferred_element_type=F32)


def after(value, *earlier):
    return lax.optimization_barrier((value,) + earlier)[0]


def stack_heads(block, count):
    return jnp.concatenate([block[:, h * HD : (h + 1) * HD] for h in range(count)], axis=0)


def causal_mask(per_group):
    key = lax.broadcasted_iota(jnp.int32, (QT, QT), 0)
    query = lax.broadcasted_iota(jnp.int32, (QT, QT), 1)
    return jnp.concatenate([key <= query] * per_group, axis=1)


def tile_masks(seg, parents, per_group):
    key = lax.broadcasted_iota(jnp.int32, (QT, QT), 0)
    query = lax.broadcasted_iota(jnp.int32, (QT, QT), 1)
    own = (key <= query) & (key // seg == query // seg)
    par = None
    for j, parent in enumerate(parents):
        hit = (key // seg == j) & (query // seg == j) & (parent > 0)
        par = hit if par is None else par | hit
    return (
        jnp.concatenate([own] * per_group, axis=1),
        jnp.concatenate([par] * per_group, axis=1),
    )


def softmax_parts(keys, masks, q):
    parts = []
    top = None
    for k, mask in zip(keys, masks):
        s = dot(k, q, 1, 1)
        if mask is not None:
            s = jnp.where(mask, s, NEG)
        parts.append(s)
        m = jnp.max(s, axis=0, keepdims=True)
        top = m if top is None else jnp.maximum(top, m)
    probs = []
    total = None
    for s in parts:
        e = jnp.exp(s - top)
        t = jnp.sum(e, axis=0, keepdims=True)
        total = t if total is None else total + t
        probs.append(e)
    inverse = 1.0 / total
    return [e * inverse for e in probs]


def each_tile(qkv_ref, parent_ref, kv, per_group, seg, work):
    rows = qkv_ref.shape[0]
    trunk = 8 * seg
    segs = QT // seg
    q_width = kv * per_group * HD
    causal = causal_mask(per_group)

    def columns(g):
        return q_width + g * HD, q_width + kv * HD + g * HD

    for i in range(trunk // QT):
        for g in range(kv):
            kc, vc = columns(g)
            spans = ([(0, i * QT)] if i > 0 else []) + [(i * QT, QT)]
            keys = [qkv_ref[a : a + n, kc : kc + HD] for a, n in spans]
            values = [qkv_ref[a : a + n, vc : vc + HD] for a, n in spans]
            masks = ([None] if i > 0 else []) + [causal]
            work(i * QT, g, keys, values, masks, [[s] for s in spans])

    def body(i, carry):
        first = pl.multiple_of(trunk + i * QT, QT)
        parents = [parent_ref[8 + i * segs + j] for j in range(segs)]
        starts = [pl.multiple_of(p * seg, seg) for p in parents]
        own, par = tile_masks(seg, parents, per_group)

        def take(c):
            blocks = [qkv_ref[pl.ds(s, seg), c : c + HD] for s in starts]
            return [
                qkv_ref[0:trunk, c : c + HD],
                qkv_ref[pl.ds(first, QT), c : c + HD],
                jnp.concatenate(blocks, axis=0) if segs > 1 else blocks[0],
            ]

        for g in range(kv):
            kc, vc = columns(g)
            places = [[(0, trunk)], [(first, QT)], [(s, seg) for s in starts]]
            work(first, g, take(kc), take(vc), [None, own, par], places)
        return carry

    lax.fori_loop(0, (rows - trunk) // QT, body, 0)


def attend_forward_kernel(kv, per_group, seg, blocks, shard_ref, parent_ref, *refs):
    ins, (qkv_ref, out_ref, full_ref) = refs[:blocks], refs[blocks:]
    local = ins[0].shape[0]
    scale = BF(1.0 / math.sqrt(HD))
    for j in range(blocks):
        at = pl.multiple_of(shard_ref[j] * local, 64)
        qkv_ref[pl.ds(at, local), :] = ins[j][...]

    def work(first, g, keys, values, masks, places):
        block = qkv_ref[pl.ds(first, QT), g * per_group * HD : (g + 1) * per_group * HD]
        probs = softmax_parts(keys, masks, stack_heads(block, per_group) * scale)
        total = None
        for p, v in zip(probs, values):
            o = dot(v, p.astype(BF), 0, 0)
            total = o if total is None else total + o
        for h in range(per_group):
            c = (g * per_group + h) * HD
            full_ref[pl.ds(first, QT), c : c + HD] = total[:, h * QT : (h + 1) * QT].T.astype(BF)

    each_tile(qkv_ref, parent_ref, kv, per_group, seg, work)
    for j in range(blocks):
        at = pl.multiple_of(shard_ref[j] * local, 64)
        out_ref[j * local : (j + 1) * local, :] = full_ref[pl.ds(at, local), :]


def attend_forward(shards, parent_block, qkv_blocks, kv, per_group, seg):
    blocks = len(qkv_blocks)
    local, wide = qkv_blocks[0].shape
    rows = blocks * local
    width = kv * per_group * HD
    cells = rows * 12 * seg * kv * per_group
    return pl.pallas_call(
        functools.partial(attend_forward_kernel, kv, per_group, seg, blocks),
        out_shape=[jax.ShapeDtypeStruct((rows, wide), BF), jax.ShapeDtypeStruct((rows, width), BF)],
        in_specs=[SMEM, SMEM] + [VMEM] * blocks,
        out_specs=[VMEM, VMEM],
        scratch_shapes=[pltpu.VMEM((rows, width), BF)],
        compiler_params=pltpu.CompilerParams(vmem_limit_bytes=40 * MIB),
        cost_estimate=pl.CostEstimate(
            flops=16 * HD * cells, bytes_accessed=4 * rows * wide, transcendentals=cells
        ),
        name="attend_forward",
    )(shards, parent_block, *qkv_blocks)


def attend_backward_kernel(kv, per_group, seg, blocks, shard_ref, parent_ref, qkv_ref, *refs):
    ins, (out_ref, do_ref, full_ref, dk_ref, dv_ref) = refs[:blocks], refs[blocks:]
    local = ins[0].shape[0]
    q_width = kv * per_group * HD
    scale = 1.0 / math.sqrt(HD)
    for j in range(blocks):
        at = pl.multiple_of(shard_ref[j] * local, 64)
        do_ref[pl.ds(at, local), :] = ins[j][...]
    dk_ref[...] = jnp.zeros_like(dk_ref)
    dv_ref[...] = jnp.zeros_like(dv_ref)

    def work(first, g, keys, values, masks, places):
        span = slice(g * per_group * HD, (g + 1) * per_group * HD)
        q = stack_heads(qkv_ref[pl.ds(first, QT), span], per_group) * BF(scale)
        d = stack_heads(do_ref[pl.ds(first, QT), span], per_group)
        probs = softmax_parts(keys, masks, q)
        grads = [dot(v, d, 1, 1) for v in values]
        delta = None
        for p, grad in zip(probs, grads):
            t = jnp.sum(grad * p, axis=0, keepdims=True)
            delta = t if delta is None else delta + t
        dq = None
        for p, grad, k, place in zip(probs, grads, keys, places):
            ds = (p * (grad - delta)).astype(BF)
            dk = dot(ds, q, 1, 0)
            dv = dot(p.astype(BF), d, 1, 0)
            o = dot(k, ds, 0, 0)
            dq = o if dq is None else dq + o
            at = 0
            for start, size in place:
                dk_ref[pl.ds(start, size), g * HD : (g + 1) * HD] += dk[at : at + size]
                dv_ref[pl.ds(start, size), g * HD : (g + 1) * HD] += dv[at : at + size]
                at += size
        dq = dq * scale
        for h in range(per_group):
            c = (g * per_group + h) * HD
            full_ref[pl.ds(first, QT), c : c + HD] = dq[:, h * QT : (h + 1) * QT].T.astype(BF)

    each_tile(qkv_ref, parent_ref, kv, per_group, seg, work)
    full_ref[:, q_width : q_width + kv * HD] = dk_ref[...].astype(BF)
    full_ref[:, q_width + kv * HD : q_width + 2 * kv * HD] = dv_ref[...].astype(BF)
    for j in range(blocks):
        at = pl.multiple_of(shard_ref[j] * local, 64)
        out_ref[j * local : (j + 1) * local, :] = full_ref[pl.ds(at, local), :]


def attend_backward(shards, parent_block, qkv, grad_blocks, kv, per_group, seg):
    blocks = len(grad_blocks)
    rows, wide = qkv.shape
    width = kv * per_group * HD
    cells = rows * 12 * seg * kv * per_group
    return pl.pallas_call(
        functools.partial(attend_backward_kernel, kv, per_group, seg, blocks),
        out_shape=jax.ShapeDtypeStruct((rows, wide), BF),
        in_specs=[SMEM, SMEM, VMEM] + [VMEM] * blocks,
        out_specs=VMEM,
        scratch_shapes=[
            pltpu.VMEM((rows, width), BF),
            pltpu.VMEM((rows, wide), BF),
            pltpu.VMEM((rows, kv * HD), F32),
            pltpu.VMEM((rows, kv * HD), F32),
        ],
        compiler_params=pltpu.CompilerParams(vmem_limit_bytes=40 * MIB),
        cost_estimate=pl.CostEstimate(
            flops=40 * HD * cells, bytes_accessed=6 * rows * wide, transcendentals=cells
        ),
        name="attend_backward",
    )(shards, parent_block, qkv, *grad_blocks)


def expert_kernel(
    at_ref, xa_ref, xb_ref, ga_ref, gb_ref, code_ref, router_ref, gate_ref, up_ref, down_ref,
    mix_a_ref, mix_b_ref, back_a_ref, back_b_ref, dot_ref, act_ref, dgate_ref, dup_ref,
):
    half = xa_ref.shape[0]
    x = jnp.concatenate([xa_ref[...], xb_ref[...]], axis=0)
    g = jnp.concatenate([ga_ref[...], gb_ref[...]], axis=0)
    code_a = code_ref[at_ref[1]]
    code_b = code_ref[at_ref[2]]
    token = lax.broadcasted_iota(jnp.int32, code_a.shape, 1)
    code = jnp.where(token < half, code_a, code_b).T
    logits = dot(x, router_ref[...], 1, 0)
    logits = jnp.where(code > 0.5, logits, NEG)
    top = jnp.max(logits, axis=1, keepdims=True)
    e = jnp.exp(logits - top)
    kept = jnp.where(code > 1.5, 1.0, 0.0)
    gates = kept * e / jnp.sum(e, axis=1, keepdims=True)
    lane = lax.broadcasted_iota(jnp.int32, gates.shape, 1)
    count = gate_ref.shape[0]
    mix = None
    back = None
    for n in range(count):
        mine = lane == at_ref[0] + n
        weight = jnp.sum(jnp.where(mine, gates, 0.0), axis=1, keepdims=True)
        keep = jnp.sum(jnp.where(mine, kept, 0.0), axis=1, keepdims=True)
        gate_pre = dot(x, gate_ref[n], 1, 0)
        up_pre = dot(x, up_ref[n], 1, 0)
        grad = dot(g, down_ref[n], 1, 1)
        sig = 1.0 / (1.0 + jnp.exp(-gate_pre))
        silu = gate_pre * sig
        act = (silu * up_pre).astype(BF).astype(F32)
        pair_dot = jnp.sum(act * grad, axis=1, keepdims=True) * keep
        dot_ref[n : n + 1, :] = pair_dot.T
        weighted = (act * weight).astype(BF)
        grad = grad * weight
        dgate = (grad * up_pre * sig * (1.0 + gate_pre * (1.0 - sig))).astype(BF)
        dup = (grad * silu).astype(BF)
        act_ref[n] = weighted
        dgate_ref[n] = dgate
        dup_ref[n] = dup
        m = dot(weighted, down_ref[n], 1, 0)
        mix = m if mix is None else mix + m
        b = dot(dgate, gate_ref[n], 1, 1) + dot(dup, up_ref[n], 1, 1)
        back = b if back is None else back + b
    mix = mix.astype(BF)
    back = back.astype(BF)
    mix_a_ref[...] = mix[:half]
    mix_b_ref[...] = mix[half:]
    back_a_ref[...] = back[:half]
    back_b_ref[...] = back[half:]


def expert_step(at, x, g, codes, router, gate, up, down):
    half, width = x[0].shape
    count, _, hidden = gate.shape
    rows = 2 * half
    half_shape = jax.ShapeDtypeStruct((half, width), BF)
    kept_shape = jax.ShapeDtypeStruct((count, rows, hidden), BF)
    return pl.pallas_call(
        expert_kernel,
        out_shape=[half_shape] * 4
        + [jax.ShapeDtypeStruct((count, rows), F32)]
        + [kept_shape] * 3,
        in_specs=[SMEM] + [VMEM] * 9,
        out_specs=[VMEM] * 8,
        compiler_params=pltpu.CompilerParams(vmem_limit_bytes=56 * MIB),
        cost_estimate=pl.CostEstimate(
            flops=2 * rows * width * hidden * count * 6 * 2,
            bytes_accessed=6 * width * hidden * count + 10 * rows * width,
            transcendentals=rows * hidden * count,
        ),
        name="expert_step",
    )(at, x[0], x[1], g[0], g[1], codes, router, gate, up, down)


def tree_moves():
    rows, cols = lax.axis_size("row"), lax.axis_size("col")
    both = ("row", "col")
    if rows == 2 and cols == 2:
        swap = [(0, 1), (1, 0)]
        cross = [(0, 3), (3, 0), (1, 2), (2, 1)]
        me = lax.axis_index("row") * 2 + lax.axis_index("col")
        shards = [me, me ^ 1, me ^ 2, me ^ 3]

        def gather(x):
            across = lax.ppermute(x, "row", swap)
            beside = lax.ppermute(x, "col", swap)
            return [x, beside, across, lax.ppermute(across, "col", swap)]

        def exchange(blocks):
            return [
                blocks[0],
                lax.ppermute(blocks[1], "col", swap),
                lax.ppermute(blocks[2], "row", swap),
                lax.ppermute(blocks[3], both, cross),
            ]

        def reduce(blocks):
            far = blocks[2].astype(F32) + lax.ppermute(blocks[3], "col", swap).astype(F32)
            far = lax.ppermute(far.astype(BF), "row", swap).astype(F32)
            near = blocks[0].astype(F32) + lax.ppermute(blocks[1], "col", swap).astype(F32)
            return near + far

        return shards, gather, exchange, reduce

    count = rows * cols

    def gather(x):
        whole = lax.all_gather(x, both, axis=0)
        return [whole[i] for i in range(count)]

    def exchange(blocks):
        whole = lax.all_to_all(jnp.stack(blocks), both, 0, 0)
        return [whole[i] for i in range(count)]

    def reduce(blocks):
        return lax.psum_scatter(jnp.stack(blocks), both, scatter_dimension=0).astype(F32)

    return [jnp.int32(i) for i in range(count)], gather, exchange, reduce


def ring_order(count):
    depth = 4 if count % 4 == 0 else 1
    ys = count // depth
    order = []
    for y in range(ys):
        zs = range(depth) if y % 2 == 0 else reversed(range(depth))
        order += [z * ys + y for z in zs]
    return order


def ring_steps(order):
    n = len(order)
    onward = [(order[i], order[(i + 1) % n]) for i in range(n)]
    return onward, [(b, a) for a, b in onward]


def ring_gather(a, b, order):
    onward, backward = ring_steps(order)
    held = [(a, b)]
    for _ in range(len(order) - 1):
        a = lax.ppermute(a, "dp", onward)
        b = lax.ppermute(b, "dp", backward)
        held.append((a, b))
    return held


def ring_reduce(parts, order):
    onward, backward = ring_steps(order)
    a, b = parts[1]
    for k in range(1, len(order)):
        a = lax.ppermute(a, "dp", onward)
        b = lax.ppermute(b, "dp", backward)
        more = parts[(k + 1) % len(order)]
        a = a.astype(F32) + more[0].astype(F32)
        b = b.astype(F32) + more[1].astype(F32)
        if k < len(order) - 1:
            a, b = a.astype(BF), b.astype(BF)
    return jnp.concatenate([a, b], axis=0)


def rms_scale(values):
    return lax.rsqrt(jnp.mean(values * values, axis=-1, keepdims=True) + EPS)


def norm_back(grad_normed, values, scale_rows, gain):
    weighted = grad_normed * gain
    grad_gain = jnp.sum(grad_normed * values * scale_rows, axis=0)
    inner = jnp.mean(weighted * values, axis=-1, keepdims=True)
    return (
        scale_rows * weighted - values * scale_rows * scale_rows * scale_rows * inner,
        grad_gain,
    )


def shards_program(
    tokens, attn_gain, query_weight, key_weight, value_weight, out_weight, mlp_gain, router_weight,
    gate_weight, up_weight, down_weight, output_grad, expert_ids, slot_rank, segment_ids, parent_ids,
):
    local_rows, width = tokens.shape
    half = local_rows // 2
    ring = lax.axis_size("dp")
    order = ring_order(ring)
    places = [order.index(i) for i in range(ring)]
    shards, tree_gather, tree_exchange, tree_reduce = tree_moves()
    count = len(shards)
    shard_ids = jnp.stack(shards).astype(jnp.int32)
    kv = key_weight.shape[1] // HD
    per_group = query_weight.shape[1] // key_weight.shape[1]
    q_width = query_weight.shape[1]
    k_width = key_weight.shape[1]
    experts_local = gate_weight.shape[0]
    experts = experts_local * ring
    capacity = 5 * local_rows * TOPK // (4 * experts)
    seg = local_rows * count // 20
    dp_index = lax.axis_index("dp")
    place = jnp.array(places, jnp.int32)[dp_index]

    token_values = tokens.astype(F32)
    scale_attn = rms_scale(token_values)
    normed = (token_values * scale_attn * attn_gain).astype(BF)
    tree_normed = tree_gather(normed)
    step = math.gcd(seg, local_rows)
    labels = jnp.stack([segment_ids[::step], parent_ids[::step]]).astype(jnp.int32)
    tree_labels = lax.all_gather(labels, ("row", "col"), axis=1, tiled=True)[:, :: seg // step]
    spot = jnp.arange(20, dtype=jnp.int32)
    parent_block = jnp.sum(
        jnp.where(
            (tree_labels[0][None, :] == tree_labels[1][:, None]) & (tree_labels[1][:, None] > 0),
            spot[None, :],
            0,
        ),
        axis=1,
    )

    flat_expert = expert_ids.reshape(-1)
    flat_rank = slot_rank.reshape(-1)
    earlier = (flat_expert[None, :] == flat_expert[:, None]) & (
        flat_rank[None, :] < flat_rank[:, None]
    )
    kept = (jnp.sum(earlier.astype(jnp.int32), axis=1) < capacity).reshape(local_rows, TOPK)
    marks = 1.0 + kept.T.astype(F32)
    columns = jnp.arange(experts, dtype=jnp.int32)
    code = jnp.sum(
        jnp.where(expert_ids.T[:, None, :] == columns[None, :, None], marks[:, None, :], 0.0), axis=0
    )
    codes = lax.all_gather(code, "dp", axis=0)

    grads = ring_gather(output_grad[:half], output_grad[half:], order)

    qkv_weight = jnp.concatenate([query_weight, key_weight, value_weight], axis=1)
    qkv_blocks = [
        jnp.dot(block, qkv_weight, preferred_element_type=F32).astype(BF) for block in tree_normed
    ]
    out_blocks = tree_gather(after(out_weight, tree_normed[2]))
    qkv, heads = attend_forward(shard_ids, parent_block, qkv_blocks, kv, per_group, seg)
    head_blocks = tree_exchange(
        [heads[j * local_rows : (j + 1) * local_rows] for j in range(count)]
    )
    gate_blocks = tree_gather(after(gate_weight, out_blocks[2]))
    up_blocks = tree_gather(after(up_weight, out_blocks[2]))
    down_blocks = tree_gather(after(down_weight, out_blocks[2]))
    full_gate = jnp.concatenate(gate_blocks, axis=2)
    full_up = jnp.concatenate(up_blocks, axis=2)
    full_down = jnp.concatenate(down_blocks, axis=1)

    hidden = token_values + jnp.dot(
        jnp.concatenate(head_blocks, axis=1),
        jnp.concatenate(out_blocks, axis=0),
        preferred_element_type=F32,
    )
    scale_mlp = rms_scale(hidden)
    mlp_in = (hidden * scale_mlp * mlp_gain).astype(BF)

    rows_held = ring_gather(mlp_in[:half], mlp_in[half:], order)
    mixes, backs, dots, acts, dgates, dups = [], [], [], [], [], []
    order_array = jnp.array(order, jnp.int32)
    for k in range(ring):
        at = jnp.stack(
            [
                dp_index * experts_local,
                order_array[(place - k) % ring],
                order_array[(place + k) % ring],
            ]
        ).astype(jnp.int32)
        mix_a, mix_b, back_a, back_b, pair_dot, act, dgate, dup = expert_step(
            at, rows_held[k], grads[k], codes, router_weight, full_gate, full_up, full_down
        )
        mixes.append((mix_a, mix_b))
        backs.append((back_a, back_b))
        dots.append(pair_dot)
        acts.append(act)
        dgates.append(dgate)
        dups.append(dup)
    grad_rows = ring_reduce(backs, order)
    mixes[1] = tuple(after(m, grad_rows) for m in mixes[1])
    output = (hidden + ring_reduce(mixes, order)).astype(BF)

    steps = jnp.arange(ring, dtype=jnp.int32)
    place_of = jnp.array(places, jnp.int32)
    all_dots = jnp.stack(dots)
    first_half = jnp.arange(local_rows) < half

    def pick(index):
        return jnp.sum(
            jnp.where((index[:, None] == steps[None, :])[:, :, None, None], all_dots[None], 0.0),
            axis=1,
        )

    send = jnp.where(first_half, pick((place - place_of) % ring), pick((place_of - place) % ring))
    grad_gates = lax.all_to_all(send, "dp", 0, 0, tiled=True).reshape(experts, local_rows).T

    code_here = code.T
    logits = jnp.dot(mlp_in, router_weight, preferred_element_type=F32)
    logits = jnp.where(code_here > 0.5, logits, NEG)
    chosen_exp = jnp.exp(logits - jnp.max(logits, axis=1, keepdims=True))
    gates = chosen_exp / jnp.sum(chosen_exp, axis=1, keepdims=True)
    weighted_sum = jnp.sum(gates * grad_gates, axis=1, keepdims=True)
    grad_logits = (gates * (grad_gates - weighted_sum)).astype(BF)
    router_part = jnp.dot(mlp_in.T, grad_logits, preferred_element_type=F32)
    grad_mlp_in = grad_rows + jnp.dot(grad_logits, router_weight.T, preferred_element_type=F32)
    grad_hidden_norm, mlp_gain_part = norm_back(grad_mlp_in, hidden, scale_mlp, mlp_gain)
    grad_hidden = output_grad.astype(F32) + grad_hidden_norm
    grad_attn = grad_hidden.astype(BF)

    grad_blocks = tree_gather(grad_attn)
    grad_head_blocks = [
        jnp.dot(block, out_weight.T, preferred_element_type=F32).astype(BF) for block in grad_blocks
    ]
    dqkv = attend_backward(shard_ids, parent_block, qkv, grad_head_blocks, kv, per_group, seg)
    normed_rows = jnp.concatenate(tree_normed, axis=0)
    out_part = jnp.dot(
        heads.T, jnp.concatenate(grad_blocks, axis=0), preferred_element_type=F32
    ).astype(BF)
    qkv_part = jnp.dot(normed_rows.T, dqkv, preferred_element_type=F32).astype(BF)
    summed = jnp.dot(dqkv, qkv_weight.T, preferred_element_type=F32).astype(BF)
    grad_normed = tree_reduce(
        [summed[j * local_rows : (j + 1) * local_rows] for j in range(count)]
    )
    grad_token_norm, attn_gain_part = norm_back(grad_normed, token_values, scale_attn, attn_gain)
    input_grad = grad_hidden + grad_token_norm

    all_rows = jnp.concatenate([r for pair in rows_held for r in pair], axis=0)
    all_grads = jnp.concatenate([r for pair in grads for r in pair], axis=0)

    def expert_grad(parts, rows, pattern):
        return jnp.einsum(
            pattern, rows, jnp.concatenate(parts, axis=1), preferred_element_type=F32
        ).astype(BF)

    unit = gate_weight.shape[2]
    gate_full = expert_grad(dgates, all_rows, "td,etf->edf")
    up_full = expert_grad(dups, all_rows, "td,etf->edf")
    down_full = expert_grad(acts, all_grads, "td,etf->efd")
    gate_grad = tree_reduce([gate_full[:, :, j * unit : (j + 1) * unit] for j in range(count)])
    up_grad = tree_reduce([up_full[:, :, j * unit : (j + 1) * unit] for j in range(count)])
    down_grad = tree_reduce([down_full[:, j * unit : (j + 1) * unit] for j in range(count)])
    out_grad = lax.psum(out_part, "dp").astype(F32)
    qkv_grad = lax.psum(qkv_part, "dp").astype(F32)
    attn_gain_grad, mlp_gain_grad, router_grad = lax.psum(
        (attn_gain_part, mlp_gain_part, router_part), ("dp", "row", "col")
    )
    return (
        output,
        input_grad,
        attn_gain_grad,
        qkv_grad[:, :q_width],
        qkv_grad[:, q_width : q_width + k_width],
        qkv_grad[:, q_width + k_width :],
        out_grad,
        mlp_gain_grad,
        router_grad,
        gate_grad,
        up_grad,
        down_grad,
    )


def solution(mesh):
    every = ("dp", "row", "col")
    tree = ("row", "col")
    return jax.shard_map(
        shards_program,
        mesh=mesh,
        in_specs=(
            P(every, None),
            P(),
            P(None, tree),
            P(None, tree),
            P(None, tree),
            P(tree, None),
            P(),
            P(),
            P("dp", None, tree),
            P("dp", None, tree),
            P("dp", tree, None),
            P(every, None),
            P(every, None),
            P(every, None),
            P(every),
            P(every),
        ),
        out_specs=(
            P(every, None),
            P(every, None),
            P(),
            P(None, tree),
            P(None, tree),
            P(None, tree),
            P(tree, None),
            P(),
            P(),
            P("dp", None, tree),
            P("dp", None, tree),
            P("dp", tree, None),
        ),
        check_vma=False,
    )
```

time: 1780 us -> 910 us (0.51)
  waiting for transfers between devices: 1010 us -> 306 us
  matrix products: 246 us -> 63.1 us
  local copies, waits for them, and re-layouts: 269 us -> 94.9 us
  starting transfers between devices: 22.1 us -> 97 us
  Pallas kernels: 0 us -> 48.8 us
  other arithmetic: 134 us -> 177 us
  blocking collectives: 52.5 us -> 87.9 us
    all_to_all x4 -> x1, waiting for transfers between devices: 711 us -> 0.01 us  [shards_program(): lax.all_to_all(send, 'dp', 0, 0, tiled=True).reshape(experts, local_rows)]
    ppermute x0 -> x89, waiting for transfers between devices: none -> 270 us  [the longest x14 83.5 us: ring_gather(): b = lax.ppermute(b, 'dp', backward)]
    dot_general x59 -> x18, matrix products: 246 us -> 63.1 us  [the longest x3 35.4 us: expert_grad(): jnp.einsum(pattern, rows, jnp.concatenate(parts, axis=1), preferred_eleme...]
    psum x2, waiting for transfers between devices: 186 us -> 35.9 us  [the longest x1 35.9 us: shards_program(): lax.psum((attn_gain_part, mlp_gain_part, router_part), ('dp', 'row', 'col'))]
    reduce_scatter x3 -> x0, waiting for transfers between devices: 95.7 us -> none  [the longest x1 59.8 us: shards(): lax.psum_scatter(jnp.dot(attn_heads, out_weight, preferred_element_type=j...]
    ppermute x0 -> x89, starting transfers between devices: none -> 92.9 us  [the longest x14 28 us: ring_reduce(): a = lax.ppermute(a, 'dp', onward)]
    pallas_call x0 -> x7, other arithmetic: none -> 87.6 us  [expert_step(): pl.pallas_call(expert_kernel, out_shape=[half_shape] * 4 + [jax.ShapeDtyp...]
    convert_element_type x2 -> x0, local copies, waits for them, and re-layouts: 78 us -> none  [the longest x1 46.8 us: shards(): grad_rows = (grad_rows + jnp.einsum('erf,edf->erd', grad_up_pre, full_up,...]
  transfers between devices with their start and end apart: 16 -> 92, of which waited for: 9 -> 29; matrix products, arithmetic and copies ran while one was open for 24% -> 33% of each run, Pallas kernels for 0% -> 5%
where the time goes in v1:
time: 910 us; the launch traced here: 902 us
  waiting for transfers between devices  306 us (34%)
  other arithmetic  177 us (19%)
  starting transfers between devices  97 us (11%)
  local copies, waits for them, and re-layouts  94.9 us (10%)
  blocking collectives  87.9 us (10%)
  matrix products  63.1 us (7%)
  Pallas kernels  48.8 us (5%)
  between operations  27.2 us (3%)
    pallas_call x7, other arithmetic, expert_step(): pl.pallas_call(expert_kernel, out_shape=[half_shape] * 4 + [jax.ShapeDtyp...  87.6 us
    ppermute x14, waiting for transfers between devices, ring_gather(): b = lax.ppermute(b, 'dp', backward)  83.5 us
    unnamed x266, local copies, waits for them, and re-layouts  73.7 us
    ppermute x14, waiting for transfers between devices, ring_reduce(): a = lax.ppermute(a, 'dp', onward)  70 us
    ppermute x6, waiting for transfers between devices, gather(): across = lax.ppermute(x, 'row', swap)  50.8 us
    all_gather x1, blocking collectives, shards_program(): codes = lax.all_gather(code, 'dp', axis=0)  41.9 us
    psum x1, blocking collectives, shards_program(): lax.psum((attn_gain_part, mlp_gain_part, router_part), ('dp', 'row', 'col'))  40.9 us
    psum x1, waiting for transfers between devices, shards_program(): lax.psum((attn_gain_part, mlp_gain_part, router_part), ('dp', 'row', 'col'))  35.9 us
  transfers between devices with their start and end apart: 92, of which 29 were waited for; matrix products, arithmetic and copies ran while one was open for 33% of the time, Pallas kernels for 5%

profile of v1, /device:TPU:0, one launch (start us, length us, event | category | flops | bytes accessed | tf_op | source)
XLA Modules:
  0.0 901.6 jit_solution(17975248310726058893)
XLA Ops:
  75.0 41.9 %all-gather = f32[128,320]{1,0:T(8,128)} all-gather(f32[16,320]{1,0:T(8,128)S(1)} %select_reduce_fusion.2), channel_id=2, replica_groups=mesh['dp'=8,'row'=2,'col'=2] {'dp'}, dimensions={0}, use_global_device_ids=true | all-gather | bytes 184320 | tf_op jit(solution)/shard_map/all_gather | solution.py:459
  153.6 13.4 %attend_forward.1 = (bf16[1280,640]{1,0:T(8,128)(2,1)S(1)}, bf16[1280,384]{1,0:T(8,128)(2,1)S(1)}) custom-call(s32[4]{0:T(128)S(1)} %pad_add_fusion.shard_ref, s32[20]{0:T(128)S(1)} %select_reduce_fusion.3.parent_ref, bf16[320,640]{1,0:T(8,128)(2,1)S(1)} %convolution_convert_fusion.4.refs_0_, bf16[320,640]{1,0:T(8,128)(2,1)S(1)} %convolution_convert_fusion.3.refs_1_, ...), custom_call_target="tpu_custom_call" | custom-call | flops 6039797760 | bytes 3276800 | tf_op jit(solution)/shard_map/attend_forward/pallas_call | solution.py:149
  172.5 15.2 %collective-permute-done.14 = bf16[2,1536,128]{2,1,0:T(8,128)(2,1)S(1)} collective-permute-done((bf16[2,1536,128]{2,1,0:T(8,128)(2,1)S(1)}, bf16[2,1536,128]{2,1,0:T(8,128)(2,1)S(1)}, u32[]{:S(2)}, u32[]{:S(2)}) %collective-permute-start.14) | collective-permute-done | bytes 786464 | tf_op jit(solution)/shard_map/ppermute | solution.py:318
  189.8 14.9 %collective-permute-done.17 = bf16[2,1536,128]{2,1,0:T(8,128)(2,1)S(1)} collective-permute-done((bf16[2,1536,128]{2,1,0:T(8,128)(2,1)S(1)}, bf16[2,1536,128]{2,1,0:T(8,128)(2,1)S(1)}, u32[]{:S(2)}, u32[]{:S(2)}) %collective-permute-start.17) | collective-permute-done | bytes 786464 | tf_op jit(solution)/shard_map/ppermute | solution.py:318
  248.5 12.8 %expert_step.8 = (bf16[160,1536]{1,0:T(8,128)(2,1)}, bf16[160,1536]{1,0:T(8,128)(2,1)}, bf16[160,1536]{1,0:T(8,128)(2,1)}, bf16[160,1536]{1,0:T(8,128)(2,1)}, f3...) custom-call(s32[3]{0:T(128)} %pad_add_fusion.8.at_ref, ...), custom_call_target="tpu_custom_call" | custom-call | flops 12079595520 | bytes 14352384 | tf_op jit(solution)/shard_map/expert_step/pallas_call | solution.py:291
  266.7 13.0 %expert_step.15 = (f32[8,2,320]{2,1,0:T(2,128)S(1)}, bf16[160,1536]{1,0:T(8,128)(2,1)}, bf16[160,1536]{1,0:T(8,128)(2,1)}, bf16[160,1536]{1,0:T(8,128)(2,1)}, bf...) fusion(f32[8,2,320]{2,1,0:T(2,128)S(1)} %constant_dynamic-updat, ...), kind=kCustom, calls=%fused_computation.141 | custom fusion | flops 12079595520 | bytes 15584768 | tf_op jit(solution)/shard_map/expert_step/pallas_call | solution.py:291
  289.1 13.3 %collective-permute-done.24 = bf16[160,1536]{1,0:T(8,128)(2,1)S(1)} collective-permute-done((bf16[160,1536]{1,0:T(8,128)(2,1)}, bf16[160,1536]{1,0:T(8,128)(2,1)S(1)}, u32[]{:S(2)}, u32[]{:S(2)}) %collective-permute-start.24) | collective-permute-done | bytes 491552 | tf_op jit(solution)/shard_map/ppermute | solution.py:375
  304.0 12.8 %expert_step.14 = (f32[8,2,320]{2,1,0:T(2,128)S(1)}, bf16[160,1536]{1,0:T(8,128)(2,1)}, bf16[160,1536]{1,0:T(8,128)(2,1)}, bf16[160,1536]{1,0:T(8,128)(2,1)}, bf...) fusion(f32[8,2,320]{2,1,0:T(2,128)S(1)} %get-tuple-element.237,, ...), kind=kCustom, calls=%fused_computation.140 | custom fusion | flops 12079595520 | bytes 15584768 | tf_op jit(solution)/shard_map/expert_step/pallas_call | solution.py:291
  329.8 13.1 %collective-permute-done.29 = bf16[160,1536]{1,0:T(8,128)(2,1)S(1)} collective-permute-done((bf16[160,1536]{1,0:T(8,128)(2,1)S(1)}, bf16[160,1536]{1,0:T(8,128)(2,1)S(1)}, u32[]{:S(2)}, u32[]{:S(2)}) %collective-permute-start.29) | collective-permute-done | bytes 491552 | tf_op jit(solution)/shard_map/ppermute | solution.py:375
  344.5 12.8 %expert_step.13 = (f32[8,2,320]{2,1,0:T(2,128)S(1)}, bf16[160,1536]{1,0:T(8,128)(2,1)}, bf16[160,1536]{1,0:T(8,128)(2,1)}, bf16[160,1536]{1,0:T(8,128)(2,1)}, bf...) fusion(f32[8,2,320]{2,1,0:T(2,128)S(1)} %get-tuple-element.253,, ...), kind=kCustom, calls=%fused_computation.139 | custom fusion | flops 12079595520 | bytes 15584768 | tf_op jit(solution)/shard_map/expert_step/pallas_call | solution.py:291
  370.4 11.9 %collective-permute-done.34 = bf16[160,1536]{1,0:T(8,128)(2,1)S(1)} collective-permute-done((bf16[160,1536]{1,0:T(8,128)(2,1)S(1)}, bf16[160,1536]{1,0:T(8,128)(2,1)S(1)}, u32[]{:S(2)}, u32[]{:S(2)}) %collective-permute-start.34) | collective-permute-done | bytes 491552 | tf_op jit(solution)/shard_map/ppermute | solution.py:375
  383.9 12.5 %expert_step.12 = (f32[8,2,320]{2,1,0:T(2,128)S(1)}, bf16[160,1536]{1,0:T(8,128)(2,1)}, bf16[160,1536]{1,0:T(8,128)(2,1)}, bf16[160,1536]{1,0:T(8,128)(2,1)}, bf...) fusion(f32[8,2,320]{2,1,0:T(2,128)S(1)} %get-tuple-element.221,, ...), kind=kCustom, calls=%fused_computation.138 | custom fusion | flops 12079595520 | bytes 15584768 | tf_op jit(solution)/shard_map/expert_step/pallas_call | solution.py:291
  420.2 12.2 %expert_step.11 = (f32[8,2,320]{2,1,0:T(2,128)S(1)}, bf16[160,1536]{1,0:T(8,128)(2,1)}, bf16[160,1536]{1,0:T(8,128)(2,1)}, bf16[160,1536]{1,0:T(8,128)(2,1)}, bf...) fusion(f32[8,2,320]{2,1,0:T(2,128)S(1)} %get-tuple-element.301,, ...), kind=kCustom, calls=%fused_computation.137 | custom fusion | flops 12079595520 | bytes 15584768 | tf_op jit(solution)/shard_map/expert_step/pallas_call | solution.py:291
  455.4 11.8 %expert_step.10 = (f32[8,2,320]{2,1,0:T(2,128)S(1)}, bf16[160,1536]{1,0:T(8,128)(2,1)S(1)}, bf16[160,1536]{1,0:T(8,128)(2,1)S(1)}, bf16[160,1536]{1,0:T(8,128)(2...) fusion(f32[8,2,320]{2,1,0:T(2,128)S(1)} %get-tuple-element.269,, ...), kind=kCustom, calls=%fused_computation.136 | custom fusion | flops 12079595520 | bytes 15584768 | tf_op jit(solution)/shard_map/expert_step/pallas_call | solution.py:291
  489.5 12.6 %expert_step.9 = (f32[8,2,320]{2,1,0:T(2,128)S(1)}, bf16[160,1536]{1,0:T(8,128)(2,1)}, bf16[160,1536]{1,0:T(8,128)(2,1)}, bf16[160,1536]{1,0:T(8,128)(2,1)}, bf1...) fusion(f32[8,2,320]{2,1,0:T(2,128)S(1)} %get-tuple-element.285,, ...), kind=kCustom, calls=%fused_computation.135 | custom fusion | flops 12079595520 | bytes 15584768 | tf_op jit(solution)/shard_map/expert_step/pallas_call | solution.py:291
  514.7 12.3 %fusion.36 = bf16[2,512,1536]{2,1,0:T(8,128)(2,1)S(1)} fusion(bf16[2,2560,512]{2,1,0:T(8,128)(2,1)} %constant_dynamic-update-slice_fusion.54, bf16[2560,1536]{1,0:T(8,128)(2,1)} %constant_dynamic-update-slice_fusion.62), kind=kOutput, calls=%fused_computation.39 | convolution fusion | flops 8054636544 | bytes 16252928 | tf_op jit(solution)/shard_map/td,etf->efd/dot_general | solution.py:559
  567.4 22.5 %attend_backward.1 = bf16[1280,640]{1,0:T(8,128)(2,1)S(1)} custom-call(s32[4]{0:T(128)S(1)} %pad_add_fusion.shard_ref, s32[20]{0:T(128)S(1)} %select_reduce_fusion.3.parent_ref, bf16[1280,640]{1,0:T(8,128)(2,1)S(1)} %get-tuple-element.131.qkv_ref, bf16[320,384]{1,0:T(8,128)(2,1)S(1)} %convolution_convert_fusion.8.refs_0_, ...), custom_call_target="tpu_custom_call" | custom-call | flops 15099494400 | bytes 4915200 | tf_op jit(solution)/shard_map/attend_backward/pallas_call | solution.py:214
  599.3 12.4 %fusion.39 = bf16[2,1536,512]{1,2,0:T(8,128)(2,1)S(1)} fusion(bf16[2,2560,512]{2,1,0:T(8,128)(2,1)} %constant_dynamic-update-slice_fusion.46, bf16[2560,1536]{1,0:T(8,128)(2,1)} %constant_dynamic-update-slice_fusion.31), kind=kOutput, calls=%fused_computation.40 | convolution fusion | flops 8054636544 | bytes 16252928 | tf_op jit(solution)/shard_map/td,etf->edf/dot_general | solution.py:559
  624.3 18.4 %collective-permute-done.60 = bf16[160,1536]{1,0:T(8,128)(2,1)S(1)} collective-permute-done((bf16[160,1536]{1,0:T(8,128)(2,1)}, bf16[160,1536]{1,0:T(8,128)(2,1)S(1)}, u32[]{:S(2)}, u32[]{:S(2)}) %collective-permute-start.60) | collective-permute-done | bytes 491552 | tf_op jit(solution)/shard_map/ppermute | solution.py:384
  653.4 18.1 %collective-permute-done.61 = bf16[160,1536]{1,0:T(8,128)(2,1)S(1)} collective-permute-done((bf16[160,1536]{1,0:T(8,128)(2,1)S(1)}, bf16[160,1536]{1,0:T(8,128)(2,1)S(1)}, u32[]{:S(2)}, u32[]{:S(2)}) %collective-permute-start.61) | collective-permute-done | bytes 491552 | tf_op jit(solution)/shard_map/ppermute | solution.py:384
  692.9 12.6 %collective-permute-done.85 = bf16[2,1536,128]{1,2,0:T(8,128)(2,1)} collective-permute-done((bf16[2,1536,128]{1,2,0:T(8,128)(2,1)}, bf16[2,1536,128]{1,2,0:T(8,128)(2,1)}, u32[]{:S(2)}, u32[]{:S(2)}) %collective-permute-start.85) | collective-permute-done | bytes 786464 | tf_op jit(solution)/shard_map/ppermute | solution.py:332
  727.1 19.0 %collective-permute-done.63 = bf16[160,1536]{1,0:T(8,128)(2,1)S(1)} collective-permute-done((bf16[160,1536]{1,0:T(8,128)(2,1)S(1)}, bf16[160,1536]{1,0:T(8,128)(2,1)S(1)}, u32[]{:S(2)}, u32[]{:S(2)}) %collective-permute-start.63) | collective-permute-done | bytes 491552 | tf_op jit(solution)/shard_map/ppermute | solution.py:384
  804.8 40.9 %all-reduce = (f32[1536]{0:T(1024)}, f32[1536]{0:T(1024)}) all-reduce(f32[1536]{0:T(1024)S(1)} %get-tuple-element.316, f32[1536]{0:T(1024)S(1)} %get-tuple-element.318), channel_id=1, replica_groups=mesh['dp'=8,'row'=2,'col'=2] {'dp','row','col'}, use_global_device_ids=true, to_apply=%region_13.14 | all-reduce | flops 3072 | bytes 24576 | tf_op jit(solution)/shard_map/psum | solution.py:572
  856.9 35.9 %all-reduce.5.cloned.1.call-done = f32[1536,16]{0,1:T(8,128)} async-done(((f32[1536,16]{0,1:T(8,128)}), f32[1536,16]{0,1:T(8,128)}) %all-reduce.5.cloned.1.call-update) | async-done | bytes 98320 | tf_op jit(solution)/shard_map/psum | solution.py:572
  (559 shorter events, 458.1 us)
Async XLA Ops:
  10.4 111.1 %collective-permute-start.1 = (bf16[320,1536]{1,0:T(8,128)(2,1)S(1)}, bf16[320,1536]{1,0:T(8,128)(2,1)}, u32[]{:S(2)}, u32[]{:S(2)}) collective-permute-start(bf16[320,1536]{1,0:T(8,128)(2,1)S(1)} %fusion.55), channel_id=1, source_target_pairs={{0,2},{2,0},{1,3},{3,1},{4,6},{6,4},{5,7},{7,5},{8,10},{10,8},{9,1... | collective-permute-start | bytes 2949128 | tf_op jit(solution)/shard_map/ppermute | solution.py:318
  13.4 114.4 %collective-permute-start = (bf16[320,1536]{1,0:T(8,128)(2,1)S(1)}, bf16[320,1536]{1,0:T(8,128)(2,1)}, u32[]{:S(2)}, u32[]{:S(2)}) collective-permute-start(bf16[320,1536]{1,0:T(8,128)(2,1)S(1)} %fusion.55), channel_id=1, source_target_pairs={{0,1},{1,0},{2,3},{3,2},{4,5},{5,4},{6,7},{7,6},{8,9},{9,8},{10,11... | collective-permute-start | bytes 2949128 | tf_op jit(solution)/shard_map/ppermute | solution.py:319
  14.5 58.4 %collective-permute-start.12 = (bf16[160,1536]{1,0:T(8,128)(2,1)}, bf16[160,1536]{1,0:T(8,128)(2,1)}, u32[]{:S(2)}, u32[]{:S(2)}) collective-permute-start(bf16[160,1536]{1,0:T(8,128)(2,1)} %get-tuple-element.340.gb_ref), channel_id=1, source_target_pairs={{8,0},{16,8},{24,16},{28,24},{20,28},{12,20},{4,12},{0,4},{9,1},{1... | collective-permute-start | bytes 1474568 | tf_op jit(solution)/shard_map/ppermute | solution.py:375
  16.0 58.5 %collective-permute-start.11 = (bf16[160,1536]{1,0:T(8,128)(2,1)}, bf16[160,1536]{1,0:T(8,128)(2,1)}, u32[]{:S(2)}, u32[]{:S(2)}) collective-permute-start(bf16[160,1536]{1,0:T(8,128)(2,1)} %get-tuple-element.341.ga_ref), channel_id=1, source_target_pairs={{0,8},{8,16},{16,24},{24,28},{28,20},{20,12},{12,4},{4,0},{1,9},{9... | collective-permute-start | bytes 1474568 | tf_op jit(solution)/shard_map/ppermute | solution.py:374
  72.9 49.2 %collective-permute-start.26 = (bf16[160,1536]{1,0:T(8,128)(2,1)}, bf16[160,1536]{1,0:T(8,128)(2,1)S(1)}, u32[]{:S(2)}, u32[]{:S(2)}) collective-permute-start(bf16[160,1536]{1,0:T(8,128)(2,1)} %collective-permute-done.12), channel_id=1, source_target_pairs={{8,0},{16,8},{24,16},{28,24},{20,28},{12,20},{4,12},{0,4},{9,1},{1... | collective-permute-start | bytes 1474568 | tf_op jit(solution)/shard_map/ppermute | solution.py:375
  74.5 47.7 %collective-permute-start.25 = (bf16[160,1536]{1,0:T(8,128)(2,1)}, bf16[160,1536]{1,0:T(8,128)(2,1)S(1)}, u32[]{:S(2)}, u32[]{:S(2)}) collective-permute-start(bf16[160,1536]{1,0:T(8,128)(2,1)} %collective-permute-done.11), channel_id=1, source_target_pairs={{0,8},{8,16},{16,24},{24,28},{28,20},{20,12},{12,4},{4,0},{1,9},{9... | collective-permute-start | bytes 1474568 | tf_op jit(solution)/shard_map/ppermute | solution.py:374
  121.6 45.7 %collective-permute-start.7 = (bf16[384,1536]{1,0:T(8,128)(2,1)}, bf16[384,1536]{1,0:T(8,128)(2,1)S(1)}, u32[]{:S(2)}, u32[]{:S(2)}) collective-permute-start(bf16[384,1536]{1,0:T(8,128)(2,1)} %param.24), channel_id=1, source_target_pairs={{0,2},{2,0},{1,3},{3,1},{4,6},{6,4},{5,7},{7,5},{8,10},{10,8},{9,1... | collective-permute-start | bytes 3538952 | tf_op jit(solution)/shard_map/ppermute | solution.py:318
  122.1 100.3 %collective-permute-start.6 = (bf16[384,1536]{1,0:T(8,128)(2,1)}, bf16[384,1536]{1,0:T(8,128)(2,1)S(1)}, u32[]{:S(2)}, u32[]{:S(2)}) collective-permute-start(bf16[384,1536]{1,0:T(8,128)(2,1)} %param.24), channel_id=1, source_target_pairs={{0,1},{1,0},{2,3},{3,2},{4,5},{5,4},{6,7},{7,6},{8,9},{9,8},{10,11... | collective-permute-start | bytes 3538952 | tf_op jit(solution)/shard_map/ppermute | solution.py:319
  189.5 43.2 %collective-permute-start.8 = (bf16[384,1536]{1,0:T(8,128)(2,1)S(1)}, bf16[384,1536]{1,0:T(8,128)(2,1)S(1)}, u32[]{:S(2)}, u32[]{:S(2)}) collective-permute-start(bf16[384,1536]{1,0:T(8,128)(2,1)S(1)} %collective-permute-done.7), channel_id=1, source_target_pairs={{0,1},{1,0},{2,3},{3,2},{4,5},{5,4},{6,7},{7,6},{8,9},{9,8},{10,11... | collective-permute-start | bytes 3538952 | tf_op jit(solution)/shard_map/ppermute | solution.py:320
  279.7 37.2 %collective-permute-start.22 = (bf16[160,1536]{1,0:T(8,128)(2,1)}, bf16[160,1536]{1,0:T(8,128)(2,1)}, u32[]{:S(2)}, u32[]{:S(2)}) collective-permute-start(bf16[160,1536]{1,0:T(8,128)(2,1)} %get-tuple-element.240), channel_id=1, source_target_pairs={{0,8},{8,16},{16,24},{24,28},{28,20},{20,12},{12,4},{4,0},{1,9},{9... | collective-permute-start | bytes 1474568 | tf_op jit(solution)/shard_map/ppermute | solution.py:384
  280.0 39.6 %collective-permute-start.53 = (bf16[160,1536]{1,0:T(8,128)(2,1)}, bf16[160,1536]{1,0:T(8,128)(2,1)}, u32[]{:S(2)}, u32[]{:S(2)}) collective-permute-start(bf16[160,1536]{1,0:T(8,128)(2,1)} %get-tuple-element.242), channel_id=1, source_target_pairs={{8,0},{16,8},{24,16},{28,24},{20,28},{12,20},{4,12},{0,4},{9,1},{1... | collective-permute-start | bytes 1474568 | tf_op jit(solution)/shard_map/ppermute | solution.py:385
  319.1 38.2 %collective-permute-start.27 = (bf16[160,1536]{1,0:T(8,128)(2,1)}, bf16[160,1536]{1,0:T(8,128)(2,1)}, u32[]{:S(2)}, u32[]{:S(2)}) collective-permute-start(bf16[160,1536]{1,0:T(8,128)(2,1)} %add_convert_fusion.27), channel_id=1, source_target_pairs={{0,8},{8,16},{16,24},{24,28},{28,20},{20,12},{12,4},{4,0},{1,9},{9... | collective-permute-start | bytes 1474568 | tf_op jit(solution)/shard_map/ppermute | solution.py:384
  321.7 38.5 %collective-permute-start.54 = (bf16[160,1536]{1,0:T(8,128)(2,1)}, bf16[160,1536]{1,0:T(8,128)(2,1)}, u32[]{:S(2)}, u32[]{:S(2)}) collective-permute-start(bf16[160,1536]{1,0:T(8,128)(2,1)} %add_convert_fusion.21), channel_id=1, source_target_pairs={{8,0},{16,8},{24,16},{28,24},{20,28},{12,20},{4,12},{0,4},{9,1},{1... | collective-permute-start | bytes 1474568 | tf_op jit(solution)/shard_map/ppermute | solution.py:385
  362.3 36.9 %collective-permute-start.55 = (bf16[160,1536]{1,0:T(8,128)(2,1)}, bf16[160,1536]{1,0:T(8,128)(2,1)}, u32[]{:S(2)}, u32[]{:S(2)}) collective-permute-start(bf16[160,1536]{1,0:T(8,128)(2,1)} %add_convert_fusion.20), channel_id=1, source_target_pairs={{8,0},{16,8},{24,16},{28,24},{20,28},{12,20},{4,12},{0,4},{9,1},{1... | collective-permute-start | bytes 1474568 | tf_op jit(solution)/shard_map/ppermute | solution.py:385
  469.2 37.9 %collective-permute-start.47 = (bf16[160,1536]{1,0:T(8,128)(2,1)}, bf16[160,1536]{1,0:T(8,128)(2,1)}, u32[]{:S(2)}, u32[]{:S(2)}) collective-permute-start(bf16[160,1536]{1,0:T(8,128)(2,1)} %add_convert_fusion.23), channel_id=1, source_target_pairs={{0,8},{8,16},{16,24},{24,28},{28,20},{20,12},{12,4},{4,0},{1,9},{9... | collective-permute-start | bytes 1474568 | tf_op jit(solution)/shard_map/ppermute | solution.py:384
  472.9 38.3 %collective-permute-start.58 = (bf16[160,1536]{1,0:T(8,128)(2,1)}, bf16[160,1536]{1,0:T(8,128)(2,1)}, u32[]{:S(2)}, u32[]{:S(2)}) collective-permute-start(bf16[160,1536]{1,0:T(8,128)(2,1)} %add_convert_fusion.17), channel_id=1, source_target_pairs={{8,0},{16,8},{24,16},{28,24},{20,28},{12,20},{4,12},{0,4},{9,1},{1... | collective-permute-start | bytes 1474568 | tf_op jit(solution)/shard_map/ppermute | solution.py:385
  507.0 343.9 %all-reduce.7.cloned.1.call-start = ((), (), s32[]{:S(2)}) async-start(), calls=%async_computation.2 | async-start | bytes 6291456 | tf_op jit(solution)/shard_map/psum | solution.py:571
  530.0 179.0 %collective-permute-start.86 = (bf16[2,128,1536]{2,1,0:T(8,128)(2,1)}, bf16[2,128,1536]{2,1,0:T(8,128)(2,1)}, u32[]{:S(2)}, u32[]{:S(2)}) collective-permute-start(bf16[2,128,1536]{2,1,0:T(8,128)(2,1)} %get-tuple-element.330), channel_id=1, source_target_pairs={{0,1},{1,0},{2,3},{3,2},{4,5},{5,4},{6,7},{7,6},{8,9},{9,8},{10,11... | collective-permute-start | bytes 2359304 | tf_op jit(solution)/shard_map/ppermute | solution.py:333
  530.0 85.7 %collective-permute-start.87 = (bf16[2,128,1536]{2,1,0:T(8,128)(2,1)}, bf16[2,128,1536]{2,1,0:T(8,128)(2,1)}, u32[]{:S(2)}, u32[]{:S(2)}) collective-permute-start(bf16[2,128,1536]{2,1,0:T(8,128)(2,1)} %get-tuple-element.331), channel_id=1, source_target_pairs={{0,1},{1,0},{2,3},{3,2},{4,5},{5,4},{6,7},{7,6},{8,9},{9,8},{10,11... | collective-permute-start | bytes 2359304 | tf_op jit(solution)/shard_map/ppermute | solution.py:331
  553.6 132.3 %collective-permute-start.80 = (bf16[2,1536,128]{1,2,0:T(8,128)(2,1)}, bf16[2,1536,128]{1,2,0:T(8,128)(2,1)}, u32[]{:S(2)}, u32[]{:S(2)}) collective-permute-start(bf16[2,1536,128]{1,2,0:T(8,128)(2,1)} %get-tuple-element.334), channel_id=1, source_target_pairs={{0,1},{1,0},{2,3},{3,2},{4,5},{5,4},{6,7},{7,6},{8,9},{9,8},{10,11... | collective-permute-start | bytes 2359304 | tf_op jit(solution)/shard_map/ppermute | solution.py:333
  565.4 52.9 %collective-permute-start.81 = (bf16[2,1536,128]{1,2,0:T(8,128)(2,1)}, bf16[2,1536,128]{1,2,0:T(8,128)(2,1)}, u32[]{:S(2)}, u32[]{:S(2)}) collective-permute-start(bf16[2,1536,128]{1,2,0:T(8,128)(2,1)} %get-tuple-element.335), channel_id=1, source_target_pairs={{0,1},{1,0},{2,3},{3,2},{4,5},{5,4},{6,7},{7,6},{8,9},{9,8},{10,11... | collective-permute-start | bytes 2359304 | tf_op jit(solution)/shard_map/ppermute | solution.py:331
  599.3 293.5 %all-reduce.5.cloned.1.call-start = ((), (), s32[]{:S(2)}) async-start(), calls=%async_computation.1 | async-start | bytes 196608 | tf_op jit(solution)/shard_map/psum | solution.py:572
  614.3 77.3 %collective-permute-start.83 = (bf16[2,1536,128]{1,2,0:T(8,128)(2,1)}, bf16[2,1536,128]{1,2,0:T(8,128)(2,1)}, u32[]{:S(2)}, u32[]{:S(2)}) collective-permute-start(bf16[2,1536,128]{1,2,0:T(8,128)(2,1)} %get-tuple-element.332), channel_id=1, source_target_pairs={{0,1},{1,0},{2,3},{3,2},{4,5},{5,4},{6,7},{7,6},{8,9},{9,8},{10,11... | collective-permute-start | bytes 2359304 | tf_op jit(solution)/shard_map/ppermute | solution.py:333
  642.7 44.9 %collective-permute-start.82 = (bf16[2,1536,128]{1,2,0:T(8,128)(2,1)S(1)}, bf16[2,1536,128]{1,2,0:T(8,128)(2,1)S(1)}, u32[]{:S(2)}, u32[]{:S(2)}) collective-permute-start(bf16[2,1536,128]{1,2,0:T(8,128)(2,1)S(1)} %add_convert_fusion.3), channel_id=1, source_target_pairs={{0,2},{2,0},{1,3},{3,1},{4,6},{6,4},{5,7},{7,5},{8,10},{10,8},{9,1... | collective-permute-start | bytes 2359304 | tf_op jit(solution)/shard_map/ppermute | solution.py:332
  (168 other events, 2886.6 us)
Sparse Core Ops, SparseCore 0:
  599.4 160.4 all-reduce.6
  766.9 125.8 all-reduce.4

commit v2 on v1

--- a/solution.py
+++ b/solution.py
@@ -18,14 +18,15 @@
 F32 = jnp.float32
 VMEM = pl.BlockSpec(memory_space=pltpu.VMEM)
 SMEM = pl.BlockSpec(memory_space=pltpu.SMEM)
+ANY = pl.BlockSpec(memory_space=pl.ANY)
 
 
 def dot(a, b, ca, cb):
     return lax.dot_general(a, b, (((ca,), (cb,)), ((), ())), preferred_element_type=F32)
 
 
-def after(value, *earlier):
-    return lax.optimization_barrier((value,) + earlier)[0]
+def tie(*values):
+    return lax.optimization_barrier(values)
 
 
 def stack_heads(block, count):
@@ -117,11 +118,11 @@
 
 def attend_forward_kernel(kv, per_group, seg, blocks, shard_ref, parent_ref, *refs):
     ins, (qkv_ref, out_ref, full_ref) = refs[:blocks], refs[blocks:]
-    local = ins[0].shape[0]
+    local = out_ref.shape[0] // blocks
     scale = BF(1.0 / math.sqrt(HD))
     for j in range(blocks):
         at = pl.multiple_of(shard_ref[j] * local, 64)
-        qkv_ref[pl.ds(at, local), :] = ins[j][...]
+        qkv_ref[pl.ds(at, local), :] = ins[j][0:local, :]
 
     def work(first, g, keys, values, masks, places):
         block = qkv_ref[pl.ds(first, QT), g * per_group * HD : (g + 1) * per_group * HD]
@@ -142,8 +143,8 @@
 
 def attend_forward(shards, parent_block, qkv_blocks, kv, per_group, seg):
     blocks = len(qkv_blocks)
-    local, wide = qkv_blocks[0].shape
-    rows = blocks * local
+    wide = qkv_blocks[0].shape[1]
+    rows = 20 * seg
     width = kv * per_group * HD
     cells = rows * 12 * seg * kv * per_group
     return pl.pallas_call(
@@ -230,17 +231,59 @@
     )(shards, parent_block, qkv, *grad_blocks)
 
 
-def expert_kernel(
-    at_ref, xa_ref, xb_ref, ga_ref, gb_ref, code_ref, router_ref, gate_ref, up_ref, down_ref,
-    mix_a_ref, mix_b_ref, back_a_ref, back_b_ref, dot_ref, act_ref, dgate_ref, dup_ref,
-):
-    half = xa_ref.shape[0]
-    x = jnp.concatenate([xa_ref[...], xb_ref[...]], axis=0)
-    g = jnp.concatenate([ga_ref[...], gb_ref[...]], axis=0)
-    code_a = code_ref[at_ref[1]]
-    code_b = code_ref[at_ref[2]]
-    token = lax.broadcasted_iota(jnp.int32, code_a.shape, 1)
-    code = jnp.where(token < half, code_a, code_b).T
+def expert_kernel(first, blocks, fresh, at_ref, xa_ref, xb_ref, grads_ref, router_ref, *refs):
+    count = len(blocks)
+    weight_refs, refs = refs[: sum(blocks)], refs[sum(blocks) :]
+    if not fresh:
+        refs = refs[6:]
+    back_a_ref, back_b_ref, dot_ref, mix_ref, rows_ref, grad_rows_ref, *kept_refs = refs[:9]
+    weights, held, g_held, mix_held, weight_sem, held_sem, row_sem, g_sem, mix_sem = refs[9:]
+    half = back_a_ref.shape[0]
+    rows = 2 * half
+    experts = router_ref.shape[1]
+    spots = [pl.multiple_of(at_ref[1 + i] * rows + i * half, 16) for i in range(2)]
+    arrived = []
+    for i in range(2):
+        copy = pltpu.make_async_copy(
+            grads_ref.at[pl.ds(spots[i], half)], g_held.at[pl.ds(i * half, half)], g_sem.at[i]
+        )
+        copy.start()
+        arrived.append(copy)
+    loads = []
+    for i in (2, 0, 1):
+        for n in range(count):
+            at = sum(blocks[:n])
+            for j in range(blocks[n]):
+                source = weight_refs[at + j].at[i]
+                unit = source.shape[1]
+                copy = pltpu.make_async_copy(
+                    source,
+                    weights[i].at[n, :, pl.ds(j * unit, unit)],
+                    weight_sem.at[i * sum(blocks) + at + j],
+                )
+                loads.append((n, i, copy))
+    for n in range(count):
+        for m, _, copy in loads:
+            if m == n:
+                copy.start()
+
+    def loaded(n, i):
+        for m, k, copy in loads:
+            if (m, k) == (n, i):
+                copy.wait()
+
+    stores = []
+    for i, ref in enumerate((xa_ref, xb_ref)):
+        stores.append(
+            pltpu.make_async_copy(
+                ref.at[pl.ds(0, half)], rows_ref.at[pl.ds(first + i * half, half)], row_sem.at[i]
+            )
+        )
+        stores[-1].start()
+    x = jnp.concatenate([xa_ref[0:half], xb_ref[0:half]], axis=0)
+    code = jnp.concatenate(
+        [ref[half : half + experts, 0:half].astype(F32).T for ref in (xa_ref, xb_ref)], axis=0
+    )
     logits = dot(x, router_ref[...], 1, 0)
     logits = jnp.where(code > 0.5, logits, NEG)
     top = jnp.max(logits, axis=1, keepdims=True)
@@ -248,16 +291,24 @@
     kept = jnp.where(code > 1.5, 1.0, 0.0)
     gates = kept * e / jnp.sum(e, axis=1, keepdims=True)
     lane = lax.broadcasted_iota(jnp.int32, gates.shape, 1)
-    count = gate_ref.shape[0]
+    for copy in arrived:
+        copy.wait()
+    copy = pltpu.make_async_copy(g_held, grad_rows_ref.at[pl.ds(first, rows)], row_sem.at[2])
+    copy.start()
+    stores.append(copy)
+    g = g_held[...]
     mix = None
     back = None
     for n in range(count):
         mine = lane == at_ref[0] + n
         weight = jnp.sum(jnp.where(mine, gates, 0.0), axis=1, keepdims=True)
         keep = jnp.sum(jnp.where(mine, kept, 0.0), axis=1, keepdims=True)
-        gate_pre = dot(x, gate_ref[n], 1, 0)
-        up_pre = dot(x, up_ref[n], 1, 0)
-        grad = dot(g, down_ref[n], 1, 1)
+        loaded(n, 2)
+        grad = dot(g, weights[2][n], 1, 0)
+        loaded(n, 0)
+        gate_pre = dot(x, weights[0][n], 1, 0)
+        loaded(n, 1)
+        up_pre = dot(x, weights[1][n], 1, 0)
         sig = 1.0 / (1.0 + jnp.exp(-gate_pre))
         silu = gate_pre * sig
         act = (silu * up_pre).astype(BF).astype(F32)
@@ -267,128 +318,267 @@
         grad = grad * weight
         dgate = (grad * up_pre * sig * (1.0 + gate_pre * (1.0 - sig))).astype(BF)
         dup = (grad * silu).astype(BF)
-        act_ref[n] = weighted
-        dgate_ref[n] = dgate
-        dup_ref[n] = dup
-        m = dot(weighted, down_ref[n], 1, 0)
+        for i, value in enumerate((weighted, dgate, dup)):
+            held[i][n] = value
+            copy = pltpu.make_async_copy(
+                held[i].at[n], kept_refs[i].at[n, pl.ds(first, rows)], held_sem.at[n * 3 + i]
+            )
+            copy.start()
+            stores.append(copy)
+        m = dot(weighted, weights[2][n], 1, 1)
         mix = m if mix is None else mix + m
-        b = dot(dgate, gate_ref[n], 1, 1) + dot(dup, up_ref[n], 1, 1)
+        b = dot(dgate, weights[0][n], 1, 1) + dot(dup, weights[1][n], 1, 1)
         back = b if back is None else back + b
-    mix = mix.astype(BF)
+    mix_held[...] = mix.astype(BF)
+    for i in range(2):
+        copy = pltpu.make_async_copy(
+            mix_held.at[pl.ds(i * half, half)], mix_ref.at[pl.ds(spots[i], half)], mix_sem.at[i]
+        )
+        copy.start()
+        stores.append(copy)
     back = back.astype(BF)
-    mix_a_ref[...] = mix[:half]
-    mix_b_ref[...] = mix[half:]
     back_a_ref[...] = back[:half]
     back_b_ref[...] = back[half:]
-
-
-def expert_step(at, x, g, codes, router, gate, up, down):
-    half, width = x[0].shape
-    count, _, hidden = gate.shape
+    for copy in stores:
+        copy.wait()
+
+
+def expert_step(k, steps, at, x, grads, router, weights, buffers):
+    width = x[0].shape[1]
+    half = grads.shape[0] // steps // 2
     rows = 2 * half
+    count = len(weights)
+    hidden = sum(w.shape[2] for w in weights[0])
     half_shape = jax.ShapeDtypeStruct((half, width), BF)
-    kept_shape = jax.ShapeDtypeStruct((count, rows, hidden), BF)
-    return pl.pallas_call(
-        expert_kernel,
-        out_shape=[half_shape] * 4
-        + [jax.ShapeDtypeStruct((count, rows), F32)]
-        + [kept_shape] * 3,
-        in_specs=[SMEM] + [VMEM] * 9,
-        out_specs=[VMEM] * 8,
-        compiler_params=pltpu.CompilerParams(vmem_limit_bytes=56 * MIB),
+    big_shapes = [jax.ShapeDtypeStruct((steps * rows, width), BF)] * 3
+    big_shapes += [jax.ShapeDtypeStruct((count, steps * rows, hidden), BF)] * 3
+    operands = [at, *x, grads, router, *[b for w in weights for b in w]]
+    specs = [SMEM, VMEM, VMEM, ANY, VMEM] + [ANY] * (len(operands) - 5)
+    aliases = {}
+    if buffers is not None:
+        aliases = {len(operands) + i: 3 + i for i in range(6)}
+        operands += buffers
+        specs += [ANY] * 6
+    blocks = [len(w) for w in weights]
+    out = pl.pallas_call(
+        functools.partial(expert_kernel, k * rows, blocks, buffers is None),
+        out_shape=[half_shape] * 2 + [jax.ShapeDtypeStruct((count, rows), F32)] + big_shapes,
+        in_specs=specs,
+        out_specs=[VMEM] * 3 + [ANY] * 6,
+        input_output_aliases=aliases,
+        scratch_shapes=[
+            [pltpu.VMEM((count, width, hidden), BF)] * 3,
+            [pltpu.VMEM((count, rows, hidden), BF)] * 3,
+            pltpu.VMEM((rows, width), BF),
+            pltpu.VMEM((rows, width), BF),
+            pltpu.SemaphoreType.DMA((3 * sum(blocks),)),
+            pltpu.SemaphoreType.DMA((count * 3,)),
+            pltpu.SemaphoreType.DMA((3,)),
+            pltpu.SemaphoreType.DMA((2,)),
+            pltpu.SemaphoreType.DMA((2,)),
+        ],
+        compiler_params=pltpu.CompilerParams(vmem_limit_bytes=40 * MIB),
         cost_estimate=pl.CostEstimate(
-            flops=2 * rows * width * hidden * count * 6 * 2,
+            flops=2 * rows * width * hidden * count * 6,
             bytes_accessed=6 * width * hidden * count + 10 * rows * width,
             transcendentals=rows * hidden * count,
         ),
         name="expert_step",
-    )(at, x[0], x[1], g[0], g[1], codes, router, gate, up, down)
+    )(*operands)
+    return out[:2], out[2], out[3:]
+
+
+def expert_grad_kernel(act_ref, dgate_ref, dup_ref, x_ref, g_ref, *outs):
+    half, _, _, unit = outs[0].shape
+    for i, (rows, ref) in enumerate(((x_ref, dgate_ref), (x_ref, dup_ref), (g_ref, act_ref))):
+        grad = dot(rows[...], ref[0], 0, 0).astype(BF)
+        for j in range(2 * half):
+            outs[j // half][j % half, i] = grad[:, j * unit : (j + 1) * unit]
+
+
+def expert_grads(kept, x, g, parts, expert):
+    _, rows, hidden = kept[0].shape
+    width = x.shape[1]
+    unit = hidden // parts
+    tile = 512 if width % 512 == 0 else width
+    half = parts // 2
+    return list(pl.pallas_call(
+        expert_grad_kernel,
+        grid=(width // tile,),
+        out_shape=[jax.ShapeDtypeStruct((half, 3, width, unit), BF)] * 2,
+        in_specs=[pl.BlockSpec((1, rows, hidden), lambda i: (expert, 0, 0))] * 3
+        + [pl.BlockSpec((rows, tile), lambda i: (0, i))] * 2,
+        out_specs=[pl.BlockSpec((half, 3, tile, unit), lambda i: (0, 0, i, 0))] * 2,
+        compiler_params=pltpu.CompilerParams(vmem_limit_bytes=56 * MIB),
+        cost_estimate=pl.CostEstimate(
+            flops=6 * rows * width * hidden,
+            bytes_accessed=12 * width * hidden,
+            transcendentals=0,
+        ),
+        name="expert_grads",
+    )(*kept, x, g))
 
 
 def tree_moves():
     rows, cols = lax.axis_size("row"), lax.axis_size("col")
-    both = ("row", "col")
     if rows == 2 and cols == 2:
         swap = [(0, 1), (1, 0)]
-        cross = [(0, 3), (3, 0), (1, 2), (2, 1)]
         me = lax.axis_index("row") * 2 + lax.axis_index("col")
-        shards = [me, me ^ 1, me ^ 2, me ^ 3]
 
         def gather(x):
             across = lax.ppermute(x, "row", swap)
             beside = lax.ppermute(x, "col", swap)
-            return [x, beside, across, lax.ppermute(across, "col", swap)]
-
-        def exchange(blocks):
-            return [
-                blocks[0],
-                lax.ppermute(blocks[1], "col", swap),
-                lax.ppermute(blocks[2], "row", swap),
-                lax.ppermute(blocks[3], both, cross),
-            ]
-
-        def reduce(blocks):
-            far = blocks[2].astype(F32) + lax.ppermute(blocks[3], "col", swap).astype(F32)
-            far = lax.ppermute(far.astype(BF), "row", swap).astype(F32)
-            near = blocks[0].astype(F32) + lax.ppermute(blocks[1], "col", swap).astype(F32)
-            return near + far
-
-        return shards, gather, exchange, reduce
+            return [x, across, beside, lax.ppermute(across, "col", swap)]
+
+        def reduce(mine, other):
+            came = lax.ppermute(other, "col", swap)
+            far = (mine[1].astype(F32) + came[1].astype(F32)).astype(BF)
+            near = mine[0].astype(F32) + came[0].astype(F32)
+            return near, lax.ppermute(far, "row", swap)
+
+        return [me, me ^ 2, me ^ 1, me ^ 3], gather, reduce
 
     count = rows * cols
+    both = ("row", "col")
 
     def gather(x):
         whole = lax.all_gather(x, both, axis=0)
         return [whole[i] for i in range(count)]
 
-    def exchange(blocks):
-        whole = lax.all_to_all(jnp.stack(blocks), both, 0, 0)
-        return [whole[i] for i in range(count)]
-
-    def reduce(blocks):
-        return lax.psum_scatter(jnp.stack(blocks), both, scatter_dimension=0).astype(F32)
-
-    return [jnp.int32(i) for i in range(count)], gather, exchange, reduce
+    def reduce(mine, other):
+        blocks = jnp.concatenate([mine, other], axis=0)
+        total = lax.psum_scatter(blocks, both, scatter_dimension=0)
+        return total.astype(F32), jnp.zeros_like(total)
+
+    return [jnp.int32(i) for i in range(count)], gather, reduce
+
+
+def half_orders(count):
+    ys = count // 4
+    near = [y for y in range(ys)] + [ys + y for y in reversed(range(ys))]
+    return [near, [partner_of(i, count) for i in near]]
+
+
+def partner_of(index, count):
+    ys = count // 4
+    return (3 - index // ys) * ys + index % ys
 
 
 def ring_order(count):
-    depth = 4 if count % 4 == 0 else 1
-    ys = count // depth
+    ys = count // 4
     order = []
     for y in range(ys):
-        zs = range(depth) if y % 2 == 0 else reversed(range(depth))
+        zs = range(4) if y % 2 == 0 else reversed(range(4))
         order += [z * ys + y for z in zs]
     return order
 
 
-def ring_steps(order):
+def ring_move(x, order, by):
     n = len(order)
-    onward = [(order[i], order[(i + 1) % n]) for i in range(n)]
-    return onward, [(b, a) for a, b in onward]
-
-
-def ring_gather(a, b, order):
-    onward, backward = ring_steps(order)
-    held = [(a, b)]
-    for _ in range(len(order) - 1):
-        a = lax.ppermute(a, "dp", onward)
-        b = lax.ppermute(b, "dp", backward)
-        held.append((a, b))
-    return held
-
-
-def ring_reduce(parts, order):
-    onward, backward = ring_steps(order)
-    a, b = parts[1]
-    for k in range(1, len(order)):
-        a = lax.ppermute(a, "dp", onward)
-        b = lax.ppermute(b, "dp", backward)
-        more = parts[(k + 1) % len(order)]
-        a = a.astype(F32) + more[0].astype(F32)
-        b = b.astype(F32) + more[1].astype(F32)
-        if k < len(order) - 1:
-            a, b = a.astype(BF), b.astype(BF)
-    return jnp.concatenate([a, b], axis=0)
+    return lax.ppermute(x, "dp", [(order[i], order[(i + by) % n]) for i in range(n)])
+
+
+class Ring:
+    def __init__(self, count, dp_index):
+        self.orders = half_orders(count)
+        self.steps = len(self.orders[0])
+        at = [[o.index(i) for o in self.orders if i in o][0] for i in range(count)]
+        self.place = jnp.array(at, jnp.int32)[dp_index]
+        self.four = self.steps == 4
+        if self.four:
+            self.places = [lax.rem(self.place + k, 4) for k in (0, 3, 1, 2)]
+        else:
+            self.places = [jnp.int32(k) for k in range(self.steps)]
+
+    def shift(self, x, by):
+        n = self.steps
+        return lax.ppermute(
+            x, "dp", [(o[i], o[(i + by) % n]) for o in self.orders for i in range(n)]
+        )
+
+    def gather(self, x):
+        if not self.four:
+            whole = lax.all_gather(x, "dp", axis=0, axis_index_groups=self.orders)
+            return [[whole[k]] for k in range(self.steps)]
+        half = x.shape[0] // 2
+        left, right = self.shift(x, 1), self.shift(x, -1)
+        a, b = right[:half], left[half:]
+        return [[x], [left], [right], [self.shift(a, -1), self.shift(b, 1)]]
+
+    def reduce_stages(self, parts):
+        if not self.four:
+            yield []
+            whole = jnp.stack([jnp.concatenate(p, axis=0) for p in parts])
+            yield lax.psum_scatter(
+                whole, "dp", scatter_dimension=0, axis_index_groups=self.orders
+            ).astype(F32)
+            return
+        (own,), (left,), (right,), (far_a, far_b) = parts
+        half = far_a.shape[0]
+        a, b = yield [self.shift(far_a, 1), self.shift(far_b, -1)]
+        right = jnp.concatenate(
+            [(right[:half].astype(F32) + a.astype(F32)).astype(BF), right[half:]], axis=0
+        )
+        left = jnp.concatenate(
+            [left[:half], (left[half:].astype(F32) + b.astype(F32)).astype(BF)], axis=0
+        )
+        yield own.astype(F32) + (
+            self.shift(right, 1).astype(F32) + self.shift(left, -1).astype(F32)
+        )
+
+    def reduce(self, parts):
+        stages = self.reduce_stages(parts)
+        return stages.send(next(stages))
+
+
+def sum_over_all(value):
+    sizes = [lax.axis_size(name) for name in ("dp", "row", "col")]
+    if sizes != [8, 2, 2]:
+        return lax.psum(value, ("dp", "row", "col"))
+    for name, size, bit in (("col", 2, 1), ("row", 2, 1), ("dp", 8, 1), ("dp", 8, 2), ("dp", 8, 4)):
+        value = value + lax.ppermute(value, name, [(i, i ^ bit) for i in range(size)])
+    return value
+
+
+def write_kernel(spans, sizes, place_ref, *refs):
+    pieces, outs = refs[: sum(sizes)], refs[sum(sizes) :]
+    at = 0
+    for k, size in enumerate(sizes):
+        for i in range(size):
+            rows = pieces[at].shape[0]
+            start = pl.multiple_of(place_ref[k] * (rows * size) + i * rows, 16)
+            for (a, b), out in zip(spans, outs):
+                out[pl.ds(start, rows), :] = pieces[at][:, a:b].astype(F32)
+            at += 1
+
+
+def sum_over_dp(part, spans, ring, pairs):
+    rows, width = part.shape
+    chunk = rows // ring.steps
+
+    def cut(place, at, size):
+        return lax.dynamic_slice(part, (place * chunk + at, 0), (size, width))
+
+    parts = [[cut(place, 0, chunk)] for place in ring.places]
+    if ring.four:
+        half = chunk // 2
+        parts[3] = [cut(ring.places[3], 0, half), cut(ring.places[3], half, half)]
+    stages = ring.reduce_stages(parts)
+    total = stages.send((yield next(stages)))
+    total = (yield [total])[0].astype(BF)
+    came = (yield [lax.ppermute(total, "dp", pairs)])[0]
+    total = (total.astype(F32) + came.astype(F32)).astype(BF)
+    pieces = ring.gather(total)
+    pieces[0] = yield pieces[0]
+    sizes = [len(p) for p in pieces]
+    yield pl.pallas_call(
+        functools.partial(write_kernel, spans, sizes),
+        out_shape=[jax.ShapeDtypeStruct((rows, b - a), F32) for a, b in spans],
+        in_specs=[SMEM] + [VMEM] * sum(sizes),
+        out_specs=[VMEM] * len(spans),
+        compiler_params=pltpu.CompilerParams(vmem_limit_bytes=24 * MIB),
+        name="write_grads",
+    )(jnp.stack(ring.places).astype(jnp.int32), *[p for pair in pieces for p in pair])
 
 
 def rms_scale(values):
@@ -411,10 +601,11 @@
 ):
     local_rows, width = tokens.shape
     half = local_rows // 2
-    ring = lax.axis_size("dp")
-    order = ring_order(ring)
-    places = [order.index(i) for i in range(ring)]
-    shards, tree_gather, tree_exchange, tree_reduce = tree_moves()
+    dp_size = lax.axis_size("dp")
+    dp_index = lax.axis_index("dp")
+    pairs = [(i, partner_of(i, dp_size)) for i in range(dp_size)]
+    ring = Ring(dp_size, dp_index)
+    shards, tree_gather, tree_reduce = tree_moves()
     count = len(shards)
     shard_ids = jnp.stack(shards).astype(jnp.int32)
     kv = key_weight.shape[1] // HD
@@ -422,28 +613,31 @@
     q_width = query_weight.shape[1]
     k_width = key_weight.shape[1]
     experts_local = gate_weight.shape[0]
-    experts = experts_local * ring
+    unit = gate_weight.shape[2]
+    experts = experts_local * dp_size
     capacity = 5 * local_rows * TOPK // (4 * experts)
     seg = local_rows * count // 20
-    dp_index = lax.axis_index("dp")
-    place = jnp.array(places, jnp.int32)[dp_index]
 
     token_values = tokens.astype(F32)
     scale_attn = rms_scale(token_values)
     normed = (token_values * scale_attn * attn_gain).astype(BF)
-    tree_normed = tree_gather(normed)
     step = math.gcd(seg, local_rows)
-    labels = jnp.stack([segment_ids[::step], parent_ids[::step]]).astype(jnp.int32)
-    tree_labels = lax.all_gather(labels, ("row", "col"), axis=1, tiled=True)[:, :: seg // step]
-    spot = jnp.arange(20, dtype=jnp.int32)
+    each = local_rows // step
+    labels = jnp.stack([segment_ids[::step], parent_ids[::step]]).astype(BF)
+    normed_packet = jnp.concatenate(
+        [normed, jnp.pad(labels, ((0, 14), (0, width - each)))], axis=0
+    )
+    tree_normed = tree_gather(normed_packet)
+    labels = jnp.concatenate([v[local_rows : local_rows + 2, :each] for v in tree_normed], axis=1)
+    spots = jnp.concatenate([s * each + jnp.arange(each, dtype=jnp.int32) for s in shards])
+    spots = spots.astype(jnp.int32)
+    block_spot = spots * step // seg
+    is_parent = (labels[0][None, :] == labels[1][:, None]) & (labels[1][:, None] > 0)
+    parent_spot = jnp.max(jnp.where(is_parent, block_spot[None, :], 0), axis=1)
+    natural = jnp.arange(20, dtype=jnp.int32) * (seg // step)
     parent_block = jnp.sum(
-        jnp.where(
-            (tree_labels[0][None, :] == tree_labels[1][:, None]) & (tree_labels[1][:, None] > 0),
-            spot[None, :],
-            0,
-        ),
-        axis=1,
-    )
+        jnp.where(spots[None, :] == natural[:, None], parent_spot[None, :], 0), axis=1
+    ).astype(jnp.int32)
 
     flat_expert = expert_ids.reshape(-1)
     flat_rank = slot_rank.reshape(-1)
@@ -456,62 +650,89 @@
     code = jnp.sum(
         jnp.where(expert_ids.T[:, None, :] == columns[None, :, None], marks[:, None, :], 0.0), axis=0
     )
-    codes = lax.all_gather(code, "dp", axis=0)
-
-    grads = ring_gather(output_grad[:half], output_grad[half:], order)
-
+    extra = -(-experts // 16) * 16
+    codes = [
+        jnp.pad(code[:, at : at + half].astype(BF), ((0, extra - experts), (0, width - half)))
+        for at in (0, half)
+    ]
+    all_output_grad = lax.all_gather(output_grad, "dp", axis=0, tiled=True)
+
+    raw = [
+        jnp.stack([gate_weight[n], up_weight[n], down_weight[n].T]) for n in range(experts_local)
+    ]
+
+    def blocks_of(value):
+        blocks = tree_gather(value)
+        return blocks if unit % 128 == 0 else [jnp.concatenate(blocks, axis=2)]
+
+    weights = [blocks_of(raw[0])]
     qkv_weight = jnp.concatenate([query_weight, key_weight, value_weight], axis=1)
     qkv_blocks = [
         jnp.dot(block, qkv_weight, preferred_element_type=F32).astype(BF) for block in tree_normed
     ]
-    out_blocks = tree_gather(after(out_weight, tree_normed[2]))
     qkv, heads = attend_forward(shard_ids, parent_block, qkv_blocks, kv, per_group, seg)
-    head_blocks = tree_exchange(
-        [heads[j * local_rows : (j + 1) * local_rows] for j in range(count)]
-    )
-    gate_blocks = tree_gather(after(gate_weight, out_blocks[2]))
-    up_blocks = tree_gather(after(up_weight, out_blocks[2]))
-    down_blocks = tree_gather(after(down_weight, out_blocks[2]))
-    full_gate = jnp.concatenate(gate_blocks, axis=2)
-    full_up = jnp.concatenate(up_blocks, axis=2)
-    full_down = jnp.concatenate(down_blocks, axis=1)
-
-    hidden = token_values + jnp.dot(
-        jnp.concatenate(head_blocks, axis=1),
-        jnp.concatenate(out_blocks, axis=0),
-        preferred_element_type=F32,
-    )
+    heads, weights[0][-1 if count != 4 else 1] = tie(heads, weights[0][-1 if count != 4 else 1])
+    def by_shard(rows, weight):
+        result = jnp.dot(rows, weight, preferred_element_type=F32).astype(BF)
+        return result.reshape(-1, local_rows, width)
+
+    middle = (count + 1) // 2 * local_rows
+    attn_near, attn_far = tree_reduce(
+        by_shard(heads[:middle], out_weight), by_shard(heads[middle:], out_weight)
+    )
+    attn_far, *later = tie(attn_far, *raw[1:])
+    weights += [blocks_of(v) for v in later]
+    hidden = token_values + attn_near + attn_far.astype(F32)
     scale_mlp = rms_scale(hidden)
     mlp_in = (hidden * scale_mlp * mlp_gain).astype(BF)
 
-    rows_held = ring_gather(mlp_in[:half], mlp_in[half:], order)
-    mixes, backs, dots, acts, dgates, dups = [], [], [], [], [], []
-    order_array = jnp.array(order, jnp.int32)
-    for k in range(ring):
-        at = jnp.stack(
-            [
-                dp_index * experts_local,
-                order_array[(place - k) % ring],
-                order_array[(place + k) % ring],
-            ]
-        ).astype(jnp.int32)
-        mix_a, mix_b, back_a, back_b, pair_dot, act, dgate, dup = expert_step(
-            at, rows_held[k], grads[k], codes, router_weight, full_gate, full_up, full_down
+    order = ring_order(dp_size)
+    all_places = jnp.array([order.index(i) for i in range(dp_size)], jnp.int32)
+    place = all_places[dp_index]
+    walk = jnp.array(order, jnp.int32)
+    steps = jnp.arange(dp_size, dtype=jnp.int32)
+    at = jnp.stack(
+        [
+            jnp.full_like(steps, dp_index * experts_local),
+            walk[(place - steps) % dp_size],
+            walk[(place + steps) % dp_size],
+        ],
+        axis=1,
+    ).astype(jnp.int32)
+    x = [
+        jnp.concatenate([mlp_in[start : start + half], c], axis=0)
+        for start, c in zip((0, half), codes)
+    ]
+    kept = None
+    backs, dots, came = [], [], []
+    for k in range(dp_size):
+        if k > 0:
+            x = [ring_move(x[0], order, 1), ring_move(x[1], order, -1)]
+        if k == 1:
+            *x, all_output_grad = tie(*x, all_output_grad)
+        if k == 2:
+            *x, dots[0] = tie(*x, dots[0])
+        if k > 2:
+            *x, a, b, dots[k - 2] = tie(*x, *came[k - 2], dots[k - 2])
+            came[k - 2] = (a, b)
+        back, pair_dot, kept = expert_step(
+            k, dp_size, at[k], x, all_output_grad, router_weight, weights, kept
         )
-        mixes.append((mix_a, mix_b))
-        backs.append((back_a, back_b))
+        backs.append(back)
         dots.append(pair_dot)
-        acts.append(act)
-        dgates.append(dgate)
-        dups.append(dup)
-    grad_rows = ring_reduce(backs, order)
-    mixes[1] = tuple(after(m, grad_rows) for m in mixes[1])
-    output = (hidden + ring_reduce(mixes, order)).astype(BF)
-
-    steps = jnp.arange(ring, dtype=jnp.int32)
-    place_of = jnp.array(places, jnp.int32)
+        came.append(None)
+        if k > 0:
+            if k > 1:
+                back = [(n.astype(F32) + c.astype(F32)).astype(BF) for n, c in zip(back, came[k - 1])]
+            came[k] = (ring_move(back[0], order, 1), ring_move(back[1], order, -1))
+    mixes, all_rows, all_grads, *factors = kept
+    grad_rows = jnp.concatenate(
+        [n.astype(F32) + c.astype(F32) for n, c in zip(backs[0], came[-1])], axis=0
+    )
+    grad_rows, mixes = tie(grad_rows, mixes)
+    mixture = lax.psum_scatter(mixes, "dp", scatter_dimension=0, tiled=True)
+
     all_dots = jnp.stack(dots)
-    first_half = jnp.arange(local_rows) < half
 
     def pick(index):
         return jnp.sum(
@@ -519,7 +740,11 @@
             axis=1,
         )
 
-    send = jnp.where(first_half, pick((place - place_of) % ring), pick((place_of - place) % ring))
+    send = jnp.where(
+        jnp.arange(local_rows) < half,
+        pick((place - all_places) % dp_size),
+        pick((all_places - place) % dp_size),
+    )
     grad_gates = lax.all_to_all(send, "dp", 0, 0, tiled=True).reshape(experts, local_rows).T
 
     code_here = code.T
@@ -535,56 +760,78 @@
     grad_hidden = output_grad.astype(F32) + grad_hidden_norm
     grad_attn = grad_hidden.astype(BF)
 
+    grad_attn, *factors = tie(grad_attn, *factors)
     grad_blocks = tree_gather(grad_attn)
+    expert_parts = [expert_grads(factors, all_rows, all_grads, count, 0)]
+    grad_blocks[1], expert_parts[0][1] = tie(grad_blocks[1], expert_parts[0][1])
+    expert_sums = [tree_reduce(*expert_parts[0])]
     grad_head_blocks = [
         jnp.dot(block, out_weight.T, preferred_element_type=F32).astype(BF) for block in grad_blocks
     ]
-    dqkv = attend_backward(shard_ids, parent_block, qkv, grad_head_blocks, kv, per_group, seg)
-    normed_rows = jnp.concatenate(tree_normed, axis=0)
     out_part = jnp.dot(
         heads.T, jnp.concatenate(grad_blocks, axis=0), preferred_element_type=F32
     ).astype(BF)
+    dqkv = attend_backward(
+        shard_ids, parent_block, qkv, grad_head_blocks, kv, per_group, seg
+    )
+    out_stages = sum_over_dp(out_part, ((0, width),), ring, pairs)
+    out_came = next(out_stages)
+    near, across = expert_sums[0]
+    dqkv, across, *tied = tie(dqkv, across, *factors, *out_came)
+    expert_sums[0] = (near, across)
+    factors, out_came = tied[:3], tied[3:]
+    normed_rows = jnp.concatenate([v[:local_rows] for v in tree_normed], axis=0)
     qkv_part = jnp.dot(normed_rows.T, dqkv, preferred_element_type=F32).astype(BF)
-    summed = jnp.dot(dqkv, qkv_weight.T, preferred_element_type=F32).astype(BF)
-    grad_normed = tree_reduce(
-        [summed[j * local_rows : (j + 1) * local_rows] for j in range(count)]
-    )
+    spread = qkv_weight.T
+    spans = ((0, q_width), (q_width, q_width + k_width), (q_width + k_width, qkv_part.shape[1]))
+    qkv_stages = sum_over_dp(qkv_part, spans, ring, pairs)
+    qkv_came = next(qkv_stages)
+    normed_near, normed_far = tree_reduce(
+        by_shard(dqkv[:middle], spread), by_shard(dqkv[middle:], spread)
+    )
+    normed_far, mixture = tie(normed_far, mixture)
+    output = (hidden + mixture.astype(F32)).astype(BF)
+    grad_normed = normed_near + normed_far.astype(F32)
     grad_token_norm, attn_gain_part = norm_back(grad_normed, token_values, scale_attn, attn_gain)
     input_grad = grad_hidden + grad_token_norm
 
-    all_rows = jnp.concatenate([r for pair in rows_held for r in pair], axis=0)
-    all_grads = jnp.concatenate([r for pair in grads for r in pair], axis=0)
-
-    def expert_grad(parts, rows, pattern):
-        return jnp.einsum(
-            pattern, rows, jnp.concatenate(parts, axis=1), preferred_element_type=F32
-        ).astype(BF)
-
-    unit = gate_weight.shape[2]
-    gate_full = expert_grad(dgates, all_rows, "td,etf->edf")
-    up_full = expert_grad(dups, all_rows, "td,etf->edf")
-    down_full = expert_grad(acts, all_grads, "td,etf->efd")
-    gate_grad = tree_reduce([gate_full[:, :, j * unit : (j + 1) * unit] for j in range(count)])
-    up_grad = tree_reduce([up_full[:, :, j * unit : (j + 1) * unit] for j in range(count)])
-    down_grad = tree_reduce([down_full[:, j * unit : (j + 1) * unit] for j in range(count)])
-    out_grad = lax.psum(out_part, "dp").astype(F32)
-    qkv_grad = lax.psum(qkv_part, "dp").astype(F32)
-    attn_gain_grad, mlp_gain_grad, router_grad = lax.psum(
-        (attn_gain_part, mlp_gain_part, router_part), ("dp", "row", "col")
-    )
+    out_came = out_stages.send(out_came)
+    qkv_came = qkv_stages.send(qkv_came)
+    *out_came, total, factors[0] = tie(*out_came, *qkv_came, factors[0])
+    expert_parts += [
+        expert_grads(factors, all_rows, all_grads, count, n) for n in range(1, experts_local)
+    ]
+    out_came = out_stages.send(out_came)
+    (qkv_came,) = qkv_stages.send([total])
+    qkv_came, expert_parts[-1][1] = tie(qkv_came, expert_parts[-1][1])
+    expert_sums += [tree_reduce(*p) for p in expert_parts[1:]]
+    (out_grad,) = out_stages.send(out_stages.send(out_came))
+    (piece,) = qkv_stages.send([qkv_came])
+    near, across = expert_sums[-1]
+    piece, across = tie(piece, across)
+    expert_sums[-1] = (near, across)
+    query_grad, key_grad, value_grad = qkv_stages.send([piece])
+    expert_grad = [
+        jnp.stack([near[i] + across[i].astype(F32) for near, across in expert_sums])
+        for i in range(3)
+    ]
+    small = jnp.concatenate(
+        [router_part.T, mlp_gain_part.reshape(1, -1), attn_gain_part.reshape(1, -1)], axis=0
+    )
+    small = sum_over_all(small)
     return (
         output,
         input_grad,
-        attn_gain_grad,
-        qkv_grad[:, :q_width],
-        qkv_grad[:, q_width : q_width + k_width],
-        qkv_grad[:, q_width + k_width :],
+        small[experts + 1],
+        query_grad,
+        key_grad,
+        value_grad,
         out_grad,
-        mlp_gain_grad,
-        router_grad,
-        gate_grad,
-        up_grad,
-        down_grad,
+        small[experts],
+        small[:experts].T,
+        expert_grad[0],
+        expert_grad[1],
+        jnp.swapaxes(expert_grad[2], 1, 2),
     )
 
 

time: 910 us -> 639 us (0.70)
  Pallas kernels: 48.8 us -> 170 us
  other arithmetic: 177 us -> 56.6 us
  waiting for transfers between devices: 306 us -> 208 us
  blocking collectives: 87.9 us -> 0 us
  local copies, waits for them, and re-layouts: 94.9 us -> 39.7 us
  matrix products: 63.1 us -> 33.1 us
    pallas_call x1 -> x12, Pallas kernels: 12.8 us -> 134 us  [the longest x8 90.5 us: expert_step(): pl.pallas_call(functools.partial(expert_kernel, k * rows, blocks, buffers...]
    pallas_call x7 -> x0, other arithmetic: 87.6 us -> none  [expert_step(): pl.pallas_call(expert_kernel, out_shape=[half_shape] * 4 + [jax.ShapeDtyp...]
    ppermute x77 -> x63, waiting for transfers between devices: 219 us -> 163 us  [the longest x28 56.7 us: ring_move(): lax.ppermute(x, 'dp', [(order[i], order[(i + by) % n]) for i in range(n)])]
    unnamed x266 -> x199, local copies, waits for them, and re-layouts: 73.7 us -> 21.6 us
    all_gather x2 -> x0, blocking collectives: 47 us -> none  [the longest x1 41.9 us: shards_program(): codes = lax.all_gather(code, 'dp', axis=0)]
    psum x1 -> x0, blocking collectives: 40.9 us -> none  [shards_program(): lax.psum((attn_gain_part, mlp_gain_part, router_part), ('dp', 'row', 'col'))]
    psum x2 -> x0, waiting for transfers between devices: 35.9 us -> none  [the longest x1 35.9 us: shards_program(): lax.psum((attn_gain_part, mlp_gain_part, router_part), ('dp', 'row', 'col'))]
    dot_general x5 -> x4, matrix products: 40.7 us -> 7.07 us  [by_shard(): result = jnp.dot(rows, weight, preferred_element_type=F32).astype(BF)]
  transfers between devices with their start and end apart: 92 -> 74, of which waited for: 29 -> 25; matrix products, arithmetic and copies ran while one was open for 33% -> 18% of each run, Pallas kernels for 5% -> 27%
where the time goes in v2:
time: 639 us; the launch traced here: 631 us
  waiting for transfers between devices  208 us (33%)
  Pallas kernels  170 us (27%)
  starting transfers between devices  103 us (16%)
  other arithmetic  56.6 us (9%)
  local copies, waits for them, and re-layouts  39.7 us (6%)
  matrix products  33.1 us (5%)
  between operations  19.7 us (3%)
    pallas_call x8, Pallas kernels, expert_step(): pl.pallas_call(functools.partial(expert_kernel, k * rows, blocks, buffers...  90.5 us
    ppermute x28, waiting for transfers between devices, ring_move(): lax.ppermute(x, 'dp', [(order[i], order[(i + by) % n]) for i in range(n)])  56.7 us
    ppermute x16, waiting for transfers between devices, shift(): lax.ppermute(x, 'dp', [(o[i], o[(i + by) % n]) for o in self.orders for i...  43 us
    ppermute x4, waiting for transfers between devices, gather(): across = lax.ppermute(x, 'row', swap)  42.4 us
    ppermute x16, starting transfers between devices, shift(): lax.ppermute(x, 'dp', [(o[i], o[(i + by) % n]) for o in self.orders for i...  40.7 us
    ppermute x4, waiting for transfers between devices, reduce(): return (near, lax.ppermute(far, 'row', swap))  40.2 us
    pallas_call x2, Pallas kernels, expert_grads(): pl.pallas_call(expert_grad_kernel, grid=(width // tile,), out_shape=[jax....  39 us
    ppermute x28, starting transfers between devices, ring_move(): lax.ppermute(x, 'dp', [(order[i], order[(i + by) % n]) for i in range(n)])  33.9 us
  transfers between devices with their start and end apart: 74, of which 25 were waited for; matrix products, arithmetic and copies ran while one was open for 18% of the time, Pallas kernels for 27%

profile of v2, /device:TPU:0, one launch (start us, length us, event | category | flops | bytes accessed | tf_op | source)
XLA Modules:
  0.0 631.3 jit_solution(11479807066759713617)
XLA Ops:
  21.9 17.9 %collective-permute-done = bf16[336,1536]{1,0:T(8,128)(2,1)} collective-permute-done((bf16[336,1536]{1,0:T(8,128)(2,1)}, bf16[336,1536]{1,0:T(8,128)(2,1)}, u32[]{:S(2)}, u32[]{:S(2)}) %collective-permute-start) | collective-permute-done | bytes 1032224 | tf_op jit(solution)/shard_map/ppermute | solution.py:429
  48.7 13.6 %attend_forward.1 = (bf16[1280,640]{1,0:T(8,128)(2,1)S(1)}, bf16[1280,384]{1,0:T(8,128)(2,1)S(1)}) custom-call(s32[4]{0:T(128)S(1)} %pad_add_fusion.1.shard_ref, s32[20]{0:T(128)S(1)} %select_reduce_fusion.3.parent_ref, bf16[336,640]{1,0:T(8,128)(2,1)S(1)} %convolution_convert_fusion.7.refs_0_, bf16[336,640]{1,0:T(8,128)(2,1)S(1)} %convolution_convert_fusion.6.refs_1_, ...), custom_call_target="tpu_custom_call" | custom-call | flops 6039797760 | bytes 3276800 | tf_op jit(solution)/shard_map/attend_forward/pallas_call | solution.py:150
  92.9 20.1 %collective-permute-done.5 = bf16[320,1536]{1,0:T(8,128)(2,1)S(1)} collective-permute-done((bf16[320,1536]{1,0:T(8,128)(2,1)S(1)}, bf16[320,1536]{1,0:T(8,128)(2,1)S(1)}, u32[]{:S(2)}, u32[]{:S(2)}) %collective-permute-start.5) | collective-permute-done | bytes 983072 | tf_op jit(solution)/shard_map/ppermute | solution.py:437
  117.9 22.4 %collective-permute-done.8.refs_5_ = bf16[3,1536,128]{2,1,0:T(8,128)(2,1)} collective-permute-done((bf16[3,1536,128]{2,1,0:T(8,128)(2,1)S(1)}, bf16[3,1536,128]{2,1,0:T(8,128)(2,1)}, u32[]{:S(2)}, u32[]{:S(2)}) %collective-permute-start.8) | collective-permute-done | bytes 1179680 | tf_op jit(solution)/shard_map/ppermute | solution.py:429
  144.2 10.9 %collective-permute-done.11.xa_ref = bf16[176,1536]{1,0:T(8,128)(2,1)S(1)} collective-permute-done((bf16[176,1536]{1,0:T(8,128)(2,1)S(1)}, bf16[176,1536]{1,0:T(8,128)(2,1)S(1)}, u32[]{:S(2)}, u32[]{:S(2)}) %collective-permute-start.11) | collective-permute-done | bytes 540704 | tf_op jit(solution)/shard_map/ppermute | solution.py:478
  159.9 9.3 %collective-permute-done.12.xb_ref = bf16[176,1536]{1,0:T(8,128)(2,1)} collective-permute-done((bf16[176,1536]{1,0:T(8,128)(2,1)S(1)}, bf16[176,1536]{1,0:T(8,128)(2,1)}, u32[]{:S(2)}, u32[]{:S(2)}) %collective-permute-start.12) | collective-permute-done | bytes 540704 | tf_op jit(solution)/shard_map/ppermute | solution.py:478
  175.3 11.2 %expert_step.8 = (bf16[160,1536]{1,0:T(8,128)(2,1)S(1)}, bf16[160,1536]{1,0:T(8,128)(2,1)S(1)}, f32[2,320]{1,0:T(2,128)S(1)}, bf16[2560,1536]{1,0:T(8,128)(2,1)}...) custom-call(s32[3]{0:T(128)S(1)} %copy-done.20, ...), custom_call_target="tpu_custom_call" | custom-call | flops 6039797760 | bytes 14352384 | tf_op jit(solution)/shard_map/expert_step/pallas_call | solution.py:363
  188.1 11.7 %expert_step.9 = (bf16[160,1536]{1,0:T(8,128)(2,1)S(1)}, bf16[160,1536]{1,0:T(8,128)(2,1)S(1)}, f32[2,320]{1,0:T(2,128)S(1)}, bf16[2560,1536]{1,0:T(8,128)(2,1)}...) custom-call(s32[3]{0:T(128)S(1)} %copy-done.17, ...), custom_call_target="tpu_custom_call", output_to_operand_aliasing={{3}: (13, {}), {4}: (14, {}), {5}: (15, {}), {6}: (16, {}),... | custom-call | flops 6039797760 | bytes 14352384 | tf_op jit(solution)/shard_map/expert_step/pallas_call | solution.py:363
  204.0 11.3 %expert_step.10 = (bf16[160,1536]{1,0:T(8,128)(2,1)S(1)}, bf16[160,1536]{1,0:T(8,128)(2,1)S(1)}, f32[2,320]{1,0:T(2,128)S(1)}, bf16[2560,1536]{1,0:T(8,128)(2,1)...) custom-call(s32[3]{0:T(128)S(1)} %copy-done.16, ...), custom_call_target="tpu_custom_call", output_to_operand_aliasing={{3}: (13, {}), {4}: (14, {}), {5}: (15, {}), {6}: (16, {}),... | custom-call | flops 6039797760 | bytes 14352384 | tf_op jit(solution)/shard_map/expert_step/pallas_call | solution.py:363
  217.7 9.6 %collective-permute-done.15.xa_ref = bf16[176,1536]{1,0:T(8,128)(2,1)S(1)} collective-permute-done((bf16[176,1536]{1,0:T(8,128)(2,1)S(1)}, bf16[176,1536]{1,0:T(8,128)(2,1)S(1)}, u32[]{:S(2)}, u32[]{:S(2)}) %collective-permute-start.15) | collective-permute-done | bytes 540704 | tf_op jit(solution)/shard_map/ppermute | solution.py:478
  229.5 11.3 %expert_step.11 = (bf16[160,1536]{1,0:T(8,128)(2,1)S(1)}, bf16[160,1536]{1,0:T(8,128)(2,1)S(1)}, f32[2,320]{1,0:T(2,128)S(1)}, bf16[2560,1536]{1,0:T(8,128)(2,1)...) custom-call(s32[3]{0:T(128)S(1)} %copy-done.15, ...), custom_call_target="tpu_custom_call", output_to_operand_aliasing={{3}: (13, {}), {4}: (14, {}), {5}: (15, {}), {6}: (16, {}),... | custom-call | flops 6039797760 | bytes 14352384 | tf_op jit(solution)/shard_map/expert_step/pallas_call | solution.py:363
  243.2 6.2 collective-permute-done.19.xa_ref
  251.7 11.2 %expert_step.12 = (bf16[160,1536]{1,0:T(8,128)(2,1)S(1)}, bf16[160,1536]{1,0:T(8,128)(2,1)S(1)}, f32[2,320]{1,0:T(2,128)S(1)}, bf16[2560,1536]{1,0:T(8,128)(2,1)...) custom-call(s32[3]{0:T(128)S(1)} %get-tuple-element.319.at_ref, ...), custom_call_target="tpu_custom_call", output_to_operand_aliasing={{3}: (13, {}), {4}: (14, {}), {5}: (15, {}), {6}: (16, {}),... | custom-call | flops 6039797760 | bytes 14352384 | tf_op jit(solution)/shard_map/expert_step/pallas_call | solution.py:363
  274.0 11.3 %expert_step.13 = (bf16[160,1536]{1,0:T(8,128)(2,1)S(1)}, bf16[160,1536]{1,0:T(8,128)(2,1)S(1)}, f32[2,320]{1,0:T(2,128)S(1)}, bf16[2560,1536]{1,0:T(8,128)(2,1)...) custom-call(s32[3]{0:T(128)S(1)} %get-tuple-element.318.at_ref, ...), custom_call_target="tpu_custom_call", output_to_operand_aliasing={{3}: (13, {}), {4}: (14, {}), {5}: (15, {}), {6}: (16, {}),... | custom-call | flops 6039797760 | bytes 14352384 | tf_op jit(solution)/shard_map/expert_step/pallas_call | solution.py:363
  295.8 11.2 %expert_step.14 = (bf16[160,1536]{1,0:T(8,128)(2,1)S(1)}, bf16[160,1536]{1,0:T(8,128)(2,1)S(1)}, f32[2,320]{1,0:T(2,128)S(1)}, bf16[2560,1536]{1,0:T(8,128)(2,1)...) custom-call(s32[3]{0:T(128)S(1)} %get-tuple-element.317.at_ref, ...), custom_call_target="tpu_custom_call", output_to_operand_aliasing={{3}: (13, {}), {4}: (14, {}), {5}: (15, {}), {6}: (16, {}),... | custom-call | flops 6039797760 | bytes 14352384 | tf_op jit(solution)/shard_map/expert_step/pallas_call | solution.py:363
  315.8 11.2 %expert_step.15 = (bf16[160,1536]{1,0:T(8,128)(2,1)S(1)}, bf16[160,1536]{1,0:T(8,128)(2,1)S(1)}, f32[2,320]{1,0:T(2,128)S(1)}, bf16[2560,1536]{1,0:T(8,128)(2,1)...) custom-call(s32[3]{0:T(128)S(1)} %get-tuple-element.316.at_ref, ...), custom_call_target="tpu_custom_call", output_to_operand_aliasing={{3}: (13, {}), {4}: (14, {}), {5}: (15, {}), {6}: (16, {}),... | custom-call | flops 6039797760 | bytes 14352384 | tf_op jit(solution)/shard_map/expert_step/pallas_call | solution.py:363
  358.4 19.5 %expert_grads.2 = (bf16[2,3,1536,128]{3,2,1,0:T(8,128)(2,1)}, bf16[2,3,1536,128]{3,2,1,0:T(8,128)(2,1)}) custom-call(bf16[2,2560,512]{2,1,0:T(8,128)(2,1)} %get-tuple-element.258.act_ref, bf16[2,2560,512]{2,1,0:T(8,128)(2,1)} %get-tuple-element.259.dgate_ref, bf16[2,2560,512]{2,1,0:T(8,128)(2,1)} %get-tuple-element.260.dup_ref, ...), custom_call_target="tpu_custom_call" | custom-call | flops 12079595520 | bytes 9437184 | tf_op jit(solution)/shard_map/expert_grads/pallas_call | solution.py:405
  400.7 22.4 %attend_backward.1 = bf16[1280,640]{1,0:T(8,128)(2,1)S(1)} custom-call(s32[4]{0:T(128)S(1)} %copy-done.19, s32[20]{0:T(128)S(1)} %copy-done.22, bf16[1280,640]{1,0:T(8,128)(2,1)S(1)} %copy-done.26, bf16[320,384]{1,0:T(8,128)(2,1)S(1)} %convolution_convert_fusion.11.refs_0_, bf16[320,384]{1,0:T(8,128)(2,1)S(1)} %convolution_convert_fusion.10.refs_1_, ...), custom_call_target="tpu_custom_call" | custom-call | flops 15099494400 | bytes 4915200 | tf_op jit(solution)/shard_map/attend_backward/pallas_call | solution.py:215
  456.9 13.2 %collective-permute-done.58 = bf16[384,640]{1,0:T(8,128)(2,1)S(1)} collective-permute-done((bf16[384,640]{1,0:T(8,128)(2,1)}, bf16[384,640]{1,0:T(8,128)(2,1)S(1)}, u32[]{:S(2)}, u32[]{:S(2)}) %collective-permute-start.58) | collective-permute-done | bytes 491552 | tf_op jit(solution)/shard_map/ppermute | solution.py:495
  474.8 19.5 %expert_grads.3 = (bf16[2,3,1536,128]{3,2,1,0:T(8,128)(2,1)}, bf16[2,3,1536,128]{3,2,1,0:T(8,128)(2,1)}) custom-call(bf16[2,2560,512]{2,1,0:T(8,128)(2,1)} %get-tuple-element.258.act_ref, bf16[2,2560,512]{2,1,0:T(8,128)(2,1)} %get-tuple-element.259.dgate_ref, bf16[2,2560,512]{2,1,0:T(8,128)(2,1)} %get-tuple-element.260.dup_ref, ...), custom_call_target="tpu_custom_call" | custom-call | flops 12079595520 | bytes 9437184 | tf_op jit(solution)/shard_map/expert_grads/pallas_call | solution.py:405
  502.0 11.1 %collective-permute-done.66 = bf16[96,1536]{1,0:T(8,128)(2,1)S(1)} collective-permute-done((bf16[96,1536]{1,0:T(8,128)(2,1)S(1)}, bf16[96,1536]{1,0:T(8,128)(2,1)S(1)}, u32[]{:S(2)}, u32[]{:S(2)}) %collective-permute-start.66) | collective-permute-done | bytes 294944 | tf_op jit(solution)/shard_map/ppermute | solution.py:569
  513.3 26.0 %collective-permute-start.68 = (bf16[96,1536]{1,0:T(8,128)(2,1)S(1)}, bf16[96,1536]{1,0:T(8,128)(2,1)S(1)}, u32[]{:S(2)}, u32[]{:S(2)}) collective-permute-start(bf16[96,1536]{1,0:T(8,128)(2,1)S(1)} %add_convert_fusion.16.refs_0_), channel_id=1, source_target_pairs={{0,8},{4,0},{12,4},{8,12},{24,16},{28,24},{20,28},{16,20},{1,9},{5... | collective-permute-start | bytes 884744 | tf_op jit(solution)/shard_map/ppermute | solution.py:495
  550.7 12.2 %collective-permute-done.69.refs_3_ = bf16[48,1536]{1,0:T(8,128)(2,1)S(1)} collective-permute-done((bf16[48,1536]{1,0:T(8,128)(2,1)S(1)}, bf16[48,1536]{1,0:T(8,128)(2,1)S(1)}, u32[]{:S(2)}, u32[]{:S(2)}) %collective-permute-start.69) | collective-permute-done | bytes 147488 | tf_op jit(solution)/shard_map/ppermute | solution.py:495
  573.5 15.2 %collective-permute-done.47 = bf16[320,1536]{1,0:T(8,128)(2,1)} collective-permute-done((bf16[320,1536]{1,0:T(8,128)(2,1)S(1)}, bf16[320,1536]{1,0:T(8,128)(2,1)}, u32[]{:S(2)}, u32[]{:S(2)}) %collective-permute-start.47) | collective-permute-done | bytes 983072 | tf_op jit(solution)/shard_map/ppermute | solution.py:437
  (480 shorter events, 272.0 us)
Async XLA Ops:
  7.2 161.9 %all-gather.2.cloned.1.call-start = ((), (), s32[]{:S(2)}) async-start(), calls=%async_computation.2 | async-start | bytes 8847360 | tf_op jit(solution)/shard_map/all_gather | solution.py:658
  13.0 26.9 %collective-permute-start = (bf16[336,1536]{1,0:T(8,128)(2,1)}, bf16[336,1536]{1,0:T(8,128)(2,1)}, u32[]{:S(2)}, u32[]{:S(2)}) collective-permute-start(bf16[336,1536]{1,0:T(8,128)(2,1)} %pad_maximum_fusion.5), channel_id=1, source_target_pairs={{0,2},{2,0},{1,3},{3,1},{4,6},{6,4},{5,7},{7,5},{8,10},{10,8},{9,1... | collective-permute-start | bytes 3096584 | tf_op jit(solution)/shard_map/ppermute | solution.py:429
  19.9 44.4 %collective-permute-start.3 = (bf16[3,1536,128]{2,1,0:T(8,128)(2,1)S(1)}, bf16[3,1536,128]{2,1,0:T(8,128)(2,1)}, u32[]{:S(2)}, u32[]{:S(2)}) collective-permute-start(bf16[3,1536,128]{2,1,0:T(8,128)(2,1)S(1)} %pad_maximum_fusion.3.refs_0_), channel_id=1, source_target_pairs={{0,2},{2,0},{1,3},{3,1},{4,6},{6,4},{5,7},{7,5},{8,10},{10,8},{9,1... | collective-permute-start | bytes 3538952 | tf_op jit(solution)/shard_map/ppermute | solution.py:429
  66.8 104.1 %collective-permute-start.6 = (bf16[3,1536,128]{2,1,0:T(8,128)(2,1)S(1)}, bf16[3,1536,128]{2,1,0:T(8,128)(2,1)}, u32[]{:S(2)}, u32[]{:S(2)}) collective-permute-start(bf16[3,1536,128]{2,1,0:T(8,128)(2,1)S(1)} %pad_maximum_fusion.3.refs_0_), channel_id=1, source_target_pairs={{0,1},{1,0},{2,3},{3,2},{4,5},{5,4},{6,7},{7,6},{8,9},{9,8},{10,11... | collective-permute-start | bytes 3538952 | tf_op jit(solution)/shard_map/ppermute | solution.py:430
  92.8 78.7 %collective-permute-start.7 = (bf16[3,1536,128]{2,1,0:T(8,128)(2,1)}, bf16[3,1536,128]{2,1,0:T(8,128)(2,1)}, u32[]{:S(2)}, u32[]{:S(2)}) collective-permute-start(bf16[3,1536,128]{2,1,0:T(8,128)(2,1)} %collective-permute-done.3.refs_1_), channel_id=1, source_target_pairs={{0,1},{1,0},{2,3},{3,2},{4,5},{5,4},{6,7},{7,6},{8,9},{9,8},{10,11... | collective-permute-start | bytes 3538952 | tf_op jit(solution)/shard_map/ppermute | solution.py:431
  113.0 27.3 %collective-permute-start.8 = (bf16[3,1536,128]{2,1,0:T(8,128)(2,1)S(1)}, bf16[3,1536,128]{2,1,0:T(8,128)(2,1)}, u32[]{:S(2)}, u32[]{:S(2)}) collective-permute-start(bf16[3,1536,128]{2,1,0:T(8,128)(2,1)S(1)} %pad_maximum_fusion.4.refs_4_), channel_id=1, source_target_pairs={{0,2},{2,0},{1,3},{3,1},{4,6},{6,4},{5,7},{7,5},{8,10},{10,8},{9,1... | collective-permute-start | bytes 3538952 | tf_op jit(solution)/shard_map/ppermute | solution.py:429
  114.7 56.9 %collective-permute-start.9 = (bf16[3,1536,128]{2,1,0:T(8,128)(2,1)S(1)}, bf16[3,1536,128]{2,1,0:T(8,128)(2,1)}, u32[]{:S(2)}, u32[]{:S(2)}) collective-permute-start(bf16[3,1536,128]{2,1,0:T(8,128)(2,1)S(1)} %pad_maximum_fusion.4.refs_4_), channel_id=1, source_target_pairs={{0,1},{1,0},{2,3},{3,2},{4,5},{5,4},{6,7},{7,6},{8,9},{9,8},{10,11... | collective-permute-start | bytes 3538952 | tf_op jit(solution)/shard_map/ppermute | solution.py:430
  140.3 31.3 %collective-permute-start.10 = (bf16[3,1536,128]{2,1,0:T(8,128)(2,1)}, bf16[3,1536,128]{2,1,0:T(8,128)(2,1)}, u32[]{:S(2)}, u32[]{:S(2)}) collective-permute-start(bf16[3,1536,128]{2,1,0:T(8,128)(2,1)} %collective-permute-done.8.refs_5_), channel_id=1, source_target_pairs={{0,1},{1,0},{2,3},{3,2},{4,5},{5,4},{6,7},{7,6},{8,9},{9,8},{10,11... | collective-permute-start | bytes 3538952 | tf_op jit(solution)/shard_map/ppermute | solution.py:431
  169.1 32.8 %collective-permute-start.13 = (bf16[176,1536]{1,0:T(8,128)(2,1)}, bf16[176,1536]{1,0:T(8,128)(2,1)S(1)}, u32[]{:S(2)}, u32[]{:S(2)}) collective-permute-start(bf16[176,1536]{1,0:T(8,128)(2,1)} %copy-done.7), channel_id=1, source_target_pairs={{0,8},{8,16},{16,24},{24,28},{28,20},{20,12},{12,4},{4,0},{1,9},{9... | collective-permute-start | bytes 1622024 | tf_op jit(solution)/shard_map/ppermute | solution.py:478
  170.9 31.1 %collective-permute-start.14 = (bf16[176,1536]{1,0:T(8,128)(2,1)}, bf16[176,1536]{1,0:T(8,128)(2,1)S(1)}, u32[]{:S(2)}, u32[]{:S(2)}) collective-permute-start(bf16[176,1536]{1,0:T(8,128)(2,1)} %collective-permute-done.12.xb_ref), channel_id=1, source_target_pairs={{0,4},{8,0},{16,8},{24,16},{28,24},{20,28},{12,20},{4,12},{1,5},{9... | collective-permute-start | bytes 1622024 | tf_op jit(solution)/shard_map/ppermute | solution.py:478
  334.4 254.3 %reduce-scatter.2.cloned.1.call-start = ((), (), s32[]{:S(2)}) async-start(), calls=%async_computation.3 | async-start | bytes 8847360 | tf_op jit(solution)/shard_map/reduce_scatter | solution.py:733
  358.4 29.2 %collective-permute-start.40 = (bf16[320,1536]{1,0:T(8,128)(2,1)}, bf16[320,1536]{1,0:T(8,128)(2,1)}, u32[]{:S(2)}, u32[]{:S(2)}) collective-permute-start(bf16[320,1536]{1,0:T(8,128)(2,1)} %get-tuple-element.240), channel_id=1, source_target_pairs={{0,1},{1,0},{2,3},{3,2},{4,5},{5,4},{6,7},{7,6},{8,9},{9,8},{10,11... | collective-permute-start | bytes 2949128 | tf_op jit(solution)/shard_map/ppermute | solution.py:430
  393.5 29.7 %collective-permute-start.44 = (bf16[48,1536]{1,0:T(8,128)(2,1)S(1)}, bf16[48,1536]{1,0:T(8,128)(2,1)S(1)}, u32[]{:S(2)}, u32[]{:S(2)}) collective-permute-start(bf16[48,1536]{1,0:T(8,128)(2,1)S(1)} %get-tuple-element.351), channel_id=1, source_target_pairs={{0,4},{4,12},{12,8},{8,0},{24,28},{28,20},{20,16},{16,24},{1,5},{5... | collective-permute-start | bytes 442376 | tf_op jit(solution)/shard_map/ppermute | solution.py:495
  395.6 27.6 %collective-permute-start.45 = (bf16[48,1536]{1,0:T(8,128)(2,1)S(1)}, bf16[48,1536]{1,0:T(8,128)(2,1)S(1)}, u32[]{:S(2)}, u32[]{:S(2)}) collective-permute-start(bf16[48,1536]{1,0:T(8,128)(2,1)S(1)} %get-tuple-element.350), channel_id=1, source_target_pairs={{0,8},{4,0},{12,4},{8,12},{24,16},{28,24},{20,28},{16,20},{1,9},{5... | collective-permute-start | bytes 442376 | tf_op jit(solution)/shard_map/ppermute | solution.py:495
  400.0 28.1 %collective-permute-start.43 = (bf16[3,1536,128]{2,1,0:T(8,128)(2,1)S(1)}, bf16[3,1536,128]{2,1,0:T(8,128)(2,1)S(1)}, u32[]{:S(2)}, u32[]{:S(2)}) collective-permute-start(bf16[3,1536,128]{2,1,0:T(8,128)(2,1)S(1)} %get-tuple-element.331), channel_id=1, source_target_pairs={{0,2},{2,0},{1,3},{3,1},{4,6},{6,4},{5,7},{7,5},{8,10},{10,8},{9,1... | collective-permute-start | bytes 3538952 | tf_op jit(solution)/shard_map/ppermute | solution.py:437
  494.3 44.9 %collective-permute-start.60 = (bf16[2,3,1536,128]{3,2,1,0:T(8,128)(2,1)}, bf16[2,3,1536,128]{3,2,1,0:T(8,128)(2,1)S(1)}, u32[]{:S(2)}, u32[]{:S(2)}) collective-permute-start(bf16[2,3,1536,128]{3,2,1,0:T(8,128)(2,1)} %get-tuple-element.264), channel_id=1, source_target_pairs={{0,1},{1,0},{2,3},{3,2},{4,5},{5,4},{6,7},{7,6},{8,9},{9,8},{10,11... | collective-permute-start | bytes 7077896 | tf_op jit(solution)/shard_map/ppermute | solution.py:434
  496.2 53.8 %collective-permute-start.46 = (bf16[2,320,1536]{2,1,0:T(8,128)(2,1)S(1)}, bf16[2,320,1536]{2,1,0:T(8,128)(2,1)S(1)}, u32[]{:S(2)}, u32[]{:S(2)}) collective-permute-start(bf16[2,320,1536]{2,1,0:T(8,128)(2,1)S(1)} %bitcast.162), channel_id=1, source_target_pairs={{0,1},{1,0},{2,3},{3,2},{4,5},{5,4},{6,7},{7,6},{8,9},{9,8},{10,11... | collective-permute-start | bytes 5898248 | tf_op jit(solution)/shard_map/ppermute | solution.py:434
  513.2 35.1 %collective-permute-start.67 = (bf16[96,1536]{1,0:T(8,128)(2,1)S(1)}, bf16[96,1536]{1,0:T(8,128)(2,1)S(1)}, u32[]{:S(2)}, u32[]{:S(2)}) collective-permute-start(bf16[96,1536]{1,0:T(8,128)(2,1)S(1)} %add_convert_fusion.16.refs_0_), channel_id=1, source_target_pairs={{0,4},{4,12},{12,8},{8,0},{24,28},{28,20},{20,16},{16,24},{1,5},{5... | collective-permute-start | bytes 884744 | tf_op jit(solution)/shard_map/ppermute | solution.py:495
  513.3 34.1 %collective-permute-start.68 = (bf16[96,1536]{1,0:T(8,128)(2,1)S(1)}, bf16[96,1536]{1,0:T(8,128)(2,1)S(1)}, u32[]{:S(2)}, u32[]{:S(2)}) collective-permute-start(bf16[96,1536]{1,0:T(8,128)(2,1)S(1)} %add_convert_fusion.16.refs_0_), channel_id=1, source_target_pairs={{0,8},{4,0},{12,4},{8,12},{24,16},{28,24},{20,28},{16,20},{1,9},{5... | collective-permute-start | bytes 884744 | tf_op jit(solution)/shard_map/ppermute | solution.py:495
  539.8 31.2 %collective-permute-start.61 = (bf16[3,1536,128]{2,1,0:T(8,128)(2,1)S(1)}, bf16[3,1536,128]{2,1,0:T(8,128)(2,1)S(1)}, u32[]{:S(2)}, u32[]{:S(2)}) collective-permute-start(bf16[3,1536,128]{2,1,0:T(8,128)(2,1)S(1)} %get-tuple-element.333), channel_id=1, source_target_pairs={{0,2},{2,0},{1,3},{3,1},{4,6},{6,4},{5,7},{7,5},{8,10},{10,8},{9,1... | collective-permute-start | bytes 3538952 | tf_op jit(solution)/shard_map/ppermute | solution.py:437
  541.5 28.0 %collective-permute-start.62 = (bf16[384,640]{1,0:T(8,128)(2,1)S(1)}, bf16[384,640]{1,0:T(8,128)(2,1)S(1)}, u32[]{:S(2)}, u32[]{:S(2)}) collective-permute-start(bf16[384,640]{1,0:T(8,128)(2,1)S(1)} %add_convert_fusion.3.refs_0_), channel_id=1, source_target_pairs={{0,4},{4,12},{12,8},{8,0},{24,28},{28,20},{20,16},{16,24},{1,5},{5... | collective-permute-start | bytes 1474568 | tf_op jit(solution)/shard_map/ppermute | solution.py:495
  562.9 25.8 %collective-permute-start.47 = (bf16[320,1536]{1,0:T(8,128)(2,1)S(1)}, bf16[320,1536]{1,0:T(8,128)(2,1)}, u32[]{:S(2)}, u32[]{:S(2)}) collective-permute-start(bf16[320,1536]{1,0:T(8,128)(2,1)S(1)} %fusion.35), channel_id=1, source_target_pairs={{0,2},{2,0},{1,3},{3,1},{4,6},{6,4},{5,7},{7,5},{8,10},{10,8},{9,1... | collective-permute-start | bytes 2949128 | tf_op jit(solution)/shard_map/ppermute | solution.py:437
  568.0 31.2 %collective-permute-start.64 = (bf16[192,640]{1,0:T(8,128)(2,1)}, bf16[192,640]{1,0:T(8,128)(2,1)S(1)}, u32[]{:S(2)}, u32[]{:S(2)}) collective-permute-start(bf16[192,640]{1,0:T(8,128)(2,1)} %slice.359), channel_id=1, source_target_pairs={{0,8},{4,0},{12,4},{8,12},{24,16},{28,24},{20,28},{16,20},{1,9},{5... | collective-permute-start | bytes 737288 | tf_op jit(solution)/shard_map/ppermute | solution.py:495
  570.2 29.0 %collective-permute-start.65 = (bf16[192,640]{1,0:T(8,128)(2,1)}, bf16[192,640]{1,0:T(8,128)(2,1)S(1)}, u32[]{:S(2)}, u32[]{:S(2)}) collective-permute-start(bf16[192,640]{1,0:T(8,128)(2,1)} %slice.360), channel_id=1, source_target_pairs={{0,4},{4,12},{12,8},{8,0},{24,28},{28,20},{20,16},{16,24},{1,5},{5... | collective-permute-start | bytes 737288 | tf_op jit(solution)/shard_map/ppermute | solution.py:495
  (143 other events, 1922.6 us)
Sparse Core Ops, SparseCore 0:
  10.2 121.0 all-gather.1
  352.3 182.4 reduce-scatter.1

commit v3 on v2

--- a/solution.py
+++ b/solution.py
@@ -117,8 +117,17 @@
 
 
 def attend_forward_kernel(kv, per_group, seg, blocks, shard_ref, parent_ref, *refs):
-    ins, (qkv_ref, out_ref, full_ref) = refs[:blocks], refs[blocks:]
+    ins, row_refs, refs = refs[:blocks], refs[blocks : 2 * blocks], refs[2 * blocks :]
+    qkv_ref, out_ref, rows_ref, full_ref, row_sem = refs
     local = out_ref.shape[0] // blocks
+    copies = [
+        pltpu.make_async_copy(
+            row_refs[j].at[pl.ds(0, local)], rows_ref.at[pl.ds(j * local, local)], row_sem.at[j]
+        )
+        for j in range(blocks)
+    ]
+    for copy in copies:
+        copy.start()
     scale = BF(1.0 / math.sqrt(HD))
     for j in range(blocks):
         at = pl.multiple_of(shard_ref[j] * local, 64)
@@ -139,9 +148,11 @@
     for j in range(blocks):
         at = pl.multiple_of(shard_ref[j] * local, 64)
         out_ref[j * local : (j + 1) * local, :] = full_ref[pl.ds(at, local), :]
-
-
-def attend_forward(shards, parent_block, qkv_blocks, kv, per_group, seg):
+    for copy in copies:
+        copy.wait()
+
+
+def attend_forward(shards, parent_block, qkv_blocks, row_blocks, kv, per_group, seg):
     blocks = len(qkv_blocks)
     wide = qkv_blocks[0].shape[1]
     rows = 20 * seg
@@ -149,16 +160,20 @@
     cells = rows * 12 * seg * kv * per_group
     return pl.pallas_call(
         functools.partial(attend_forward_kernel, kv, per_group, seg, blocks),
-        out_shape=[jax.ShapeDtypeStruct((rows, wide), BF), jax.ShapeDtypeStruct((rows, width), BF)],
-        in_specs=[SMEM, SMEM] + [VMEM] * blocks,
-        out_specs=[VMEM, VMEM],
-        scratch_shapes=[pltpu.VMEM((rows, width), BF)],
+        out_shape=[
+            jax.ShapeDtypeStruct((rows, wide), BF),
+            jax.ShapeDtypeStruct((rows, width), BF),
+            jax.ShapeDtypeStruct((rows, row_blocks[0].shape[1]), BF),
+        ],
+        in_specs=[SMEM, SMEM] + [VMEM] * blocks + [ANY] * blocks,
+        out_specs=[VMEM, VMEM, ANY],
+        scratch_shapes=[pltpu.VMEM((rows, width), BF), pltpu.SemaphoreType.DMA((blocks,))],
         compiler_params=pltpu.CompilerParams(vmem_limit_bytes=40 * MIB),
         cost_estimate=pl.CostEstimate(
             flops=16 * HD * cells, bytes_accessed=4 * rows * wide, transcendentals=cells
         ),
         name="attend_forward",
-    )(shards, parent_block, *qkv_blocks)
+    )(shards, parent_block, *qkv_blocks, *row_blocks)
 
 
 def attend_backward_kernel(kv, per_group, seg, blocks, shard_ref, parent_ref, qkv_ref, *refs):
@@ -231,24 +246,35 @@
     )(shards, parent_block, qkv, *grad_blocks)
 
 
-def expert_kernel(first, blocks, fresh, at_ref, xa_ref, xb_ref, grads_ref, router_ref, *refs):
+def expert_kernel(first, blocks, fresh, local, at_ref, xa_ref, xb_ref, packet_ref, router_ref, *refs):
     count = len(blocks)
     weight_refs, refs = refs[: sum(blocks)], refs[sum(blocks) :]
     if not fresh:
-        refs = refs[6:]
-    back_a_ref, back_b_ref, dot_ref, mix_ref, rows_ref, grad_rows_ref, *kept_refs = refs[:9]
-    weights, held, g_held, mix_held, weight_sem, held_sem, row_sem, g_sem, mix_sem = refs[9:]
+        refs = refs[5:]
+    back_a_ref, back_b_ref, mix_a_ref, mix_b_ref, dot_ref, rows_ref, grad_rows_ref = refs[:7]
+    kept_refs = refs[7:10]
+    weights, held, g_held, x_held, code_held, weight_sem, held_sem, row_sem, g_sem = refs[10:]
     half = back_a_ref.shape[0]
     rows = 2 * half
     experts = router_ref.shape[1]
-    spots = [pl.multiple_of(at_ref[1 + i] * rows + i * half, 16) for i in range(2)]
-    arrived = []
-    for i in range(2):
-        copy = pltpu.make_async_copy(
-            grads_ref.at[pl.ds(spots[i], half)], g_held.at[pl.ds(i * half, half)], g_sem.at[i]
+    extra = code_held.shape[1]
+    x_came, codes_came, arrived = [], [], []
+    for i, ref in enumerate((xa_ref, xb_ref)):
+        spot = i * (half + extra)
+        if not local:
+            spot = pl.multiple_of(at_ref[1 + i] * (rows + 2 * extra) + spot, 16)
+        span = pl.ds(i * half, half)
+        x_came.append(pltpu.make_async_copy(ref, x_held.at[span], g_sem.at[i]))
+        codes_came.append(
+            pltpu.make_async_copy(
+                packet_ref.at[pl.ds(spot + half, extra)], code_held.at[i], g_sem.at[2 + i]
+            )
         )
+        arrived.append(
+            pltpu.make_async_copy(packet_ref.at[pl.ds(spot, half)], g_held.at[span], g_sem.at[4 + i])
+        )
+    for copy in x_came + codes_came + arrived:
         copy.start()
-        arrived.append(copy)
     loads = []
     for i in (2, 0, 1):
         for n in range(count):
@@ -272,17 +298,15 @@
             if (m, k) == (n, i):
                 copy.wait()
 
-    stores = []
-    for i, ref in enumerate((xa_ref, xb_ref)):
-        stores.append(
-            pltpu.make_async_copy(
-                ref.at[pl.ds(0, half)], rows_ref.at[pl.ds(first + i * half, half)], row_sem.at[i]
-            )
-        )
-        stores[-1].start()
-    x = jnp.concatenate([xa_ref[0:half], xb_ref[0:half]], axis=0)
+    for copy in x_came:
+        copy.wait()
+    stores = [pltpu.make_async_copy(x_held, rows_ref.at[pl.ds(first, rows)], row_sem.at[0])]
+    stores[0].start()
+    x = x_held[...]
+    for copy in codes_came:
+        copy.wait()
     code = jnp.concatenate(
-        [ref[half : half + experts, 0:half].astype(F32).T for ref in (xa_ref, xb_ref)], axis=0
+        [code_held[i, 0:experts, 0:half].astype(F32).T for i in range(2)], axis=0
     )
     logits = dot(x, router_ref[...], 1, 0)
     logits = jnp.where(code > 0.5, logits, NEG)
@@ -293,7 +317,7 @@
     lane = lax.broadcasted_iota(jnp.int32, gates.shape, 1)
     for copy in arrived:
         copy.wait()
-    copy = pltpu.make_async_copy(g_held, grad_rows_ref.at[pl.ds(first, rows)], row_sem.at[2])
+    copy = pltpu.make_async_copy(g_held, grad_rows_ref.at[pl.ds(first, rows)], row_sem.at[1])
     copy.start()
     stores.append(copy)
     g = g_held[...]
@@ -329,13 +353,9 @@
         mix = m if mix is None else mix + m
         b = dot(dgate, weights[0][n], 1, 1) + dot(dup, weights[1][n], 1, 1)
         back = b if back is None else back + b
-    mix_held[...] = mix.astype(BF)
-    for i in range(2):
-        copy = pltpu.make_async_copy(
-            mix_held.at[pl.ds(i * half, half)], mix_ref.at[pl.ds(spots[i], half)], mix_sem.at[i]
-        )
-        copy.start()
-        stores.append(copy)
+    mix = mix.astype(BF)
+    mix_a_ref[...] = mix[:half]
+    mix_b_ref[...] = mix[half:]
     back = back.astype(BF)
     back_a_ref[...] = back[:half]
     back_b_ref[...] = back[half:]
@@ -343,39 +363,40 @@
         copy.wait()
 
 
-def expert_step(k, steps, at, x, grads, router, weights, buffers):
+def expert_step(k, steps, local, at, x, packets, router, weights, buffers):
     width = x[0].shape[1]
-    half = grads.shape[0] // steps // 2
+    extra = -(-router.shape[1] // 16) * 16
+    half = x[0].shape[0]
     rows = 2 * half
     count = len(weights)
     hidden = sum(w.shape[2] for w in weights[0])
     half_shape = jax.ShapeDtypeStruct((half, width), BF)
-    big_shapes = [jax.ShapeDtypeStruct((steps * rows, width), BF)] * 3
+    big_shapes = [jax.ShapeDtypeStruct((steps * rows, width), BF)] * 2
     big_shapes += [jax.ShapeDtypeStruct((count, steps * rows, hidden), BF)] * 3
-    operands = [at, *x, grads, router, *[b for w in weights for b in w]]
-    specs = [SMEM, VMEM, VMEM, ANY, VMEM] + [ANY] * (len(operands) - 5)
+    operands = [at, *x, packets, router, *[b for w in weights for b in w]]
+    specs = [SMEM, ANY, ANY, ANY, VMEM] + [ANY] * (len(operands) - 5)
     aliases = {}
     if buffers is not None:
-        aliases = {len(operands) + i: 3 + i for i in range(6)}
+        aliases = {len(operands) + i: 5 + i for i in range(5)}
         operands += buffers
-        specs += [ANY] * 6
+        specs += [ANY] * 5
     blocks = [len(w) for w in weights]
     out = pl.pallas_call(
-        functools.partial(expert_kernel, k * rows, blocks, buffers is None),
-        out_shape=[half_shape] * 2 + [jax.ShapeDtypeStruct((count, rows), F32)] + big_shapes,
+        functools.partial(expert_kernel, k * rows, blocks, buffers is None, local),
+        out_shape=[half_shape] * 4 + [jax.ShapeDtypeStruct((count, rows), F32)] + big_shapes,
         in_specs=specs,
-        out_specs=[VMEM] * 3 + [ANY] * 6,
+        out_specs=[VMEM] * 5 + [ANY] * 5,
         input_output_aliases=aliases,
         scratch_shapes=[
             [pltpu.VMEM((count, width, hidden), BF)] * 3,
             [pltpu.VMEM((count, rows, hidden), BF)] * 3,
             pltpu.VMEM((rows, width), BF),
             pltpu.VMEM((rows, width), BF),
+            pltpu.VMEM((2, extra, width), BF),
             pltpu.SemaphoreType.DMA((3 * sum(blocks),)),
             pltpu.SemaphoreType.DMA((count * 3,)),
-            pltpu.SemaphoreType.DMA((3,)),
             pltpu.SemaphoreType.DMA((2,)),
-            pltpu.SemaphoreType.DMA((2,)),
+            pltpu.SemaphoreType.DMA((6,)),
         ],
         compiler_params=pltpu.CompilerParams(vmem_limit_bytes=40 * MIB),
         cost_estimate=pl.CostEstimate(
@@ -385,7 +406,7 @@
         ),
         name="expert_step",
     )(*operands)
-    return out[:2], out[2], out[3:]
+    return out[:2], out[2:4], out[4], out[5:]
 
 
 def expert_grad_kernel(act_ref, dgate_ref, dup_ref, x_ref, g_ref, *outs):
@@ -419,38 +440,76 @@
     )(*kept, x, g))
 
 
+def finish_kernel(terms, *refs):
+    ins, outs = refs[: len(refs) - 3], refs[len(refs) - 3 :]
+    for n in range(len(ins) // terms):
+        refs = ins[n * terms : (n + 1) * terms]
+        for i in range(3):
+            total = refs[-1][i].astype(F32)
+            for ref in refs[:-1]:
+                total = total + ref[0, i].astype(F32)
+            outs[i][n] = total.T if i == 2 else total
+
+
+def finish_grads(sums):
+    count = len(sums)
+    _, width, unit = sums[0][1].shape
+    terms = len(sums[0][0]) + 1
+    first = pl.BlockSpec((1, 3, width, unit), lambda i: (0, 0, 0, 0))
+    specs = [first] * (terms - 1) + [pl.BlockSpec((3, width, unit), lambda i: (0, 0, 0))]
+    shapes = [(count, width, unit), (count, width, unit), (count, unit, width)]
+    return pl.pallas_call(
+        functools.partial(finish_kernel, terms),
+        grid=(1,),
+        out_shape=[jax.ShapeDtypeStruct(v, F32) for v in shapes],
+        in_specs=specs * count,
+        out_specs=[pl.BlockSpec(v, lambda i: (0, 0, 0)) for v in shapes],
+        compiler_params=pltpu.CompilerParams(vmem_limit_bytes=48 * MIB),
+        name="finish_grads",
+    )(*[v for near, across in sums for v in (*near, across)])
+
+
 def tree_moves():
     rows, cols = lax.axis_size("row"), lax.axis_size("col")
     if rows == 2 and cols == 2:
         swap = [(0, 1), (1, 0)]
         me = lax.axis_index("row") * 2 + lax.axis_index("col")
 
-        def gather(x):
-            across = lax.ppermute(x, "row", swap)
+        def gather(x, again=None, finish=True):
+            across = lax.ppermute(x if again is None else again, "row", swap)
             beside = lax.ppermute(x, "col", swap)
-            return [x, across, beside, lax.ppermute(across, "col", swap)]
-
-        def reduce(mine, other):
-            came = lax.ppermute(other, "col", swap)
+            blocks = [x, across, beside]
+            return finish_gather(blocks) if finish else blocks
+
+        def finish_gather(blocks):
+            return blocks + [lax.ppermute(blocks[1], "col", swap)]
+
+        def reduce_first(mine, other):
+            return [mine, lax.ppermute(other, "col", swap)]
+
+        def reduce_second(mine, came):
             far = (mine[1].astype(F32) + came[1].astype(F32)).astype(BF)
-            near = mine[0].astype(F32) + came[0].astype(F32)
-            return near, lax.ppermute(far, "row", swap)
-
-        return [me, me ^ 2, me ^ 1, me ^ 3], gather, reduce
+            return [mine, came], lax.ppermute(far, "row", swap)
+
+        reduce = (reduce_first, reduce_second)
+
+        return [me, me ^ 2, me ^ 1, me ^ 3], gather, finish_gather, reduce
 
     count = rows * cols
     both = ("row", "col")
 
-    def gather(x):
-        whole = lax.all_gather(x, both, axis=0)
+    def gather(x, again=None, finish=True):
+        whole = lax.all_gather(x if again is None else again, both, axis=0)
         return [whole[i] for i in range(count)]
 
-    def reduce(mine, other):
+    def reduce_second(mine, other):
         blocks = jnp.concatenate([mine, other], axis=0)
         total = lax.psum_scatter(blocks, both, scatter_dimension=0)
-        return total.astype(F32), jnp.zeros_like(total)
-
-    return [jnp.int32(i) for i in range(count)], gather, reduce
+        return [total[None]], jnp.zeros_like(total)
+
+    reduce = (lambda mine, other: [mine, other], reduce_second)
+
+    return [jnp.int32(i) for i in range(count)], gather, list, reduce
 
 
 def half_orders(count):
@@ -476,6 +535,24 @@
 def ring_move(x, order, by):
     n = len(order)
     return lax.ppermute(x, "dp", [(order[i], order[(i + by) % n]) for i in range(n)])
+
+
+def add_halves(came, own, last):
+    total = [c.astype(F32) + n.astype(F32) for c, n in zip(came, own)]
+    if last:
+        return [jnp.concatenate(total, axis=0)]
+    return list(tie(*[t.astype(BF) for t in total]))
+
+
+def walk_hops(parts, order):
+    n = len(order)
+    a, b = parts[1]
+    for k in range(1, n):
+        came = yield [ring_move(a, order, 1), ring_move(b, order, -1)]
+        total = add_halves(came, parts[(k + 1) % n], k == n - 1)
+        if k < n - 1:
+            a, b = total
+    yield total
 
 
 class Ring:
@@ -500,8 +577,16 @@
         if not self.four:
             whole = lax.all_gather(x, "dp", axis=0, axis_index_groups=self.orders)
             return [[whole[k]] for k in range(self.steps)]
+        return self.gather_second(x, self.gather_first(x))
+
+    def gather_first(self, x):
+        return [self.shift(x, 1), self.shift(x, -1)] if self.four else [x]
+
+    def gather_second(self, x, came):
+        if not self.four:
+            return self.gather(x)
         half = x.shape[0] // 2
-        left, right = self.shift(x, 1), self.shift(x, -1)
+        left, right = came
         a, b = right[:half], left[half:]
         return [[x], [left], [right], [self.shift(a, -1), self.shift(b, 1)]]
 
@@ -531,54 +616,72 @@
         return stages.send(next(stages))
 
 
-def sum_over_all(value):
+def small_sum(value, part):
     sizes = [lax.axis_size(name) for name in ("dp", "row", "col")]
     if sizes != [8, 2, 2]:
-        return lax.psum(value, ("dp", "row", "col"))
-    for name, size, bit in (("col", 2, 1), ("row", 2, 1), ("dp", 8, 1), ("dp", 8, 2), ("dp", 8, 4)):
+        return lax.psum(value, ("col", "row", "dp")[part])
+    hops = [[("col", 2, 1), ("dp", 8, 1)], [("row", 2, 1)], [("dp", 8, 2), ("dp", 8, 4)]]
+    for name, size, bit in hops[part]:
         value = value + lax.ppermute(value, name, [(i, i ^ bit) for i in range(size)])
     return value
 
 
-def write_kernel(spans, sizes, place_ref, *refs):
+def write_kernel(spans, sizes, turned, place_ref, *refs):
     pieces, outs = refs[: sum(sizes)], refs[sum(sizes) :]
     at = 0
     for k, size in enumerate(sizes):
-        for i in range(size):
-            rows = pieces[at].shape[0]
-            start = pl.multiple_of(place_ref[k] * (rows * size) + i * rows, 16)
-            for (a, b), out in zip(spans, outs):
-                out[pl.ds(start, rows), :] = pieces[at][:, a:b].astype(F32)
-            at += 1
-
-
-def sum_over_dp(part, spans, ring, pairs):
-    rows, width = part.shape
+        chunk = jnp.concatenate([ref[...] for ref in pieces[at : at + size]], axis=0).astype(F32)
+        rows = chunk.shape[0]
+        at += size
+        for n, ((a, b), out) in enumerate(zip(spans, outs)):
+            if n == turned:
+                start = pl.multiple_of(place_ref[k] * rows, 128)
+                out[:, pl.ds(start, rows)] = chunk[:, a:b].T
+            else:
+                start = pl.multiple_of(place_ref[k] * rows, 16)
+                out[pl.ds(start, rows), :] = chunk[:, a:b]
+
+
+def sum_over_dp(parts, spans, ring, pairs):
+    rows = parts[0].shape[0]
     chunk = rows // ring.steps
 
     def cut(place, at, size):
-        return lax.dynamic_slice(part, (place * chunk + at, 0), (size, width))
-
-    parts = [[cut(place, 0, chunk)] for place in ring.places]
+        return jnp.concatenate(
+            [lax.dynamic_slice(v, (place * chunk + at, 0), (size, v.shape[1])) for v in parts],
+            axis=1,
+        )
+
+    terms = [[cut(place, 0, chunk)] for place in ring.places]
     if ring.four:
         half = chunk // 2
-        parts[3] = [cut(ring.places[3], 0, half), cut(ring.places[3], half, half)]
-    stages = ring.reduce_stages(parts)
+        terms[3] = [cut(ring.places[3], 0, half), cut(ring.places[3], half, half)]
+    stages = ring.reduce_stages(terms)
     total = stages.send((yield next(stages)))
     total = (yield [total])[0].astype(BF)
     came = (yield [lax.ppermute(total, "dp", pairs)])[0]
     total = (total.astype(F32) + came.astype(F32)).astype(BF)
-    pieces = ring.gather(total)
-    pieces[0] = yield pieces[0]
+    pieces = ring.gather_second(total, (yield ring.gather_first(total)))
+    pieces[-1] = yield pieces[-1]
     sizes = [len(p) for p in pieces]
-    yield pl.pallas_call(
-        functools.partial(write_kernel, spans, sizes),
-        out_shape=[jax.ShapeDtypeStruct((rows, b - a), F32) for a, b in spans],
-        in_specs=[SMEM] + [VMEM] * sum(sizes),
-        out_specs=[VMEM] * len(spans),
-        compiler_params=pltpu.CompilerParams(vmem_limit_bytes=24 * MIB),
-        name="write_grads",
-    )(jnp.stack(ring.places).astype(jnp.int32), *[p for pair in pieces for p in pair])
+    turned = len(spans) - 1 if chunk % 128 == 0 else None
+    shapes = [
+        jax.ShapeDtypeStruct((b - a, rows) if n == turned else (rows, b - a), F32)
+        for n, (a, b) in enumerate(spans)
+    ]
+    sums = list(
+        pl.pallas_call(
+            functools.partial(write_kernel, spans, sizes, turned),
+            out_shape=shapes,
+            in_specs=[SMEM] + [VMEM] * sum(sizes),
+            out_specs=[VMEM] * len(spans),
+            compiler_params=pltpu.CompilerParams(vmem_limit_bytes=32 * MIB),
+            name="write_grads",
+        )(jnp.stack(ring.places).astype(jnp.int32), *[p for pair in pieces for p in pair])
+    )
+    if turned is None:
+        sums[-1] = sums[-1].T
+    yield sums
 
 
 def rms_scale(values):
@@ -605,7 +708,11 @@
     dp_index = lax.axis_index("dp")
     pairs = [(i, partner_of(i, dp_size)) for i in range(dp_size)]
     ring = Ring(dp_size, dp_index)
-    shards, tree_gather, tree_reduce = tree_moves()
+    shards, tree_gather, tree_finish, (reduce_first, reduce_second) = tree_moves()
+
+    def tree_reduce(mine, other):
+        return reduce_second(*reduce_first(mine, other))
+
     count = len(shards)
     shard_ids = jnp.stack(shards).astype(jnp.int32)
     kv = key_weight.shape[1] // HD
@@ -639,50 +746,53 @@
         jnp.where(spots[None, :] == natural[:, None], parent_spot[None, :], 0), axis=1
     ).astype(jnp.int32)
 
-    flat_expert = expert_ids.reshape(-1)
-    flat_rank = slot_rank.reshape(-1)
-    earlier = (flat_expert[None, :] == flat_expert[:, None]) & (
-        flat_rank[None, :] < flat_rank[:, None]
-    )
-    kept = (jnp.sum(earlier.astype(jnp.int32), axis=1) < capacity).reshape(local_rows, TOPK)
-    marks = 1.0 + kept.T.astype(F32)
     columns = jnp.arange(experts, dtype=jnp.int32)
-    code = jnp.sum(
-        jnp.where(expert_ids.T[:, None, :] == columns[None, :, None], marks[:, None, :], 0.0), axis=0
-    )
+    unranked = local_rows * TOPK
+    rank = jnp.min(
+        jnp.where(
+            expert_ids.T[:, None, :] == columns[None, :, None], slot_rank.T[:, None, :], unranked
+        ),
+        axis=0,
+    )
+    slot = jnp.sum((rank[:, :, None] < rank[:, None, :]).astype(jnp.int32), axis=1)
+    code = jnp.where(rank == unranked, 0.0, jnp.where(slot < capacity, 2.0, 1.0))
     extra = -(-experts // 16) * 16
-    codes = [
-        jnp.pad(code[:, at : at + half].astype(BF), ((0, extra - experts), (0, width - half)))
-        for at in (0, half)
-    ]
-    all_output_grad = lax.all_gather(output_grad, "dp", axis=0, tiled=True)
+    packet = []
+    for at in (0, half):
+        lanes = ((0, extra - experts), (0, width - half))
+        packet += [output_grad[at : at + half], jnp.pad(code[:, at : at + half].astype(BF), lanes)]
+    packet = jnp.concatenate(packet, axis=0)
+    packets = lax.all_gather(packet, "dp", axis=0, tiled=True)
+    tree_normed[1], packet = tie(tree_normed[1], packet)
 
     raw = [
         jnp.stack([gate_weight[n], up_weight[n], down_weight[n].T]) for n in range(experts_local)
     ]
 
-    def blocks_of(value):
-        blocks = tree_gather(value)
+    def joined(blocks):
         return blocks if unit % 128 == 0 else [jnp.concatenate(blocks, axis=2)]
 
-    weights = [blocks_of(raw[0])]
+    weights = [tree_gather(raw[0])]
     qkv_weight = jnp.concatenate([query_weight, key_weight, value_weight], axis=1)
     qkv_blocks = [
         jnp.dot(block, qkv_weight, preferred_element_type=F32).astype(BF) for block in tree_normed
     ]
-    qkv, heads = attend_forward(shard_ids, parent_block, qkv_blocks, kv, per_group, seg)
-    heads, weights[0][-1 if count != 4 else 1] = tie(heads, weights[0][-1 if count != 4 else 1])
+    qkv, heads, normed_rows = attend_forward(
+        shard_ids, parent_block, qkv_blocks, tree_normed, kv, per_group, seg
+    )
+    heads, weights[0][1] = tie(heads, weights[0][1])
     def by_shard(rows, weight):
         result = jnp.dot(rows, weight, preferred_element_type=F32).astype(BF)
         return result.reshape(-1, local_rows, width)
 
     middle = (count + 1) // 2 * local_rows
     attn_near, attn_far = tree_reduce(
-        by_shard(heads[:middle], out_weight), by_shard(heads[middle:], out_weight)
-    )
-    attn_far, *later = tie(attn_far, *raw[1:])
-    weights += [blocks_of(v) for v in later]
-    hidden = token_values + attn_near + attn_far.astype(F32)
+        *tie(by_shard(heads[:middle], out_weight), by_shard(heads[middle:], out_weight))
+    )
+    attn_far, *later = tie(attn_far, *raw[1:], *weights[0][2:])
+    weights[0][2:] = later[len(raw) - 1 :]
+    weights += [tree_gather(v, again, False) for v, again in zip(raw[1:], later)]
+    hidden = token_values + attn_far.astype(F32) + sum(v[0].astype(F32) for v in attn_near)
     scale_mlp = rms_scale(hidden)
     mlp_in = (hidden * scale_mlp * mlp_gain).astype(BF)
 
@@ -699,38 +809,61 @@
         ],
         axis=1,
     ).astype(jnp.int32)
-    x = [
-        jnp.concatenate([mlp_in[start : start + half], c], axis=0)
-        for start, c in zip((0, half), codes)
-    ]
+    x = [mlp_in[:half], mlp_in[half:]]
     kept = None
-    backs, dots, came = [], [], []
+    backs, mixes, dots, came = [], [], [], []
+    coming = [ring_move(x[0], order, 1), ring_move(x[1], order, -1)]
+    *coming, weights[-1][1] = tie(*coming, weights[-1][1])
+    weights[1:] = [tree_finish(blocks) for blocks in weights[1:]]
+    weights = [joined(blocks) for blocks in weights]
     for k in range(dp_size):
         if k > 0:
-            x = [ring_move(x[0], order, 1), ring_move(x[1], order, -1)]
-        if k == 1:
-            *x, all_output_grad = tie(*x, all_output_grad)
-        if k == 2:
-            *x, dots[0] = tie(*x, dots[0])
-        if k > 2:
-            *x, a, b, dots[k - 2] = tie(*x, *came[k - 2], dots[k - 2])
-            came[k - 2] = (a, b)
-        back, pair_dot, kept = expert_step(
-            k, dp_size, at[k], x, all_output_grad, router_weight, weights, kept
+            x = coming
+            if k > 1:
+                x = [ring_move(x[0], order, 1), ring_move(x[1], order, -1)]
+            if k > 1:
+                *x, dots[k - 2] = tie(*x, dots[k - 2])
+            if k > 2:
+                *x, came[k - 2][0], came[k - 2][1] = tie(*x, *came[k - 2])
+            coming = x
+        back, mix, pair_dot, kept = expert_step(
+            k,
+            dp_size,
+            k == 0,
+            at[k],
+            x,
+            packets if k > 0 else packet,
+            router_weight,
+            weights,
+            kept,
         )
         backs.append(back)
+        mixes.append(list(mix))
         dots.append(pair_dot)
         came.append(None)
         if k > 0:
             if k > 1:
-                back = [(n.astype(F32) + c.astype(F32)).astype(BF) for n, c in zip(back, came[k - 1])]
-            came[k] = (ring_move(back[0], order, 1), ring_move(back[1], order, -1))
-    mixes, all_rows, all_grads, *factors = kept
-    grad_rows = jnp.concatenate(
-        [n.astype(F32) + c.astype(F32) for n, c in zip(backs[0], came[-1])], axis=0
-    )
-    grad_rows, mixes = tie(grad_rows, mixes)
-    mixture = lax.psum_scatter(mixes, "dp", scatter_dimension=0, tiled=True)
+                *came[k - 1], dots[k] = tie(*came[k - 1], dots[k])
+                back = add_halves(came[k - 1], back, False)
+            if k == dp_size - 1:
+                *back, mixes[1][0], mixes[1][1] = tie(*back, *mixes[1])
+            came[k] = [ring_move(back[0], order, 1), ring_move(back[1], order, -1)]
+    all_rows, all_grads, *factors = kept
+    mlp_in, code, dots[-1] = tie(mlp_in, code, dots[-1])
+    (grad_rows,) = add_halves(came[-1], backs[0], True)
+    hops = walk_hops(mixes, order)
+    hop = next(hops)
+    left = dp_size - 1
+
+    def next_hop(*values):
+        nonlocal hop, left
+        if left == 0:
+            return values
+        *values, a, b = tie(*values, *hop)
+        hop = hops.send([a, b])
+        left -= 1
+        return values
+
 
     all_dots = jnp.stack(dots)
 
@@ -760,65 +893,70 @@
     grad_hidden = output_grad.astype(F32) + grad_hidden_norm
     grad_attn = grad_hidden.astype(BF)
 
-    grad_attn, *factors = tie(grad_attn, *factors)
+    grad_attn, *factors = next_hop(*tie(grad_attn, *factors))
     grad_blocks = tree_gather(grad_attn)
     expert_parts = [expert_grads(factors, all_rows, all_grads, count, 0)]
-    grad_blocks[1], expert_parts[0][1] = tie(grad_blocks[1], expert_parts[0][1])
+    grad_blocks[1], expert_parts[0][1] = next_hop(*tie(grad_blocks[1], expert_parts[0][1]))
     expert_sums = [tree_reduce(*expert_parts[0])]
     grad_head_blocks = [
         jnp.dot(block, out_weight.T, preferred_element_type=F32).astype(BF) for block in grad_blocks
     ]
-    out_part = jnp.dot(
-        heads.T, jnp.concatenate(grad_blocks, axis=0), preferred_element_type=F32
-    ).astype(BF)
+    (grad_head_blocks[-1],) = next_hop(grad_head_blocks[-1])
     dqkv = attend_backward(
         shard_ids, parent_block, qkv, grad_head_blocks, kv, per_group, seg
     )
-    out_stages = sum_over_dp(out_part, ((0, width),), ring, pairs)
-    out_came = next(out_stages)
     near, across = expert_sums[0]
-    dqkv, across, *tied = tie(dqkv, across, *factors, *out_came)
+    dqkv, across, *factors = next_hop(*tie(dqkv, across, *factors))
     expert_sums[0] = (near, across)
-    factors, out_came = tied[:3], tied[3:]
-    normed_rows = jnp.concatenate([v[:local_rows] for v in tree_normed], axis=0)
     qkv_part = jnp.dot(normed_rows.T, dqkv, preferred_element_type=F32).astype(BF)
+    out_rows = jnp.concatenate(grad_blocks, axis=0)
+    out_part = jnp.dot(out_rows.T, heads, preferred_element_type=F32).astype(BF)
+    spans = (
+        (0, q_width),
+        (q_width, q_width + k_width),
+        (q_width + k_width, q_width + 2 * k_width),
+        (q_width + 2 * k_width, 2 * q_width + 2 * k_width),
+    )
+    stages = sum_over_dp([qkv_part, out_part], spans, ring, pairs)
+    came = next(stages)
     spread = qkv_weight.T
-    spans = ((0, q_width), (q_width, q_width + k_width), (q_width + k_width, qkv_part.shape[1]))
-    qkv_stages = sum_over_dp(qkv_part, spans, ring, pairs)
-    qkv_came = next(qkv_stages)
     normed_near, normed_far = tree_reduce(
         by_shard(dqkv[:middle], spread), by_shard(dqkv[middle:], spread)
     )
-    normed_far, mixture = tie(normed_far, mixture)
-    output = (hidden + mixture.astype(F32)).astype(BF)
-    grad_normed = normed_near + normed_far.astype(F32)
-    grad_token_norm, attn_gain_part = norm_back(grad_normed, token_values, scale_attn, attn_gain)
-    input_grad = grad_hidden + grad_token_norm
-
-    out_came = out_stages.send(out_came)
-    qkv_came = qkv_stages.send(qkv_came)
-    *out_came, total, factors[0] = tie(*out_came, *qkv_came, factors[0])
+
+    *came, factors[0] = next_hop(*tie(*came, factors[0]))
+    came = stages.send(came)
     expert_parts += [
         expert_grads(factors, all_rows, all_grads, count, n) for n in range(1, experts_local)
     ]
-    out_came = out_stages.send(out_came)
-    (qkv_came,) = qkv_stages.send([total])
-    qkv_came, expert_parts[-1][1] = tie(qkv_came, expert_parts[-1][1])
-    expert_sums += [tree_reduce(*p) for p in expert_parts[1:]]
-    (out_grad,) = out_stages.send(out_stages.send(out_came))
-    (piece,) = qkv_stages.send([qkv_came])
-    near, across = expert_sums[-1]
-    piece, across = tie(piece, across)
-    expert_sums[-1] = (near, across)
-    query_grad, key_grad, value_grad = qkv_stages.send([piece])
-    expert_grad = [
-        jnp.stack([near[i] + across[i].astype(F32) for near, across in expert_sums])
-        for i in range(3)
-    ]
+    *came, normed_far, expert_parts[-1][1] = next_hop(
+        *tie(*came, normed_far, expert_parts[-1][1])
+    )
+    came = stages.send(came)
+    grad_normed = normed_far.astype(F32) + sum(v[0].astype(F32) for v in normed_near)
+    grad_token_norm, attn_gain_part = norm_back(grad_normed, token_values, scale_attn, attn_gain)
+    input_grad = grad_hidden + grad_token_norm
     small = jnp.concatenate(
         [router_part.T, mlp_gain_part.reshape(1, -1), attn_gain_part.reshape(1, -1)], axis=0
     )
-    small = sum_over_all(small)
+    small = small_sum(small, 0)
+    expert_sums += [tree_reduce(*p) for p in expert_parts[1:]]
+    near, across = expert_sums[-1]
+    across, small, *came = next_hop(*tie(across, small, *came))
+    expert_sums[-1] = (near, across)
+    while left > 0:
+        next_hop()
+    output = (hidden + hop[0]).astype(BF)
+    came = stages.send(came)
+    small = small_sum(small, 1)
+    near, across = expert_sums[-1]
+    across, *came = tie(across, *came)
+    expert_sums[-1] = (near, across)
+    came = stages.send(came)
+    small, *came = tie(small, *came)
+    query_grad, key_grad, value_grad, out_grad = stages.send(came)
+    small = small_sum(small, 2)
+    expert_grad = finish_grads(expert_sums)
     return (
         output,
         input_grad,
@@ -831,7 +969,7 @@
         small[:experts].T,
         expert_grad[0],
         expert_grad[1],
-        jnp.swapaxes(expert_grad[2], 1, 2),
+        expert_grad[2],
     )
 
 

time: 639 us -> 574 us (0.90)
  waiting for transfers between devices: 208 us -> 172 us
  other arithmetic: 56.6 us -> 43.8 us
  starting transfers between devices: 103 us -> 93.8 us
  matrix products: 33.1 us -> 25.8 us
  local copies, waits for them, and re-layouts: 39.7 us -> 33.3 us
    ppermute x21, waiting for transfers between devices: 94.1 us -> 68.7 us  [the longest x4 27.7 us: reduce_second(): return ([mine, came], lax.ppermute(far, 'row', swap))]
    ppermute x16 -> x8, starting transfers between devices: 40.7 us -> 21.9 us  [shift(): lax.ppermute(x, 'dp', [(o[i], o[(i + by) % n]) for o in self.orders for i...]
    ppermute x28 -> x42, starting transfers between devices: 33.9 us -> 47.3 us  [ring_move(): lax.ppermute(x, 'dp', [(order[i], order[(i + by) % n]) for i in range(n)])]
    ppermute x28 -> x42, waiting for transfers between devices: 56.7 us -> 69.6 us  [ring_move(): lax.ppermute(x, 'dp', [(order[i], order[(i + by) % n]) for i in range(n)])]
    convert_element_type x15 -> x30, other arithmetic: 7.03 us -> 17.3 us  [the longest x24 12.4 us: add_halves(): return list(tie(*[t.astype(BF) for t in total]))]
    ppermute x2 -> x1, waiting for transfers between devices: 11.1 us -> 0.83 us  [sum_over_dp(): came = (yield [lax.ppermute(total, 'dp', pairs)])[0]]
    ppermute x16 -> x8, waiting for transfers between devices: 43 us -> 33.1 us  [shift(): lax.ppermute(x, 'dp', [(o[i], o[(i + by) % n]) for o in self.orders for i...]
    reduce_sum x3 -> x2, other arithmetic: 9.7 us -> 3.28 us  [the longest x1 2.2 us: norm_back(): inner = jnp.mean(weighted * values, axis=-1, keepdims=True)]
  transfers between devices with their start and end apart: 74 -> 78, of which waited for: 25 -> 32; matrix products, arithmetic and copies ran while one was open for 18% -> 14% of each run, Pallas kernels for 27% -> 31%
where the time goes in v3:
time: 574 us; the launch traced here: 565 us
  Pallas kernels  176 us (31%)
  waiting for transfers between devices  172 us (30%)
  starting transfers between devices  93.8 us (16%)
  other arithmetic  43.8 us (8%)
  local copies, waits for them, and re-layouts  33.3 us (6%)
  matrix products  25.8 us (4%)
  between operations  20 us (3%)
    pallas_call x8, Pallas kernels, expert_step(): pl.pallas_call(functools.partial(expert_kernel, k * rows, blocks, buffers...  93.2 us
    ppermute x42, waiting for transfers between devices, ring_move(): lax.ppermute(x, 'dp', [(order[i], order[(i + by) % n]) for i in range(n)])  69.6 us
    ppermute x42, starting transfers between devices, ring_move(): lax.ppermute(x, 'dp', [(order[i], order[(i + by) % n]) for i in range(n)])  47.3 us
    pallas_call x2, Pallas kernels, expert_grads(): pl.pallas_call(expert_grad_kernel, grid=(width // tile,), out_shape=[jax....  37.7 us
    ppermute x8, waiting for transfers between devices, shift(): lax.ppermute(x, 'dp', [(o[i], o[(i + by) % n]) for o in self.orders for i...  33.1 us
    ppermute x4, waiting for transfers between devices, reduce_second(): return ([mine, came], lax.ppermute(far, 'row', swap))  27.7 us
    pallas_call x1, Pallas kernels, attend_backward(): pl.pallas_call(functools.partial(attend_backward_kernel, kv, per_group, s...  22.4 us
    ppermute x8, starting transfers between devices, shift(): lax.ppermute(x, 'dp', [(o[i], o[(i + by) % n]) for o in self.orders for i...  21.9 us
  transfers between devices with their start and end apart: 78, of which 32 were waited for; matrix products, arithmetic and copies ran while one was open for 14% of the time, Pallas kernels for 31%

profile of v3, /device:TPU:0, one launch (start us, length us, event | category | flops | bytes accessed | tf_op | source)
XLA Modules:
  0.0 565.3 jit_solution(6948144489378534528)
XLA Ops:
  23.9 17.7 %collective-permute-done.refs_5_ = bf16[336,1536]{1,0:T(8,128)(2,1)} collective-permute-done((bf16[336,1536]{1,0:T(8,128)(2,1)S(1)}, bf16[336,1536]{1,0:T(8,128)(2,1)}, u32[]{:S(2)}, u32[]{:S(2)}) %collective-permute-start) | collective-permute-done | bytes 1032224 | tf_op jit(solution)/shard_map/ppermute | solution.py:479
  49.8 14.2 %attend_forward.1 = (bf16[1280,640]{1,0:T(8,128)(2,1)S(1)}, bf16[1280,384]{1,0:T(8,128)(2,1)S(1)}, bf16[1280,1536]{1,0:T(8,128)(2,1)S(1)}) custom-call(s32[4]{0:T(128)S(1)} %pad_add_fusion.1.shard_ref, s32[20]{0:T(128)S(1)} %select_reduce_fusion.3.parent_ref, bf16[336,640]{1,0:T(8,128)(2,1)S(1)} %convolution_convert_fusion.8.refs_0_, ...), custom_call_target="tpu_custom_call" | custom-call | flops 6039797760 | bytes 3276800 | tf_op jit(solution)/shard_map/attend_forward/pallas_call | solution.py:161
  80.1 19.9 %collective-permute-done.5 = bf16[320,1536]{1,0:T(8,128)(2,1)} collective-permute-done((bf16[320,1536]{1,0:T(8,128)(2,1)}, bf16[320,1536]{1,0:T(8,128)(2,1)}, u32[]{:S(2)}, u32[]{:S(2)}) %collective-permute-start.5) | collective-permute-done | bytes 983072 | tf_op jit(solution)/shard_map/ppermute | solution.py:492
  114.4 12.3 %collective-permute-done.8.xa_ref = bf16[160,1536]{1,0:T(8,128)(2,1)} collective-permute-done((bf16[160,1536]{1,0:T(8,128)(2,1)}, bf16[160,1536]{1,0:T(8,128)(2,1)}, u32[]{:S(2)}, u32[]{:S(2)}) %collective-permute-start.8) | collective-permute-done | bytes 491552 | tf_op jit(solution)/shard_map/ppermute | solution.py:537
  126.7 14.3 %collective-permute-done.9.xb_ref = bf16[160,1536]{1,0:T(8,128)(2,1)} collective-permute-done((bf16[160,1536]{1,0:T(8,128)(2,1)}, bf16[160,1536]{1,0:T(8,128)(2,1)}, u32[]{:S(2)}, u32[]{:S(2)}) %collective-permute-start.9) | collective-permute-done | bytes 491552 | tf_op jit(solution)/shard_map/ppermute | solution.py:537
  153.5 11.5 %expert_step.8 = (bf16[160,1536]{1,0:T(8,128)(2,1)S(1)}, bf16[160,1536]{1,0:T(8,128)(2,1)S(1)}, bf16[160,1536]{1,0:T(8,128)(2,1)S(1)}, bf16[160,1536]{1,0:T(8,12...) custom-call(s32[3]{0:T(128)S(1)} %get-tuple-element.516.at_ref, ...), custom_call_target="tpu_custom_call" | custom-call | flops 6039797760 | bytes 14352384 | tf_op jit(solution)/shard_map/expert_step/pallas_call | solution.py:384
  172.9 11.4 %expert_step.9 = (bf16[160,1536]{1,0:T(8,128)(2,1)S(1)}, bf16[160,1536]{1,0:T(8,128)(2,1)S(1)}, bf16[160,1536]{1,0:T(8,128)(2,1)S(1)}, bf16[160,1536]{1,0:T(8,12...) custom-call(s32[3]{0:T(128)S(1)} %copy-done.42, ...), custom_call_target="tpu_custom_call", output_to_operand_aliasing={{5}: (13, {}), {6}: (14, {}), {7}: (15, {}), {8}: (16, {}),... | custom-call | flops 6039797760 | bytes 14352384 | tf_op jit(solution)/shard_map/expert_step/pallas_call | solution.py:384
  186.6 11.4 %expert_step.10 = (bf16[160,1536]{1,0:T(8,128)(2,1)S(1)}, bf16[160,1536]{1,0:T(8,128)(2,1)S(1)}, bf16[160,1536]{1,0:T(8,128)(2,1)S(1)}, bf16[160,1536]{1,0:T(8,1...) custom-call(s32[3]{0:T(128)S(1)} %copy-done.41, ...), custom_call_target="tpu_custom_call", output_to_operand_aliasing={{5}: (13, {}), {6}: (14, {}), {7}: (15, {}), {8}: (16, {}),... | custom-call | flops 6039797760 | bytes 14352384 | tf_op jit(solution)/shard_map/expert_step/pallas_call | solution.py:384
  203.3 11.4 %expert_step.11 = (bf16[160,1536]{1,0:T(8,128)(2,1)S(1)}, bf16[160,1536]{1,0:T(8,128)(2,1)S(1)}, bf16[160,1536]{1,0:T(8,128)(2,1)S(1)}, bf16[160,1536]{1,0:T(8,1...) custom-call(s32[3]{0:T(128)S(1)} %copy-done.40, ...), custom_call_target="tpu_custom_call", output_to_operand_aliasing={{5}: (13, {}), {6}: (14, {}), {7}: (15, {}), {8}: (16, {}),... | custom-call | flops 6039797760 | bytes 14352384 | tf_op jit(solution)/shard_map/expert_step/pallas_call | solution.py:384
  214.8 6.4 %collective-permute-done.23.xa_ref = bf16[160,1536]{1,0:T(8,128)(2,1)S(1)} collective-permute-done((bf16[160,1536]{1,0:T(8,128)(2,1)}, bf16[160,1536]{1,0:T(8,128)(2,1)S(1)}, u32[]{:S(2)}, u32[]{:S(2)}) %collective-permute-start.23) | collective-permute-done | bytes 491552 | tf_op jit(solution)/shard_map/ppermute | solution.py:537
  227.2 11.9 %expert_step.12 = (bf16[160,1536]{1,0:T(8,128)(2,1)S(1)}, bf16[160,1536]{1,0:T(8,128)(2,1)S(1)}, bf16[160,1536]{1,0:T(8,128)(2,1)S(1)}, bf16[160,1536]{1,0:T(8,1...) custom-call(s32[3]{0:T(128)S(1)} %get-tuple-element.513.at_ref, ...), custom_call_target="tpu_custom_call", output_to_operand_aliasing={{5}: (13, {}), {6}: (14, {}), {7}: (15, {}), {8}: (16, {}),... | custom-call | flops 6039797760 | bytes 14352384 | tf_op jit(solution)/shard_map/expert_step/pallas_call | solution.py:384
  249.3 11.9 %expert_step.13 = (bf16[160,1536]{1,0:T(8,128)(2,1)S(1)}, bf16[160,1536]{1,0:T(8,128)(2,1)S(1)}, bf16[160,1536]{1,0:T(8,128)(2,1)S(1)}, bf16[160,1536]{1,0:T(8,1...) custom-call(s32[3]{0:T(128)S(1)} %get-tuple-element.512.at_ref, ...), custom_call_target="tpu_custom_call", output_to_operand_aliasing={{5}: (13, {}), {6}: (14, {}), {7}: (15, {}), {8}: (16, {}),... | custom-call | flops 6039797760 | bytes 14352384 | tf_op jit(solution)/shard_map/expert_step/pallas_call | solution.py:384
  271.2 11.9 %expert_step.14 = (bf16[160,1536]{1,0:T(8,128)(2,1)S(1)}, bf16[160,1536]{1,0:T(8,128)(2,1)S(1)}, bf16[160,1536]{1,0:T(8,128)(2,1)S(1)}, bf16[160,1536]{1,0:T(8,1...) custom-call(s32[3]{0:T(128)S(1)} %get-tuple-element.511.at_ref, ...), custom_call_target="tpu_custom_call", output_to_operand_aliasing={{5}: (13, {}), {6}: (14, {}), {7}: (15, {}), {8}: (16, {}),... | custom-call | flops 6039797760 | bytes 14352384 | tf_op jit(solution)/shard_map/expert_step/pallas_call | solution.py:384
  292.0 11.9 %expert_step.15 = (bf16[160,1536]{1,0:T(8,128)(2,1)S(1)}, bf16[160,1536]{1,0:T(8,128)(2,1)S(1)}, bf16[160,1536]{1,0:T(8,128)(2,1)S(1)}, bf16[160,1536]{1,0:T(8,1...) custom-call(s32[3]{0:T(128)S(1)} %get-tuple-element.510.at_ref, ...), custom_call_target="tpu_custom_call", output_to_operand_aliasing={{5}: (13, {}), {6}: (14, {}), {7}: (15, {}), {8}: (16, {}),... | custom-call | flops 6039797760 | bytes 14352384 | tf_op jit(solution)/shard_map/expert_step/pallas_call | solution.py:384
  338.5 18.8 %expert_grads.2 = (bf16[2,3,1536,128]{3,2,1,0:T(8,128)(2,1)}, bf16[2,3,1536,128]{3,2,1,0:T(8,128)(2,1)}) custom-call(bf16[2,2560,512]{2,1,0:T(8,128)(2,1)} %get-tuple-element.453.act_ref, bf16[2,2560,512]{2,1,0:T(8,128)(2,1)} %get-tuple-element.454.dgate_ref, bf16[2,2560,512]{2,1,0:T(8,128)(2,1)} %get-tuple-element.455.dup_ref, ...), custom_call_target="tpu_custom_call" | custom-call | flops 12079595520 | bytes 9437184 | tf_op jit(solution)/shard_map/expert_grads/pallas_call | solution.py:426
  365.6 6.7 %collective-permute-done.46 = bf16[160,1536]{1,0:T(8,128)(2,1)S(1)} collective-permute-done((bf16[160,1536]{1,0:T(8,128)(2,1)S(1)}, bf16[160,1536]{1,0:T(8,128)(2,1)S(1)}, u32[]{:S(2)}, u32[]{:S(2)}) %collective-permute-start.46) | collective-permute-done | bytes 491552 | tf_op jit(solution)/shard_map/ppermute | solution.py:537
  377.7 22.4 %attend_backward.1 = bf16[1280,640]{1,0:T(8,128)(2,1)S(1)} custom-call(s32[4]{0:T(128)S(1)} %copy-done.44, s32[20]{0:T(128)S(1)} %copy-done.50, bf16[1280,640]{1,0:T(8,128)(2,1)S(1)} %copy-done.56, bf16[320,384]{1,0:T(8,128)(2,1)S(1)} %convolution_convert_fusion.12.refs_0_, bf16[320,384]{1,0:T(8,128)(2,1)S(1)} %convolution_convert_fusion.11.refs_1_, ...), custom_call_target="tpu_custom_call" | custom-call | flops 15099494400 | bytes 4915200 | tf_op jit(solution)/shard_map/attend_backward/pallas_call | solution.py:230
  416.9 8.3 %collective-permute-done.53 = bf16[192,1024]{1,0:T(8,128)(2,1)S(1)} collective-permute-done((bf16[192,1024]{1,0:T(8,128)(2,1)S(1)}, bf16[192,1024]{1,0:T(8,128)(2,1)S(1)}, u32[]{:S(2)}, u32[]{:S(2)}) %collective-permute-start.53) | collective-permute-done | bytes 393248 | tf_op jit(solution)/shard_map/ppermute | solution.py:572
  437.6 18.9 %expert_grads.3 = (bf16[2,3,1536,128]{3,2,1,0:T(8,128)(2,1)}, bf16[2,3,1536,128]{3,2,1,0:T(8,128)(2,1)}) custom-call(bf16[2,2560,512]{2,1,0:T(8,128)(2,1)} %get-tuple-element.453.act_ref, bf16[2,2560,512]{2,1,0:T(8,128)(2,1)} %get-tuple-element.454.dgate_ref, bf16[2,2560,512]{2,1,0:T(8,128)(2,1)} %get-tuple-element.455.dup_ref, ...), custom_call_target="tpu_custom_call" | custom-call | flops 12079595520 | bytes 9437184 | tf_op jit(solution)/shard_map/expert_grads/pallas_call | solution.py:426
  470.8 12.3 %collective-permute-done.65 = f32[18,1536]{1,0:T(8,128)S(1)} collective-permute-done((f32[18,1536]{1,0:T(8,128)S(1)}, f32[18,1536]{1,0:T(8,128)S(1)}, u32[]{:S(2)}, u32[]{:S(2)}) %collective-permute-start.65) | collective-permute-done | bytes 110624 | tf_op jit(solution)/shard_map/ppermute | solution.py:625
  484.0 7.7 %collective-permute-done.63.refs_5_ = bf16[3,1536,128]{2,1,0:T(8,128)(2,1)S(1)} collective-permute-done((bf16[3,1536,128]{2,1,0:T(8,128)(2,1)S(1)}, bf16[3,1536,128]{2,1,0:T(8,128)(2,1)S(1)}, u32[]{:S(2)}, u32[]{:S(2)}) %collective-permute-start.63) | collective-permute-done | bytes 1179680 | tf_op jit(solution)/shard_map/ppermute | solution.py:492
  495.0 14.6 %collective-permute-start.71 = (bf16[384,1024]{1,0:T(8,128)(2,1)S(1)}, bf16[384,1024]{1,0:T(8,128)(2,1)S(1)}, u32[]{:S(2)}, u32[]{:S(2)}) collective-permute-start(bf16[384,1024]{1,0:T(8,128)(2,1)S(1)} %add_convert_fusion.3.refs_0_), channel_id=1, source_target_pairs={{0,8},{4,0},{12,4},{8,12},{24,16},{28,24},{20,28},{16,20},{1,9},{5... | collective-permute-start | bytes 2359304 | tf_op jit(solution)/shard_map/ppermute | solution.py:572
  512.7 14.3 %collective-permute-done.70.refs_1_ = bf16[384,1024]{1,0:T(8,128)(2,1)S(1)} collective-permute-done((bf16[384,1024]{1,0:T(8,128)(2,1)S(1)}, bf16[384,1024]{1,0:T(8,128)(2,1)S(1)}, u32[]{:S(2)}, u32[]{:S(2)}) %collective-permute-start.70) | collective-permute-done | bytes 786464 | tf_op jit(solution)/shard_map/ppermute | solution.py:572
  529.5 7.6 %collective-permute-done.72.refs_3_ = bf16[192,1024]{1,0:T(8,128)(2,1)S(1)} collective-permute-done((bf16[192,1024]{1,0:T(8,128)(2,1)S(1)}, bf16[192,1024]{1,0:T(8,128)(2,1)S(1)}, u32[]{:S(2)}, u32[]{:S(2)}) %collective-permute-start.72) | collective-permute-done | bytes 393248 | tf_op jit(solution)/shard_map/ppermute | solution.py:572
  (512 shorter events, 235.5 us)
Async XLA Ops:
  7.2 164.1 %all-gather.2.cloned.1.call-start = ((), (), s32[]{:S(2)}) async-start(), calls=%async_computation.1 | async-start | bytes 9732096 | tf_op jit(solution)/shard_map/all_gather | solution.py:765
  14.9 26.7 %collective-permute-start = (bf16[336,1536]{1,0:T(8,128)(2,1)S(1)}, bf16[336,1536]{1,0:T(8,128)(2,1)}, u32[]{:S(2)}, u32[]{:S(2)}) collective-permute-start(bf16[336,1536]{1,0:T(8,128)(2,1)S(1)} %pad_maximum_fusion.2.refs_4_), channel_id=1, source_target_pairs={{0,2},{2,0},{1,3},{3,1},{4,6},{6,4},{5,7},{7,5},{8,10},{10,8},{9,1... | collective-permute-start | bytes 3096584 | tf_op jit(solution)/shard_map/ppermute | solution.py:479
  17.8 25.5 %collective-permute-start.1 = (bf16[336,1536]{1,0:T(8,128)(2,1)S(1)}, bf16[336,1536]{1,0:T(8,128)(2,1)}, u32[]{:S(2)}, u32[]{:S(2)}) collective-permute-start(bf16[336,1536]{1,0:T(8,128)(2,1)S(1)} %pad_maximum_fusion.2.refs_4_), channel_id=1, source_target_pairs={{0,1},{1,0},{2,3},{3,2},{4,5},{5,4},{6,7},{7,6},{8,9},{9,8},{10,11... | collective-permute-start | bytes 3096584 | tf_op jit(solution)/shard_map/ppermute | solution.py:480
  21.8 44.2 %collective-permute-start.3 = (bf16[3,1536,128]{2,1,0:T(8,128)(2,1)S(1)}, bf16[3,1536,128]{2,1,0:T(8,128)(2,1)}, u32[]{:S(2)}, u32[]{:S(2)}) collective-permute-start(bf16[3,1536,128]{2,1,0:T(8,128)(2,1)S(1)} %pad_maximum_fusion.refs_0_), channel_id=1, source_target_pairs={{0,2},{2,0},{1,3},{3,1},{4,6},{6,4},{5,7},{7,5},{8,10},{10,8},{9,1... | collective-permute-start | bytes 3538952 | tf_op jit(solution)/shard_map/ppermute | solution.py:479
  75.9 24.1 %collective-permute-start.5 = (bf16[320,1536]{1,0:T(8,128)(2,1)}, bf16[320,1536]{1,0:T(8,128)(2,1)}, u32[]{:S(2)}, u32[]{:S(2)}) collective-permute-start(bf16[320,1536]{1,0:T(8,128)(2,1)} %fusion.36), channel_id=1, source_target_pairs={{0,2},{2,0},{1,3},{3,1},{4,6},{6,4},{5,7},{7,5},{8,10},{10,8},{9,1... | collective-permute-start | bytes 2949128 | tf_op jit(solution)/shard_map/ppermute | solution.py:492
  100.0 40.9 %collective-permute-start.10 = (bf16[3,1536,128]{2,1,0:T(8,128)(2,1)S(1)}, bf16[3,1536,128]{2,1,0:T(8,128)(2,1)}, u32[]{:S(2)}, u32[]{:S(2)}) collective-permute-start(bf16[3,1536,128]{2,1,0:T(8,128)(2,1)S(1)} %pad_maximum_fusion.1.refs_4_), channel_id=1, source_target_pairs={{0,2},{2,0},{1,3},{3,1},{4,6},{6,4},{5,7},{7,5},{8,10},{10,8},{9,1... | collective-permute-start | bytes 3538952 | tf_op jit(solution)/shard_map/ppermute | solution.py:479
  107.5 33.5 %collective-permute-start.9 = (bf16[160,1536]{1,0:T(8,128)(2,1)}, bf16[160,1536]{1,0:T(8,128)(2,1)}, u32[]{:S(2)}, u32[]{:S(2)}) collective-permute-start(bf16[160,1536]{1,0:T(8,128)(2,1)} %get-tuple-element.536.xb_ref), channel_id=1, source_target_pairs={{0,4},{8,0},{16,8},{24,16},{28,24},{20,28},{12,20},{4,12},{1,5},{9... | collective-permute-start | bytes 1474568 | tf_op jit(solution)/shard_map/ppermute | solution.py:537
  108.0 43.3 %collective-permute-start.11 = (bf16[3,1536,128]{2,1,0:T(8,128)(2,1)S(1)}, bf16[3,1536,128]{2,1,0:T(8,128)(2,1)}, u32[]{:S(2)}, u32[]{:S(2)}) collective-permute-start(bf16[3,1536,128]{2,1,0:T(8,128)(2,1)S(1)} %pad_maximum_fusion.1.refs_4_), channel_id=1, source_target_pairs={{0,1},{1,0},{2,3},{3,2},{4,5},{5,4},{6,7},{7,6},{8,9},{9,8},{10,11... | collective-permute-start | bytes 3538952 | tf_op jit(solution)/shard_map/ppermute | solution.py:480
  283.4 23.7 %collective-permute-start.33 = (bf16[160,1536]{1,0:T(8,128)(2,1)S(1)}, bf16[160,1536]{1,0:T(8,128)(2,1)S(1)}, u32[]{:S(2)}, u32[]{:S(2)}) collective-permute-start(bf16[160,1536]{1,0:T(8,128)(2,1)S(1)} %add_convert_fusion.19), channel_id=1, source_target_pairs={{0,8},{8,16},{16,24},{24,28},{28,20},{20,12},{12,4},{4,0},{1,9},{9... | collective-permute-start | bytes 1474568 | tf_op jit(solution)/shard_map/ppermute | solution.py:537
  283.7 23.4 %collective-permute-start.34 = (bf16[160,1536]{1,0:T(8,128)(2,1)S(1)}, bf16[160,1536]{1,0:T(8,128)(2,1)S(1)}, u32[]{:S(2)}, u32[]{:S(2)}) collective-permute-start(bf16[160,1536]{1,0:T(8,128)(2,1)S(1)} %add_convert_fusion.18), channel_id=1, source_target_pairs={{0,4},{8,0},{16,8},{24,16},{28,24},{20,28},{12,20},{4,12},{1,5},{9... | collective-permute-start | bytes 1474568 | tf_op jit(solution)/shard_map/ppermute | solution.py:537
  333.1 24.9 %collective-permute-start.41 = (bf16[320,1536]{1,0:T(8,128)(2,1)S(1)}, bf16[320,1536]{1,0:T(8,128)(2,1)}, u32[]{:S(2)}, u32[]{:S(2)}) collective-permute-start(bf16[320,1536]{1,0:T(8,128)(2,1)S(1)} %get-tuple-element.406), channel_id=1, source_target_pairs={{0,2},{2,0},{1,3},{3,1},{4,6},{6,4},{5,7},{7,5},{8,10},{10,8},{9,1... | collective-permute-start | bytes 2949128 | tf_op jit(solution)/shard_map/ppermute | solution.py:479
  333.7 29.2 %collective-permute-start.44 = (bf16[320,1536]{1,0:T(8,128)(2,1)S(1)}, bf16[320,1536]{1,0:T(8,128)(2,1)}, u32[]{:S(2)}, u32[]{:S(2)}) collective-permute-start(bf16[320,1536]{1,0:T(8,128)(2,1)S(1)} %get-tuple-element.406), channel_id=1, source_target_pairs={{0,1},{1,0},{2,3},{3,2},{4,5},{5,4},{6,7},{7,6},{8,9},{9,8},{10,11... | collective-permute-start | bytes 2949128 | tf_op jit(solution)/shard_map/ppermute | solution.py:480
  373.8 31.0 %collective-permute-start.50 = (bf16[160,1536]{1,0:T(8,128)(2,1)S(1)}, bf16[160,1536]{1,0:T(8,128)(2,1)S(1)}, u32[]{:S(2)}, u32[]{:S(2)}) collective-permute-start(bf16[160,1536]{1,0:T(8,128)(2,1)S(1)} %add_convert_fusion.11), channel_id=1, source_target_pairs={{0,8},{8,16},{16,24},{24,28},{28,20},{20,12},{12,4},{4,0},{1,9},{9... | collective-permute-start | bytes 1474568 | tf_op jit(solution)/shard_map/ppermute | solution.py:537
  375.3 29.5 %collective-permute-start.51 = (bf16[160,1536]{1,0:T(8,128)(2,1)S(1)}, bf16[160,1536]{1,0:T(8,128)(2,1)S(1)}, u32[]{:S(2)}, u32[]{:S(2)}) collective-permute-start(bf16[160,1536]{1,0:T(8,128)(2,1)S(1)} %add_convert_fusion.10), channel_id=1, source_target_pairs={{0,4},{8,0},{16,8},{24,16},{28,24},{20,28},{12,20},{4,12},{1,5},{9... | collective-permute-start | bytes 1474568 | tf_op jit(solution)/shard_map/ppermute | solution.py:537
  376.2 28.6 %collective-permute-start.49 = (bf16[3,1536,128]{2,1,0:T(8,128)(2,1)S(1)}, bf16[3,1536,128]{2,1,0:T(8,128)(2,1)S(1)}, u32[]{:S(2)}, u32[]{:S(2)}) collective-permute-start(bf16[3,1536,128]{2,1,0:T(8,128)(2,1)S(1)} %fusion.31), channel_id=1, source_target_pairs={{0,2},{2,0},{1,3},{3,1},{4,6},{6,4},{5,7},{7,5},{8,10},{10,8},{9,1... | collective-permute-start | bytes 3538952 | tf_op jit(solution)/shard_map/ppermute | solution.py:492
  428.4 30.2 %collective-permute-start.60 = (bf16[160,1536]{1,0:T(8,128)(2,1)}, bf16[160,1536]{1,0:T(8,128)(2,1)}, u32[]{:S(2)}, u32[]{:S(2)}) collective-permute-start(bf16[160,1536]{1,0:T(8,128)(2,1)} %add_convert_fusion.7), channel_id=1, source_target_pairs={{0,8},{8,16},{16,24},{24,28},{28,20},{20,12},{12,4},{4,0},{1,9},{9... | collective-permute-start | bytes 1474568 | tf_op jit(solution)/shard_map/ppermute | solution.py:537
  428.5 30.0 %collective-permute-start.61 = (bf16[160,1536]{1,0:T(8,128)(2,1)}, bf16[160,1536]{1,0:T(8,128)(2,1)}, u32[]{:S(2)}, u32[]{:S(2)}) collective-permute-start(bf16[160,1536]{1,0:T(8,128)(2,1)} %add_convert_fusion.6), channel_id=1, source_target_pairs={{0,4},{8,0},{16,8},{24,16},{28,24},{20,28},{12,20},{4,12},{1,5},{9... | collective-permute-start | bytes 1474568 | tf_op jit(solution)/shard_map/ppermute | solution.py:537
  431.5 25.0 %collective-permute-start.56 = (bf16[384,1024]{1,0:T(8,128)(2,1)}, bf16[384,1024]{1,0:T(8,128)(2,1)}, u32[]{:S(2)}, u32[]{:S(2)}) collective-permute-start(bf16[384,1024]{1,0:T(8,128)(2,1)} %fusion.40), channel_id=1, source_target_pairs={{0,4},{4,12},{12,8},{8,0},{24,28},{28,20},{20,16},{16,24},{1,5},{5... | collective-permute-start | bytes 2359304 | tf_op jit(solution)/shard_map/ppermute | solution.py:572
  433.1 23.4 %collective-permute-start.57 = (bf16[384,1024]{1,0:T(8,128)(2,1)}, bf16[384,1024]{1,0:T(8,128)(2,1)}, u32[]{:S(2)}, u32[]{:S(2)}) collective-permute-start(bf16[384,1024]{1,0:T(8,128)(2,1)} %pad_maximum_fusion.3), channel_id=1, source_target_pairs={{0,8},{4,0},{12,4},{8,12},{24,16},{28,24},{20,28},{16,20},{1,9},{5... | collective-permute-start | bytes 2359304 | tf_op jit(solution)/shard_map/ppermute | solution.py:572
  463.7 28.1 %collective-permute-start.63 = (bf16[3,1536,128]{2,1,0:T(8,128)(2,1)S(1)}, bf16[3,1536,128]{2,1,0:T(8,128)(2,1)S(1)}, u32[]{:S(2)}, u32[]{:S(2)}) collective-permute-start(bf16[3,1536,128]{2,1,0:T(8,128)(2,1)S(1)} %fusion.32), channel_id=1, source_target_pairs={{0,2},{2,0},{1,3},{3,1},{4,6},{6,4},{5,7},{7,5},{8,10},{10,8},{9,1... | collective-permute-start | bytes 3538952 | tf_op jit(solution)/shard_map/ppermute | solution.py:492
  467.0 24.7 %collective-permute-start.67 = (bf16[160,1536]{1,0:T(8,128)(2,1)S(1)}, bf16[160,1536]{1,0:T(8,128)(2,1)S(1)}, u32[]{:S(2)}, u32[]{:S(2)}) collective-permute-start(bf16[160,1536]{1,0:T(8,128)(2,1)S(1)} %add_convert_fusion.5), channel_id=1, source_target_pairs={{0,8},{8,16},{16,24},{24,28},{28,20},{20,12},{12,4},{4,0},{1,9},{9... | collective-permute-start | bytes 1474568 | tf_op jit(solution)/shard_map/ppermute | solution.py:537
  467.6 26.3 %collective-permute-start.68 = (bf16[160,1536]{1,0:T(8,128)(2,1)S(1)}, bf16[160,1536]{1,0:T(8,128)(2,1)S(1)}, u32[]{:S(2)}, u32[]{:S(2)}) collective-permute-start(bf16[160,1536]{1,0:T(8,128)(2,1)S(1)} %add_convert_fusion.4), channel_id=1, source_target_pairs={{0,4},{8,0},{16,8},{24,16},{28,24},{20,28},{12,20},{4,12},{1,5},{9... | collective-permute-start | bytes 1474568 | tf_op jit(solution)/shard_map/ppermute | solution.py:537
  494.2 32.7 %collective-permute-start.70 = (bf16[384,1024]{1,0:T(8,128)(2,1)S(1)}, bf16[384,1024]{1,0:T(8,128)(2,1)S(1)}, u32[]{:S(2)}, u32[]{:S(2)}) collective-permute-start(bf16[384,1024]{1,0:T(8,128)(2,1)S(1)} %add_convert_fusion.3.refs_0_), channel_id=1, source_target_pairs={{0,4},{4,12},{12,8},{8,0},{24,28},{28,20},{20,16},{16,24},{1,5},{5... | collective-permute-start | bytes 2359304 | tf_op jit(solution)/shard_map/ppermute | solution.py:572
  495.0 32.2 %collective-permute-start.71 = (bf16[384,1024]{1,0:T(8,128)(2,1)S(1)}, bf16[384,1024]{1,0:T(8,128)(2,1)S(1)}, u32[]{:S(2)}, u32[]{:S(2)}) collective-permute-start(bf16[384,1024]{1,0:T(8,128)(2,1)S(1)} %add_convert_fusion.3.refs_0_), channel_id=1, source_target_pairs={{0,8},{4,0},{12,4},{8,12},{24,16},{28,24},{20,28},{16,20},{1,9},{5... | collective-permute-start | bytes 2359304 | tf_op jit(solution)/shard_map/ppermute | solution.py:572
  (161 other events, 1664.5 us)
Sparse Core Ops, SparseCore 0:
  12.4 139.0 all-gather.1

commit v4 on v3

--- a/solution.py
+++ b/solution.py
@@ -458,15 +458,17 @@
     first = pl.BlockSpec((1, 3, width, unit), lambda i: (0, 0, 0, 0))
     specs = [first] * (terms - 1) + [pl.BlockSpec((3, width, unit), lambda i: (0, 0, 0))]
     shapes = [(count, width, unit), (count, width, unit), (count, unit, width)]
-    return pl.pallas_call(
-        functools.partial(finish_kernel, terms),
-        grid=(1,),
-        out_shape=[jax.ShapeDtypeStruct(v, F32) for v in shapes],
-        in_specs=specs * count,
-        out_specs=[pl.BlockSpec(v, lambda i: (0, 0, 0)) for v in shapes],
-        compiler_params=pltpu.CompilerParams(vmem_limit_bytes=48 * MIB),
-        name="finish_grads",
-    )(*[v for near, across in sums for v in (*near, across)])
+    return list(
+        pl.pallas_call(
+            functools.partial(finish_kernel, terms),
+            grid=(1,),
+            out_shape=[jax.ShapeDtypeStruct(v, F32) for v in shapes],
+            in_specs=specs * count,
+            out_specs=[pl.BlockSpec(v, lambda i: (0, 0, 0)) for v in shapes],
+            compiler_params=pltpu.CompilerParams(vmem_limit_bytes=48 * MIB),
+            name="finish_grads",
+        )(*[v for near, across in sums for v in (*near, across)])
+    )
 
 
 def tree_moves():
@@ -619,8 +621,8 @@
 def small_sum(value, part):
     sizes = [lax.axis_size(name) for name in ("dp", "row", "col")]
     if sizes != [8, 2, 2]:
-        return lax.psum(value, ("col", "row", "dp")[part])
-    hops = [[("col", 2, 1), ("dp", 8, 1)], [("row", 2, 1)], [("dp", 8, 2), ("dp", 8, 4)]]
+        return lax.psum(value, ("col", "row", "dp")[part]) if part < 3 else value
+    hops = [[("col", 2, 1), ("dp", 8, 1)], [("row", 2, 1)], [("dp", 8, 2)], [("dp", 8, 4)]]
     for name, size, bit in hops[part]:
         value = value + lax.ppermute(value, name, [(i, i ^ bit) for i in range(size)])
     return value
@@ -813,7 +815,6 @@
     kept = None
     backs, mixes, dots, came = [], [], [], []
     coming = [ring_move(x[0], order, 1), ring_move(x[1], order, -1)]
-    *coming, weights[-1][1] = tie(*coming, weights[-1][1])
     weights[1:] = [tree_finish(blocks) for blocks in weights[1:]]
     weights = [joined(blocks) for blocks in weights]
     for k in range(dp_size):
@@ -821,8 +822,7 @@
             x = coming
             if k > 1:
                 x = [ring_move(x[0], order, 1), ring_move(x[1], order, -1)]
-            if k > 1:
-                *x, dots[k - 2] = tie(*x, dots[k - 2])
+            *x, dots[k - 1] = tie(*x, dots[k - 1])
             if k > 2:
                 *x, came[k - 2][0], came[k - 2][1] = tie(*x, *came[k - 2])
             coming = x
@@ -953,10 +953,11 @@
     across, *came = tie(across, *came)
     expert_sums[-1] = (near, across)
     came = stages.send(came)
-    small, *came = tie(small, *came)
+    expert_grad = finish_grads(expert_sums)
+    small = small_sum(small, 2)
+    small, expert_grad[0], *came = tie(small, expert_grad[0], *came)
     query_grad, key_grad, value_grad, out_grad = stages.send(came)
-    small = small_sum(small, 2)
-    expert_grad = finish_grads(expert_sums)
+    small = small_sum(small, 3)
     return (
         output,
         input_grad,

time: 574 us -> 556 us (0.969)
  waiting for transfers between devices: 172 us -> 155 us
    ppermute x42, waiting for transfers between devices: 69.6 us -> 54.7 us  [ring_move(): lax.ppermute(x, 'dp', [(order[i], order[(i + by) % n]) for i in range(n)])]
    ppermute x8, waiting for transfers between devices: 33.1 us -> 20.2 us  [shift(): lax.ppermute(x, 'dp', [(o[i], o[(i + by) % n]) for o in self.orders for i...]
    ppermute x4, waiting for transfers between devices: 19.6 us -> 30.4 us  [gather(): across = lax.ppermute(x if again is None else again, 'row', swap)]
    unnamed x226 -> x224, local copies, waits for them, and re-layouts: 20.4 us -> 21.4 us
  transfers between devices with their start and end apart: 78 -> 78, of which waited for: 32 -> 36; matrix products, arithmetic and copies ran while one was open for 14% -> 14% of each run, Pallas kernels for 31% -> 32%
where the time goes in v4:
time: 556 us; the launch traced here: 547 us
  Pallas kernels  177 us (32%)
  waiting for transfers between devices  155 us (28%)
  starting transfers between devices  94.1 us (17%)
  other arithmetic  44.1 us (8%)
  local copies, waits for them, and re-layouts  34.7 us (6%)
  matrix products  22 us (4%)
  between operations  19.9 us (4%)
    pallas_call x8, Pallas kernels, expert_step(): pl.pallas_call(functools.partial(expert_kernel, k * rows, blocks, buffers...  94 us
    ppermute x42, waiting for transfers between devices, ring_move(): lax.ppermute(x, 'dp', [(order[i], order[(i + by) % n]) for i in range(n)])  54.7 us
    ppermute x42, starting transfers between devices, ring_move(): lax.ppermute(x, 'dp', [(order[i], order[(i + by) % n]) for i in range(n)])  45.4 us
    pallas_call x2, Pallas kernels, expert_grads(): pl.pallas_call(expert_grad_kernel, grid=(width // tile,), out_shape=[jax....  37.6 us
    ppermute x4, waiting for transfers between devices, gather(): across = lax.ppermute(x if again is None else again, 'row', swap)  30.4 us
    ppermute x4, waiting for transfers between devices, reduce_second(): return ([mine, came], lax.ppermute(far, 'row', swap))  25.7 us
    ppermute x8, starting transfers between devices, shift(): lax.ppermute(x, 'dp', [(o[i], o[(i + by) % n]) for o in self.orders for i...  23.2 us
    pallas_call x1, Pallas kernels, attend_backward(): pl.pallas_call(functools.partial(attend_backward_kernel, kv, per_group, s...  22.4 us
  transfers between devices with their start and end apart: 78, of which 36 were waited for; matrix products, arithmetic and copies ran while one was open for 14% of the time, Pallas kernels for 32%

profile of v4, /device:TPU:0, one launch (start us, length us, event | category | flops | bytes accessed | tf_op | source)
XLA Modules:
  0.0 547.3 jit_solution(12853326988140787696)
XLA Ops:
  23.9 17.7 %collective-permute-done.refs_5_ = bf16[336,1536]{1,0:T(8,128)(2,1)} collective-permute-done((bf16[336,1536]{1,0:T(8,128)(2,1)S(1)}, bf16[336,1536]{1,0:T(8,128)(2,1)}, u32[]{:S(2)}, u32[]{:S(2)}) %collective-permute-start) | collective-permute-done | bytes 1032224 | tf_op jit(solution)/shard_map/ppermute | solution.py:481
  49.8 14.2 %attend_forward.1 = (bf16[1280,640]{1,0:T(8,128)(2,1)S(1)}, bf16[1280,384]{1,0:T(8,128)(2,1)S(1)}, bf16[1280,1536]{1,0:T(8,128)(2,1)S(1)}) custom-call(s32[4]{0:T(128)S(1)} %pad_add_fusion.1.shard_ref, s32[20]{0:T(128)S(1)} %select_reduce_fusion.3.parent_ref, bf16[336,640]{1,0:T(8,128)(2,1)S(1)} %convolution_convert_fusion.8.refs_0_, ...), custom_call_target="tpu_custom_call" | custom-call | flops 6039797760 | bytes 3276800 | tf_op jit(solution)/shard_map/attend_forward/pallas_call | solution.py:161
  69.1 5.4 collective-permute-done.4
  83.2 16.7 %collective-permute-done.5 = bf16[320,1536]{1,0:T(8,128)(2,1)} collective-permute-done((bf16[320,1536]{1,0:T(8,128)(2,1)}, bf16[320,1536]{1,0:T(8,128)(2,1)}, u32[]{:S(2)}, u32[]{:S(2)}) %collective-permute-start.5) | collective-permute-done | bytes 983072 | tf_op jit(solution)/shard_map/ppermute | solution.py:494
  116.4 10.9 %collective-permute-done.10.refs_5_ = bf16[3,1536,128]{2,1,0:T(8,128)(2,1)} collective-permute-done((bf16[3,1536,128]{2,1,0:T(8,128)(2,1)S(1)}, bf16[3,1536,128]{2,1,0:T(8,128)(2,1)}, u32[]{:S(2)}, u32[]{:S(2)}) %collective-permute-start.10) | collective-permute-done | bytes 1179680 | tf_op jit(solution)/shard_map/ppermute | solution.py:481
  130.3 12.5 %expert_step.8 = (bf16[160,1536]{1,0:T(8,128)(2,1)S(1)}, bf16[160,1536]{1,0:T(8,128)(2,1)S(1)}, bf16[160,1536]{1,0:T(8,128)(2,1)S(1)}, bf16[160,1536]{1,0:T(8,12...) custom-call(s32[3]{0:T(128)S(1)} %get-tuple-element.518.at_ref, ...), custom_call_target="tpu_custom_call" | custom-call | flops 6039797760 | bytes 14352384 | tf_op jit(solution)/shard_map/expert_step/pallas_call | solution.py:384
  158.4 11.4 %expert_step.9 = (bf16[160,1536]{1,0:T(8,128)(2,1)S(1)}, bf16[160,1536]{1,0:T(8,128)(2,1)S(1)}, bf16[160,1536]{1,0:T(8,128)(2,1)S(1)}, bf16[160,1536]{1,0:T(8,12...) custom-call(s32[3]{0:T(128)S(1)} %copy-done.44, ...), custom_call_target="tpu_custom_call", output_to_operand_aliasing={{5}: (13, {}), {6}: (14, {}), {7}: (15, {}), {8}: (16, {}),... | custom-call | flops 6039797760 | bytes 14352384 | tf_op jit(solution)/shard_map/expert_step/pallas_call | solution.py:384
  175.7 11.4 %expert_step.10 = (bf16[160,1536]{1,0:T(8,128)(2,1)S(1)}, bf16[160,1536]{1,0:T(8,128)(2,1)S(1)}, bf16[160,1536]{1,0:T(8,128)(2,1)S(1)}, bf16[160,1536]{1,0:T(8,1...) custom-call(s32[3]{0:T(128)S(1)} %copy-done.43, ...), custom_call_target="tpu_custom_call", output_to_operand_aliasing={{5}: (13, {}), {6}: (14, {}), {7}: (15, {}), {8}: (16, {}),... | custom-call | flops 6039797760 | bytes 14352384 | tf_op jit(solution)/shard_map/expert_step/pallas_call | solution.py:384
  187.2 7.3 %collective-permute-done.19.xa_ref = bf16[160,1536]{1,0:T(8,128)(2,1)S(1)} collective-permute-done((bf16[160,1536]{1,0:T(8,128)(2,1)}, bf16[160,1536]{1,0:T(8,128)(2,1)S(1)}, u32[]{:S(2)}, u32[]{:S(2)}) %collective-permute-start.19) | collective-permute-done | bytes 491552 | tf_op jit(solution)/shard_map/ppermute | solution.py:539
  200.5 11.7 %expert_step.11 = (bf16[160,1536]{1,0:T(8,128)(2,1)S(1)}, bf16[160,1536]{1,0:T(8,128)(2,1)S(1)}, bf16[160,1536]{1,0:T(8,128)(2,1)S(1)}, bf16[160,1536]{1,0:T(8,1...) custom-call(s32[3]{0:T(128)S(1)} %copy-done.42, ...), custom_call_target="tpu_custom_call", output_to_operand_aliasing={{5}: (13, {}), {6}: (14, {}), {7}: (15, {}), {8}: (16, {}),... | custom-call | flops 6039797760 | bytes 14352384 | tf_op jit(solution)/shard_map/expert_step/pallas_call | solution.py:384
  212.3 6.0 %collective-permute-done.23.xa_ref = bf16[160,1536]{1,0:T(8,128)(2,1)S(1)} collective-permute-done((bf16[160,1536]{1,0:T(8,128)(2,1)S(1)}, bf16[160,1536]{1,0:T(8,128)(2,1)S(1)}, u32[]{:S(2)}, u32[]{:S(2)}) %collective-permute-start.23) | collective-permute-done | bytes 491552 | tf_op jit(solution)/shard_map/ppermute | solution.py:539
  223.6 11.7 %expert_step.12 = (bf16[160,1536]{1,0:T(8,128)(2,1)S(1)}, bf16[160,1536]{1,0:T(8,128)(2,1)S(1)}, bf16[160,1536]{1,0:T(8,128)(2,1)S(1)}, bf16[160,1536]{1,0:T(8,1...) custom-call(s32[3]{0:T(128)S(1)} %get-tuple-element.515.at_ref, ...), custom_call_target="tpu_custom_call", output_to_operand_aliasing={{5}: (13, {}), {6}: (14, {}), {7}: (15, {}), {8}: (16, {}),... | custom-call | flops 6039797760 | bytes 14352384 | tf_op jit(solution)/shard_map/expert_step/pallas_call | solution.py:384
  246.2 11.7 %expert_step.13 = (bf16[160,1536]{1,0:T(8,128)(2,1)S(1)}, bf16[160,1536]{1,0:T(8,128)(2,1)S(1)}, bf16[160,1536]{1,0:T(8,128)(2,1)S(1)}, bf16[160,1536]{1,0:T(8,1...) custom-call(s32[3]{0:T(128)S(1)} %get-tuple-element.514.at_ref, ...), custom_call_target="tpu_custom_call", output_to_operand_aliasing={{5}: (13, {}), {6}: (14, {}), {7}: (15, {}), {8}: (16, {}),... | custom-call | flops 6039797760 | bytes 14352384 | tf_op jit(solution)/shard_map/expert_step/pallas_call | solution.py:384
  267.8 11.7 %expert_step.14 = (bf16[160,1536]{1,0:T(8,128)(2,1)S(1)}, bf16[160,1536]{1,0:T(8,128)(2,1)S(1)}, bf16[160,1536]{1,0:T(8,128)(2,1)S(1)}, bf16[160,1536]{1,0:T(8,1...) custom-call(s32[3]{0:T(128)S(1)} %get-tuple-element.513.at_ref, ...), custom_call_target="tpu_custom_call", output_to_operand_aliasing={{5}: (13, {}), {6}: (14, {}), {7}: (15, {}), {8}: (16, {}),... | custom-call | flops 6039797760 | bytes 14352384 | tf_op jit(solution)/shard_map/expert_step/pallas_call | solution.py:384
  287.9 11.8 %expert_step.15 = (bf16[160,1536]{1,0:T(8,128)(2,1)S(1)}, bf16[160,1536]{1,0:T(8,128)(2,1)S(1)}, bf16[160,1536]{1,0:T(8,128)(2,1)S(1)}, bf16[160,1536]{1,0:T(8,1...) custom-call(s32[3]{0:T(128)S(1)} %get-tuple-element.512.at_ref, ...), custom_call_target="tpu_custom_call", output_to_operand_aliasing={{5}: (13, {}), {6}: (14, {}), {7}: (15, {}), {8}: (16, {}),... | custom-call | flops 6039797760 | bytes 14352384 | tf_op jit(solution)/shard_map/expert_step/pallas_call | solution.py:384
  334.8 18.8 %expert_grads.2 = (bf16[2,3,1536,128]{3,2,1,0:T(8,128)(2,1)}, bf16[2,3,1536,128]{3,2,1,0:T(8,128)(2,1)}) custom-call(bf16[2,2560,512]{2,1,0:T(8,128)(2,1)} %get-tuple-element.454.act_ref, bf16[2,2560,512]{2,1,0:T(8,128)(2,1)} %get-tuple-element.455.dgate_ref, bf16[2,2560,512]{2,1,0:T(8,128)(2,1)} %get-tuple-element.456.dup_ref, ...), custom_call_target="tpu_custom_call" | custom-call | flops 12079595520 | bytes 9437184 | tf_op jit(solution)/shard_map/expert_grads/pallas_call | solution.py:426
  361.1 7.6 %collective-permute-done.46 = bf16[160,1536]{1,0:T(8,128)(2,1)S(1)} collective-permute-done((bf16[160,1536]{1,0:T(8,128)(2,1)S(1)}, bf16[160,1536]{1,0:T(8,128)(2,1)S(1)}, u32[]{:S(2)}, u32[]{:S(2)}) %collective-permute-start.46) | collective-permute-done | bytes 491552 | tf_op jit(solution)/shard_map/ppermute | solution.py:539
  373.1 22.4 %attend_backward.1 = bf16[1280,640]{1,0:T(8,128)(2,1)S(1)} custom-call(s32[4]{0:T(128)S(1)} %copy-done.46, s32[20]{0:T(128)S(1)} %copy-done.52, bf16[1280,640]{1,0:T(8,128)(2,1)S(1)} %copy-done.58, bf16[320,384]{1,0:T(8,128)(2,1)S(1)} %convolution_convert_fusion.12.refs_0_, bf16[320,384]{1,0:T(8,128)(2,1)S(1)} %convolution_convert_fusion.11.refs_1_, ...), custom_call_target="tpu_custom_call" | custom-call | flops 15099494400 | bytes 4915200 | tf_op jit(solution)/shard_map/attend_backward/pallas_call | solution.py:230
  411.0 8.3 %collective-permute-done.53 = bf16[192,1024]{1,0:T(8,128)(2,1)S(1)} collective-permute-done((bf16[192,1024]{1,0:T(8,128)(2,1)S(1)}, bf16[192,1024]{1,0:T(8,128)(2,1)S(1)}, u32[]{:S(2)}, u32[]{:S(2)}) %collective-permute-start.53) | collective-permute-done | bytes 393248 | tf_op jit(solution)/shard_map/ppermute | solution.py:574
  431.6 18.8 %expert_grads.3 = (bf16[2,3,1536,128]{3,2,1,0:T(8,128)(2,1)}, bf16[2,3,1536,128]{3,2,1,0:T(8,128)(2,1)}) custom-call(bf16[2,2560,512]{2,1,0:T(8,128)(2,1)} %get-tuple-element.454.act_ref, bf16[2,2560,512]{2,1,0:T(8,128)(2,1)} %get-tuple-element.455.dgate_ref, bf16[2,2560,512]{2,1,0:T(8,128)(2,1)} %get-tuple-element.456.dup_ref, ...), custom_call_target="tpu_custom_call" | custom-call | flops 12079595520 | bytes 9437184 | tf_op jit(solution)/shard_map/expert_grads/pallas_call | solution.py:426
  463.7 12.4 %collective-permute-done.65 = f32[18,1536]{1,0:T(8,128)S(1)} collective-permute-done((f32[18,1536]{1,0:T(8,128)S(1)}, f32[18,1536]{1,0:T(8,128)S(1)}, u32[]{:S(2)}, u32[]{:S(2)}) %collective-permute-start.65) | collective-permute-done | bytes 110624 | tf_op jit(solution)/shard_map/ppermute | solution.py:627
  476.7 9.0 %collective-permute-done.63.refs_5_ = bf16[3,1536,128]{2,1,0:T(8,128)(2,1)S(1)} collective-permute-done((bf16[3,1536,128]{2,1,0:T(8,128)(2,1)S(1)}, bf16[3,1536,128]{2,1,0:T(8,128)(2,1)S(1)}, u32[]{:S(2)}, u32[]{:S(2)}) %collective-permute-start.63) | collective-permute-done | bytes 1179680 | tf_op jit(solution)/shard_map/ppermute | solution.py:494
  487.9 14.3 %collective-permute-start.72 = (bf16[384,1024]{1,0:T(8,128)(2,1)S(1)}, bf16[384,1024]{1,0:T(8,128)(2,1)S(1)}, u32[]{:S(2)}, u32[]{:S(2)}) collective-permute-start(bf16[384,1024]{1,0:T(8,128)(2,1)S(1)} %add_convert_fusion.3.refs_0_), channel_id=1, source_target_pairs={{0,8},{4,0},{12,4},{8,12},{24,16},{28,24},{20,28},{16,20},{1,9},{5... | collective-permute-start | bytes 2359304 | tf_op jit(solution)/shard_map/ppermute | solution.py:574
  511.6 8.9 %collective-permute-done.71.refs_1_ = bf16[384,1024]{1,0:T(8,128)(2,1)S(1)} collective-permute-done((bf16[384,1024]{1,0:T(8,128)(2,1)S(1)}, bf16[384,1024]{1,0:T(8,128)(2,1)S(1)}, u32[]{:S(2)}, u32[]{:S(2)}) %collective-permute-start.71) | collective-permute-done | bytes 786464 | tf_op jit(solution)/shard_map/ppermute | solution.py:574
  (510 shorter events, 234.6 us)
Async XLA Ops:
  7.2 148.3 %all-gather.2.cloned.1.call-start = ((), (), s32[]{:S(2)}) async-start(), calls=%async_computation.1 | async-start | bytes 9732096 | tf_op jit(solution)/shard_map/all_gather | solution.py:767
  14.9 26.7 %collective-permute-start = (bf16[336,1536]{1,0:T(8,128)(2,1)S(1)}, bf16[336,1536]{1,0:T(8,128)(2,1)}, u32[]{:S(2)}, u32[]{:S(2)}) collective-permute-start(bf16[336,1536]{1,0:T(8,128)(2,1)S(1)} %pad_maximum_fusion.2.refs_4_), channel_id=1, source_target_pairs={{0,2},{2,0},{1,3},{3,1},{4,6},{6,4},{5,7},{7,5},{8,10},{10,8},{9,1... | collective-permute-start | bytes 3096584 | tf_op jit(solution)/shard_map/ppermute | solution.py:481
  17.8 25.5 %collective-permute-start.1 = (bf16[336,1536]{1,0:T(8,128)(2,1)S(1)}, bf16[336,1536]{1,0:T(8,128)(2,1)}, u32[]{:S(2)}, u32[]{:S(2)}) collective-permute-start(bf16[336,1536]{1,0:T(8,128)(2,1)S(1)} %pad_maximum_fusion.2.refs_4_), channel_id=1, source_target_pairs={{0,1},{1,0},{2,3},{3,2},{4,5},{5,4},{6,7},{7,6},{8,9},{9,8},{10,11... | collective-permute-start | bytes 3096584 | tf_op jit(solution)/shard_map/ppermute | solution.py:482
  21.8 44.2 %collective-permute-start.3 = (bf16[3,1536,128]{2,1,0:T(8,128)(2,1)S(1)}, bf16[3,1536,128]{2,1,0:T(8,128)(2,1)}, u32[]{:S(2)}, u32[]{:S(2)}) collective-permute-start(bf16[3,1536,128]{2,1,0:T(8,128)(2,1)S(1)} %pad_maximum_fusion.refs_0_), channel_id=1, source_target_pairs={{0,2},{2,0},{1,3},{3,1},{4,6},{6,4},{5,7},{7,5},{8,10},{10,8},{9,1... | collective-permute-start | bytes 3538952 | tf_op jit(solution)/shard_map/ppermute | solution.py:481
  75.8 24.1 %collective-permute-start.5 = (bf16[320,1536]{1,0:T(8,128)(2,1)}, bf16[320,1536]{1,0:T(8,128)(2,1)}, u32[]{:S(2)}, u32[]{:S(2)}) collective-permute-start(bf16[320,1536]{1,0:T(8,128)(2,1)} %fusion.36), channel_id=1, source_target_pairs={{0,2},{2,0},{1,3},{3,1},{4,6},{6,4},{5,7},{7,5},{8,10},{10,8},{9,1... | collective-permute-start | bytes 2949128 | tf_op jit(solution)/shard_map/ppermute | solution.py:494
  79.9 50.4 %collective-permute-start.11 = (bf16[3,1536,128]{2,1,0:T(8,128)(2,1)S(1)}, bf16[3,1536,128]{2,1,0:T(8,128)(2,1)}, u32[]{:S(2)}, u32[]{:S(2)}) collective-permute-start(bf16[3,1536,128]{2,1,0:T(8,128)(2,1)S(1)} %pad_maximum_fusion.1.refs_4_), channel_id=1, source_target_pairs={{0,1},{1,0},{2,3},{3,2},{4,5},{5,4},{6,7},{7,6},{8,9},{9,8},{10,11... | collective-permute-start | bytes 3538952 | tf_op jit(solution)/shard_map/ppermute | solution.py:482
  100.0 27.3 %collective-permute-start.10 = (bf16[3,1536,128]{2,1,0:T(8,128)(2,1)S(1)}, bf16[3,1536,128]{2,1,0:T(8,128)(2,1)}, u32[]{:S(2)}, u32[]{:S(2)}) collective-permute-start(bf16[3,1536,128]{2,1,0:T(8,128)(2,1)S(1)} %pad_maximum_fusion.1.refs_4_), channel_id=1, source_target_pairs={{0,2},{2,0},{1,3},{3,1},{4,6},{6,4},{5,7},{7,5},{8,10},{10,8},{9,1... | collective-permute-start | bytes 3538952 | tf_op jit(solution)/shard_map/ppermute | solution.py:481
  130.0 22.5 %collective-permute-start.9 = (bf16[160,1536]{1,0:T(8,128)(2,1)S(1)}, bf16[160,1536]{1,0:T(8,128)(2,1)}, u32[]{:S(2)}, u32[]{:S(2)}) collective-permute-start(bf16[160,1536]{1,0:T(8,128)(2,1)S(1)} %get-tuple-element.538.xb_ref), channel_id=1, source_target_pairs={{0,4},{8,0},{16,8},{24,16},{28,24},{20,28},{12,20},{4,12},{1,5},{9... | collective-permute-start | bytes 1474568 | tf_op jit(solution)/shard_map/ppermute | solution.py:539
  279.8 23.0 %collective-permute-start.33 = (bf16[160,1536]{1,0:T(8,128)(2,1)S(1)}, bf16[160,1536]{1,0:T(8,128)(2,1)S(1)}, u32[]{:S(2)}, u32[]{:S(2)}) collective-permute-start(bf16[160,1536]{1,0:T(8,128)(2,1)S(1)} %add_convert_fusion.19), channel_id=1, source_target_pairs={{0,8},{8,16},{16,24},{24,28},{28,20},{20,12},{12,4},{4,0},{1,9},{9... | collective-permute-start | bytes 1474568 | tf_op jit(solution)/shard_map/ppermute | solution.py:539
  280.1 22.7 %collective-permute-start.34 = (bf16[160,1536]{1,0:T(8,128)(2,1)S(1)}, bf16[160,1536]{1,0:T(8,128)(2,1)S(1)}, u32[]{:S(2)}, u32[]{:S(2)}) collective-permute-start(bf16[160,1536]{1,0:T(8,128)(2,1)S(1)} %add_convert_fusion.18), channel_id=1, source_target_pairs={{0,4},{8,0},{16,8},{24,16},{28,24},{20,28},{12,20},{4,12},{1,5},{9... | collective-permute-start | bytes 1474568 | tf_op jit(solution)/shard_map/ppermute | solution.py:539
  328.5 25.8 %collective-permute-start.41 = (bf16[320,1536]{1,0:T(8,128)(2,1)S(1)}, bf16[320,1536]{1,0:T(8,128)(2,1)S(1)}, u32[]{:S(2)}, u32[]{:S(2)}) collective-permute-start(bf16[320,1536]{1,0:T(8,128)(2,1)S(1)} %get-tuple-element.407), channel_id=1, source_target_pairs={{0,2},{2,0},{1,3},{3,1},{4,6},{6,4},{5,7},{7,5},{8,10},{10,8},{9,1... | collective-permute-start | bytes 2949128 | tf_op jit(solution)/shard_map/ppermute | solution.py:481
  330.0 28.0 %collective-permute-start.44 = (bf16[320,1536]{1,0:T(8,128)(2,1)S(1)}, bf16[320,1536]{1,0:T(8,128)(2,1)S(1)}, u32[]{:S(2)}, u32[]{:S(2)}) collective-permute-start(bf16[320,1536]{1,0:T(8,128)(2,1)S(1)} %get-tuple-element.407), channel_id=1, source_target_pairs={{0,1},{1,0},{2,3},{3,2},{4,5},{5,4},{6,7},{7,6},{8,9},{9,8},{10,11... | collective-permute-start | bytes 2949128 | tf_op jit(solution)/shard_map/ppermute | solution.py:482
  370.1 28.9 %collective-permute-start.50 = (bf16[160,1536]{1,0:T(8,128)(2,1)S(1)}, bf16[160,1536]{1,0:T(8,128)(2,1)S(1)}, u32[]{:S(2)}, u32[]{:S(2)}) collective-permute-start(bf16[160,1536]{1,0:T(8,128)(2,1)S(1)} %add_convert_fusion.11), channel_id=1, source_target_pairs={{0,8},{8,16},{16,24},{24,28},{28,20},{20,12},{12,4},{4,0},{1,9},{9... | collective-permute-start | bytes 1474568 | tf_op jit(solution)/shard_map/ppermute | solution.py:539
  371.6 27.4 %collective-permute-start.51 = (bf16[160,1536]{1,0:T(8,128)(2,1)S(1)}, bf16[160,1536]{1,0:T(8,128)(2,1)S(1)}, u32[]{:S(2)}, u32[]{:S(2)}) collective-permute-start(bf16[160,1536]{1,0:T(8,128)(2,1)S(1)} %add_convert_fusion.10), channel_id=1, source_target_pairs={{0,4},{8,0},{16,8},{24,16},{28,24},{20,28},{12,20},{4,12},{1,5},{9... | collective-permute-start | bytes 1474568 | tf_op jit(solution)/shard_map/ppermute | solution.py:539
  372.5 26.5 %collective-permute-start.49 = (bf16[3,1536,128]{2,1,0:T(8,128)(2,1)S(1)}, bf16[3,1536,128]{2,1,0:T(8,128)(2,1)S(1)}, u32[]{:S(2)}, u32[]{:S(2)}) collective-permute-start(bf16[3,1536,128]{2,1,0:T(8,128)(2,1)S(1)} %fusion.31), channel_id=1, source_target_pairs={{0,2},{2,0},{1,3},{3,1},{4,6},{6,4},{5,7},{7,5},{8,10},{10,8},{9,1... | collective-permute-start | bytes 3538952 | tf_op jit(solution)/shard_map/ppermute | solution.py:494
  422.5 30.0 %collective-permute-start.60 = (bf16[160,1536]{1,0:T(8,128)(2,1)}, bf16[160,1536]{1,0:T(8,128)(2,1)}, u32[]{:S(2)}, u32[]{:S(2)}) collective-permute-start(bf16[160,1536]{1,0:T(8,128)(2,1)} %add_convert_fusion.7), channel_id=1, source_target_pairs={{0,8},{8,16},{16,24},{24,28},{28,20},{20,12},{12,4},{4,0},{1,9},{9... | collective-permute-start | bytes 1474568 | tf_op jit(solution)/shard_map/ppermute | solution.py:539
  422.6 29.8 %collective-permute-start.61 = (bf16[160,1536]{1,0:T(8,128)(2,1)}, bf16[160,1536]{1,0:T(8,128)(2,1)}, u32[]{:S(2)}, u32[]{:S(2)}) collective-permute-start(bf16[160,1536]{1,0:T(8,128)(2,1)} %add_convert_fusion.6), channel_id=1, source_target_pairs={{0,4},{8,0},{16,8},{24,16},{28,24},{20,28},{12,20},{4,12},{1,5},{9... | collective-permute-start | bytes 1474568 | tf_op jit(solution)/shard_map/ppermute | solution.py:539
  425.6 24.8 %collective-permute-start.56 = (bf16[384,1024]{1,0:T(8,128)(2,1)}, bf16[384,1024]{1,0:T(8,128)(2,1)}, u32[]{:S(2)}, u32[]{:S(2)}) collective-permute-start(bf16[384,1024]{1,0:T(8,128)(2,1)} %fusion.40), channel_id=1, source_target_pairs={{0,4},{4,12},{12,8},{8,0},{24,28},{28,20},{20,16},{16,24},{1,5},{5... | collective-permute-start | bytes 2359304 | tf_op jit(solution)/shard_map/ppermute | solution.py:574
  427.2 23.2 %collective-permute-start.57 = (bf16[384,1024]{1,0:T(8,128)(2,1)}, bf16[384,1024]{1,0:T(8,128)(2,1)}, u32[]{:S(2)}, u32[]{:S(2)}) collective-permute-start(bf16[384,1024]{1,0:T(8,128)(2,1)} %pad_maximum_fusion.3), channel_id=1, source_target_pairs={{0,8},{4,0},{12,4},{8,12},{24,16},{28,24},{20,28},{16,20},{1,9},{5... | collective-permute-start | bytes 2359304 | tf_op jit(solution)/shard_map/ppermute | solution.py:574
  457.6 28.1 %collective-permute-start.63 = (bf16[3,1536,128]{2,1,0:T(8,128)(2,1)S(1)}, bf16[3,1536,128]{2,1,0:T(8,128)(2,1)S(1)}, u32[]{:S(2)}, u32[]{:S(2)}) collective-permute-start(bf16[3,1536,128]{2,1,0:T(8,128)(2,1)S(1)} %fusion.32), channel_id=1, source_target_pairs={{0,2},{2,0},{1,3},{3,1},{4,6},{6,4},{5,7},{7,5},{8,10},{10,8},{9,1... | collective-permute-start | bytes 3538952 | tf_op jit(solution)/shard_map/ppermute | solution.py:494
  460.1 25.6 %collective-permute-start.67 = (bf16[160,1536]{1,0:T(8,128)(2,1)S(1)}, bf16[160,1536]{1,0:T(8,128)(2,1)S(1)}, u32[]{:S(2)}, u32[]{:S(2)}) collective-permute-start(bf16[160,1536]{1,0:T(8,128)(2,1)S(1)} %add_convert_fusion.5), channel_id=1, source_target_pairs={{0,8},{8,16},{16,24},{24,28},{28,20},{20,12},{12,4},{4,0},{1,9},{9... | collective-permute-start | bytes 1474568 | tf_op jit(solution)/shard_map/ppermute | solution.py:539
  460.7 25.8 %collective-permute-start.68 = (bf16[160,1536]{1,0:T(8,128)(2,1)S(1)}, bf16[160,1536]{1,0:T(8,128)(2,1)S(1)}, u32[]{:S(2)}, u32[]{:S(2)}) collective-permute-start(bf16[160,1536]{1,0:T(8,128)(2,1)S(1)} %add_convert_fusion.4), channel_id=1, source_target_pairs={{0,4},{8,0},{16,8},{24,16},{28,24},{20,28},{12,20},{4,12},{1,5},{9... | collective-permute-start | bytes 1474568 | tf_op jit(solution)/shard_map/ppermute | solution.py:539
  486.8 33.7 %collective-permute-start.71 = (bf16[384,1024]{1,0:T(8,128)(2,1)S(1)}, bf16[384,1024]{1,0:T(8,128)(2,1)S(1)}, u32[]{:S(2)}, u32[]{:S(2)}) collective-permute-start(bf16[384,1024]{1,0:T(8,128)(2,1)S(1)} %add_convert_fusion.3.refs_0_), channel_id=1, source_target_pairs={{0,4},{4,12},{12,8},{8,0},{24,28},{28,20},{20,16},{16,24},{1,5},{5... | collective-permute-start | bytes 2359304 | tf_op jit(solution)/shard_map/ppermute | solution.py:574
  487.9 32.7 %collective-permute-start.72 = (bf16[384,1024]{1,0:T(8,128)(2,1)S(1)}, bf16[384,1024]{1,0:T(8,128)(2,1)S(1)}, u32[]{:S(2)}, u32[]{:S(2)}) collective-permute-start(bf16[384,1024]{1,0:T(8,128)(2,1)S(1)} %add_convert_fusion.3.refs_0_), channel_id=1, source_target_pairs={{0,8},{4,0},{12,4},{8,12},{24,16},{28,24},{20,28},{16,20},{1,9},{5... | collective-permute-start | bytes 2359304 | tf_op jit(solution)/shard_map/ppermute | solution.py:574
  (160 other events, 1626.8 us)
Sparse Core Ops, SparseCore 0:
  12.4 137.6 all-gather.1

commit v5 on v4

--- a/solution.py
+++ b/solution.py
@@ -113,7 +113,7 @@
             work(first, g, take(kc), take(vc), [None, own, par], places)
         return carry
 
-    lax.fori_loop(0, (rows - trunk) // QT, body, 0)
+    lax.fori_loop(0, (rows - trunk) // QT, body, 0, unroll=6)
 
 
 def attend_forward_kernel(kv, per_group, seg, blocks, shard_ref, parent_ref, *refs):

time: 556 us -> 552 us (level)
  transfers between devices with their start and end apart: 78 -> 78, of which waited for: 36 -> 34; matrix products, arithmetic and copies ran while one was open for 14% -> 14% of each run, Pallas kernels for 32% -> 32%
where the time goes in v5:
time: 552 us; the launch traced here: 546 us
  Pallas kernels  174 us (32%)
  waiting for transfers between devices  157 us (28%)
  starting transfers between devices  93.2 us (17%)
  other arithmetic  44.3 us (8%)
  local copies, waits for them, and re-layouts  34.5 us (6%)
  matrix products  22 us (4%)
  between operations  19.9 us (4%)
    pallas_call x8, Pallas kernels, expert_step(): pl.pallas_call(functools.partial(expert_kernel, k * rows, blocks, buffers...  94 us
    ppermute x42, waiting for transfers between devices, ring_move(): lax.ppermute(x, 'dp', [(order[i], order[(i + by) % n]) for i in range(n)])  54 us
    ppermute x42, starting transfers between devices, ring_move(): lax.ppermute(x, 'dp', [(order[i], order[(i + by) % n]) for i in range(n)])  45.6 us
    pallas_call x2, Pallas kernels, expert_grads(): pl.pallas_call(expert_grad_kernel, grid=(width // tile,), out_shape=[jax....  37.6 us
    ppermute x4, waiting for transfers between devices, gather(): across = lax.ppermute(x if again is None else again, 'row', swap)  31.8 us
    ppermute x4, waiting for transfers between devices, reduce_second(): return ([mine, came], lax.ppermute(far, 'row', swap))  27.2 us
    ppermute x8, starting transfers between devices, shift(): lax.ppermute(x, 'dp', [(o[i], o[(i + by) % n]) for o in self.orders for i...  23.1 us
    unnamed x224, local copies, waits for them, and re-layouts  21.2 us
  transfers between devices with their start and end apart: 78, of which 34 were waited for; matrix products, arithmetic and copies ran while one was open for 14% of the time, Pallas kernels for 32%

profile of v5, /device:TPU:0, one launch (start us, length us, event | category | flops | bytes accessed | tf_op | source)
XLA Modules:
  0.0 545.7 jit_solution(16841017903480355429)
XLA Ops:
  23.9 17.7 %collective-permute-done.refs_5_ = bf16[336,1536]{1,0:T(8,128)(2,1)} collective-permute-done((bf16[336,1536]{1,0:T(8,128)(2,1)S(1)}, bf16[336,1536]{1,0:T(8,128)(2,1)}, u32[]{:S(2)}, u32[]{:S(2)}) %collective-permute-start) | collective-permute-done | bytes 1032224 | tf_op jit(solution)/shard_map/ppermute | solution.py:481
  49.8 12.8 %attend_forward.1 = (bf16[1280,640]{1,0:T(8,128)(2,1)S(1)}, bf16[1280,384]{1,0:T(8,128)(2,1)S(1)}, bf16[1280,1536]{1,0:T(8,128)(2,1)S(1)}) custom-call(s32[4]{0:T(128)S(1)} %pad_add_fusion.1.shard_ref, s32[20]{0:T(128)S(1)} %select_reduce_fusion.3.parent_ref, bf16[336,640]{1,0:T(8,128)(2,1)S(1)} %convolution_convert_fusion.8.refs_0_, ...), custom_call_target="tpu_custom_call" | custom-call | flops 6039797760 | bytes 3276800 | tf_op jit(solution)/shard_map/attend_forward/pallas_call | solution.py:161
  69.1 5.4 collective-permute-done.4
  83.4 16.7 %collective-permute-done.5 = bf16[320,1536]{1,0:T(8,128)(2,1)} collective-permute-done((bf16[320,1536]{1,0:T(8,128)(2,1)}, bf16[320,1536]{1,0:T(8,128)(2,1)}, u32[]{:S(2)}, u32[]{:S(2)}) %collective-permute-start.5) | collective-permute-done | bytes 983072 | tf_op jit(solution)/shard_map/ppermute | solution.py:494
  116.6 10.9 %collective-permute-done.10.refs_5_ = bf16[3,1536,128]{2,1,0:T(8,128)(2,1)} collective-permute-done((bf16[3,1536,128]{2,1,0:T(8,128)(2,1)S(1)}, bf16[3,1536,128]{2,1,0:T(8,128)(2,1)}, u32[]{:S(2)}, u32[]{:S(2)}) %collective-permute-start.10) | collective-permute-done | bytes 1179680 | tf_op jit(solution)/shard_map/ppermute | solution.py:481
  130.6 12.5 %expert_step.8 = (bf16[160,1536]{1,0:T(8,128)(2,1)S(1)}, bf16[160,1536]{1,0:T(8,128)(2,1)S(1)}, bf16[160,1536]{1,0:T(8,128)(2,1)S(1)}, bf16[160,1536]{1,0:T(8,12...) custom-call(s32[3]{0:T(128)S(1)} %get-tuple-element.518.at_ref, ...), custom_call_target="tpu_custom_call" | custom-call | flops 6039797760 | bytes 14352384 | tf_op jit(solution)/shard_map/expert_step/pallas_call | solution.py:384
  158.2 11.4 %expert_step.9 = (bf16[160,1536]{1,0:T(8,128)(2,1)S(1)}, bf16[160,1536]{1,0:T(8,128)(2,1)S(1)}, bf16[160,1536]{1,0:T(8,128)(2,1)S(1)}, bf16[160,1536]{1,0:T(8,12...) custom-call(s32[3]{0:T(128)S(1)} %copy-done.44, ...), custom_call_target="tpu_custom_call", output_to_operand_aliasing={{5}: (13, {}), {6}: (14, {}), {7}: (15, {}), {8}: (16, {}),... | custom-call | flops 6039797760 | bytes 14352384 | tf_op jit(solution)/shard_map/expert_step/pallas_call | solution.py:384
  175.5 11.4 %expert_step.10 = (bf16[160,1536]{1,0:T(8,128)(2,1)S(1)}, bf16[160,1536]{1,0:T(8,128)(2,1)S(1)}, bf16[160,1536]{1,0:T(8,128)(2,1)S(1)}, bf16[160,1536]{1,0:T(8,1...) custom-call(s32[3]{0:T(128)S(1)} %copy-done.43, ...), custom_call_target="tpu_custom_call", output_to_operand_aliasing={{5}: (13, {}), {6}: (14, {}), {7}: (15, {}), {8}: (16, {}),... | custom-call | flops 6039797760 | bytes 14352384 | tf_op jit(solution)/shard_map/expert_step/pallas_call | solution.py:384
  187.0 7.3 %collective-permute-done.19.xa_ref = bf16[160,1536]{1,0:T(8,128)(2,1)S(1)} collective-permute-done((bf16[160,1536]{1,0:T(8,128)(2,1)}, bf16[160,1536]{1,0:T(8,128)(2,1)S(1)}, u32[]{:S(2)}, u32[]{:S(2)}) %collective-permute-start.19) | collective-permute-done | bytes 491552 | tf_op jit(solution)/shard_map/ppermute | solution.py:539
  200.5 11.7 %expert_step.11 = (bf16[160,1536]{1,0:T(8,128)(2,1)S(1)}, bf16[160,1536]{1,0:T(8,128)(2,1)S(1)}, bf16[160,1536]{1,0:T(8,128)(2,1)S(1)}, bf16[160,1536]{1,0:T(8,1...) custom-call(s32[3]{0:T(128)S(1)} %copy-done.42, ...), custom_call_target="tpu_custom_call", output_to_operand_aliasing={{5}: (13, {}), {6}: (14, {}), {7}: (15, {}), {8}: (16, {}),... | custom-call | flops 6039797760 | bytes 14352384 | tf_op jit(solution)/shard_map/expert_step/pallas_call | solution.py:384
  212.3 5.7 %collective-permute-done.23.xa_ref = bf16[160,1536]{1,0:T(8,128)(2,1)S(1)} collective-permute-done((bf16[160,1536]{1,0:T(8,128)(2,1)S(1)}, bf16[160,1536]{1,0:T(8,128)(2,1)S(1)}, u32[]{:S(2)}, u32[]{:S(2)}) %collective-permute-start.23) | collective-permute-done | bytes 491552 | tf_op jit(solution)/shard_map/ppermute | solution.py:539
  223.3 11.7 %expert_step.12 = (bf16[160,1536]{1,0:T(8,128)(2,1)S(1)}, bf16[160,1536]{1,0:T(8,128)(2,1)S(1)}, bf16[160,1536]{1,0:T(8,128)(2,1)S(1)}, bf16[160,1536]{1,0:T(8,1...) custom-call(s32[3]{0:T(128)S(1)} %get-tuple-element.515.at_ref, ...), custom_call_target="tpu_custom_call", output_to_operand_aliasing={{5}: (13, {}), {6}: (14, {}), {7}: (15, {}), {8}: (16, {}),... | custom-call | flops 6039797760 | bytes 14352384 | tf_op jit(solution)/shard_map/expert_step/pallas_call | solution.py:384
  245.7 11.7 %expert_step.13 = (bf16[160,1536]{1,0:T(8,128)(2,1)S(1)}, bf16[160,1536]{1,0:T(8,128)(2,1)S(1)}, bf16[160,1536]{1,0:T(8,128)(2,1)S(1)}, bf16[160,1536]{1,0:T(8,1...) custom-call(s32[3]{0:T(128)S(1)} %get-tuple-element.514.at_ref, ...), custom_call_target="tpu_custom_call", output_to_operand_aliasing={{5}: (13, {}), {6}: (14, {}), {7}: (15, {}), {8}: (16, {}),... | custom-call | flops 6039797760 | bytes 14352384 | tf_op jit(solution)/shard_map/expert_step/pallas_call | solution.py:384
  267.7 11.7 %expert_step.14 = (bf16[160,1536]{1,0:T(8,128)(2,1)S(1)}, bf16[160,1536]{1,0:T(8,128)(2,1)S(1)}, bf16[160,1536]{1,0:T(8,128)(2,1)S(1)}, bf16[160,1536]{1,0:T(8,1...) custom-call(s32[3]{0:T(128)S(1)} %get-tuple-element.513.at_ref, ...), custom_call_target="tpu_custom_call", output_to_operand_aliasing={{5}: (13, {}), {6}: (14, {}), {7}: (15, {}), {8}: (16, {}),... | custom-call | flops 6039797760 | bytes 14352384 | tf_op jit(solution)/shard_map/expert_step/pallas_call | solution.py:384
  287.7 11.8 %expert_step.15 = (bf16[160,1536]{1,0:T(8,128)(2,1)S(1)}, bf16[160,1536]{1,0:T(8,128)(2,1)S(1)}, bf16[160,1536]{1,0:T(8,128)(2,1)S(1)}, bf16[160,1536]{1,0:T(8,1...) custom-call(s32[3]{0:T(128)S(1)} %get-tuple-element.512.at_ref, ...), custom_call_target="tpu_custom_call", output_to_operand_aliasing={{5}: (13, {}), {6}: (14, {}), {7}: (15, {}), {8}: (16, {}),... | custom-call | flops 6039797760 | bytes 14352384 | tf_op jit(solution)/shard_map/expert_step/pallas_call | solution.py:384
  334.4 18.8 %expert_grads.2 = (bf16[2,3,1536,128]{3,2,1,0:T(8,128)(2,1)}, bf16[2,3,1536,128]{3,2,1,0:T(8,128)(2,1)}) custom-call(bf16[2,2560,512]{2,1,0:T(8,128)(2,1)} %get-tuple-element.454.act_ref, bf16[2,2560,512]{2,1,0:T(8,128)(2,1)} %get-tuple-element.455.dgate_ref, bf16[2,2560,512]{2,1,0:T(8,128)(2,1)} %get-tuple-element.456.dup_ref, ...), custom_call_target="tpu_custom_call" | custom-call | flops 12079595520 | bytes 9437184 | tf_op jit(solution)/shard_map/expert_grads/pallas_call | solution.py:426
  360.7 7.6 %collective-permute-done.46 = bf16[160,1536]{1,0:T(8,128)(2,1)S(1)} collective-permute-done((bf16[160,1536]{1,0:T(8,128)(2,1)S(1)}, bf16[160,1536]{1,0:T(8,128)(2,1)S(1)}, u32[]{:S(2)}, u32[]{:S(2)}) %collective-permute-start.46) | collective-permute-done | bytes 491552 | tf_op jit(solution)/shard_map/ppermute | solution.py:539
  372.7 21.0 %attend_backward.1 = bf16[1280,640]{1,0:T(8,128)(2,1)S(1)} custom-call(s32[4]{0:T(128)S(1)} %copy-done.46, s32[20]{0:T(128)S(1)} %copy-done.52, bf16[1280,640]{1,0:T(8,128)(2,1)S(1)} %copy-done.58, bf16[320,384]{1,0:T(8,128)(2,1)S(1)} %convolution_convert_fusion.12.refs_0_, bf16[320,384]{1,0:T(8,128)(2,1)S(1)} %convolution_convert_fusion.11.refs_1_, ...), custom_call_target="tpu_custom_call" | custom-call | flops 15099494400 | bytes 4915200 | tf_op jit(solution)/shard_map/attend_backward/pallas_call | solution.py:230
  410.7 7.4 %collective-permute-done.53 = bf16[192,1024]{1,0:T(8,128)(2,1)S(1)} collective-permute-done((bf16[192,1024]{1,0:T(8,128)(2,1)S(1)}, bf16[192,1024]{1,0:T(8,128)(2,1)S(1)}, u32[]{:S(2)}, u32[]{:S(2)}) %collective-permute-start.53) | collective-permute-done | bytes 393248 | tf_op jit(solution)/shard_map/ppermute | solution.py:574
  430.0 18.8 %expert_grads.3 = (bf16[2,3,1536,128]{3,2,1,0:T(8,128)(2,1)}, bf16[2,3,1536,128]{3,2,1,0:T(8,128)(2,1)}) custom-call(bf16[2,2560,512]{2,1,0:T(8,128)(2,1)} %get-tuple-element.454.act_ref, bf16[2,2560,512]{2,1,0:T(8,128)(2,1)} %get-tuple-element.455.dgate_ref, bf16[2,2560,512]{2,1,0:T(8,128)(2,1)} %get-tuple-element.456.dup_ref, ...), custom_call_target="tpu_custom_call" | custom-call | flops 12079595520 | bytes 9437184 | tf_op jit(solution)/shard_map/expert_grads/pallas_call | solution.py:426
  461.8 12.8 %collective-permute-done.65 = f32[18,1536]{1,0:T(8,128)S(1)} collective-permute-done((f32[18,1536]{1,0:T(8,128)S(1)}, f32[18,1536]{1,0:T(8,128)S(1)}, u32[]{:S(2)}, u32[]{:S(2)}) %collective-permute-start.65) | collective-permute-done | bytes 110624 | tf_op jit(solution)/shard_map/ppermute | solution.py:627
  475.1 9.1 %collective-permute-done.63.refs_5_ = bf16[3,1536,128]{2,1,0:T(8,128)(2,1)S(1)} collective-permute-done((bf16[3,1536,128]{2,1,0:T(8,128)(2,1)S(1)}, bf16[3,1536,128]{2,1,0:T(8,128)(2,1)S(1)}, u32[]{:S(2)}, u32[]{:S(2)}) %collective-permute-start.63) | collective-permute-done | bytes 1179680 | tf_op jit(solution)/shard_map/ppermute | solution.py:494
  486.2 14.7 %collective-permute-start.72 = (bf16[384,1024]{1,0:T(8,128)(2,1)S(1)}, bf16[384,1024]{1,0:T(8,128)(2,1)S(1)}, u32[]{:S(2)}, u32[]{:S(2)}) collective-permute-start(bf16[384,1024]{1,0:T(8,128)(2,1)S(1)} %add_convert_fusion.3.refs_0_), channel_id=1, source_target_pairs={{0,8},{4,0},{12,4},{8,12},{24,16},{28,24},{20,28},{16,20},{1,9},{5... | collective-permute-start | bytes 2359304 | tf_op jit(solution)/shard_map/ppermute | solution.py:574
  510.4 8.9 %collective-permute-done.71.refs_1_ = bf16[384,1024]{1,0:T(8,128)(2,1)S(1)} collective-permute-done((bf16[384,1024]{1,0:T(8,128)(2,1)S(1)}, bf16[384,1024]{1,0:T(8,128)(2,1)S(1)}, u32[]{:S(2)}, u32[]{:S(2)}) %collective-permute-start.71) | collective-permute-done | bytes 786464 | tf_op jit(solution)/shard_map/ppermute | solution.py:574
  (510 shorter events, 236.2 us)
Async XLA Ops:
  7.2 148.1 %all-gather.2.cloned.1.call-start = ((), (), s32[]{:S(2)}) async-start(), calls=%async_computation.1 | async-start | bytes 9732096 | tf_op jit(solution)/shard_map/all_gather | solution.py:767
  14.9 26.7 %collective-permute-start = (bf16[336,1536]{1,0:T(8,128)(2,1)S(1)}, bf16[336,1536]{1,0:T(8,128)(2,1)}, u32[]{:S(2)}, u32[]{:S(2)}) collective-permute-start(bf16[336,1536]{1,0:T(8,128)(2,1)S(1)} %pad_maximum_fusion.2.refs_4_), channel_id=1, source_target_pairs={{0,2},{2,0},{1,3},{3,1},{4,6},{6,4},{5,7},{7,5},{8,10},{10,8},{9,1... | collective-permute-start | bytes 3096584 | tf_op jit(solution)/shard_map/ppermute | solution.py:481
  17.8 25.5 %collective-permute-start.1 = (bf16[336,1536]{1,0:T(8,128)(2,1)S(1)}, bf16[336,1536]{1,0:T(8,128)(2,1)}, u32[]{:S(2)}, u32[]{:S(2)}) collective-permute-start(bf16[336,1536]{1,0:T(8,128)(2,1)S(1)} %pad_maximum_fusion.2.refs_4_), channel_id=1, source_target_pairs={{0,1},{1,0},{2,3},{3,2},{4,5},{5,4},{6,7},{7,6},{8,9},{9,8},{10,11... | collective-permute-start | bytes 3096584 | tf_op jit(solution)/shard_map/ppermute | solution.py:482
  21.8 44.2 %collective-permute-start.3 = (bf16[3,1536,128]{2,1,0:T(8,128)(2,1)S(1)}, bf16[3,1536,128]{2,1,0:T(8,128)(2,1)}, u32[]{:S(2)}, u32[]{:S(2)}) collective-permute-start(bf16[3,1536,128]{2,1,0:T(8,128)(2,1)S(1)} %pad_maximum_fusion.refs_0_), channel_id=1, source_target_pairs={{0,2},{2,0},{1,3},{3,1},{4,6},{6,4},{5,7},{7,5},{8,10},{10,8},{9,1... | collective-permute-start | bytes 3538952 | tf_op jit(solution)/shard_map/ppermute | solution.py:481
  76.1 24.1 %collective-permute-start.5 = (bf16[320,1536]{1,0:T(8,128)(2,1)}, bf16[320,1536]{1,0:T(8,128)(2,1)}, u32[]{:S(2)}, u32[]{:S(2)}) collective-permute-start(bf16[320,1536]{1,0:T(8,128)(2,1)} %fusion.36), channel_id=1, source_target_pairs={{0,2},{2,0},{1,3},{3,1},{4,6},{6,4},{5,7},{7,5},{8,10},{10,8},{9,1... | collective-permute-start | bytes 2949128 | tf_op jit(solution)/shard_map/ppermute | solution.py:494
  80.1 50.4 %collective-permute-start.11 = (bf16[3,1536,128]{2,1,0:T(8,128)(2,1)S(1)}, bf16[3,1536,128]{2,1,0:T(8,128)(2,1)}, u32[]{:S(2)}, u32[]{:S(2)}) collective-permute-start(bf16[3,1536,128]{2,1,0:T(8,128)(2,1)S(1)} %pad_maximum_fusion.1.refs_4_), channel_id=1, source_target_pairs={{0,1},{1,0},{2,3},{3,2},{4,5},{5,4},{6,7},{7,6},{8,9},{9,8},{10,11... | collective-permute-start | bytes 3538952 | tf_op jit(solution)/shard_map/ppermute | solution.py:482
  100.2 27.3 %collective-permute-start.10 = (bf16[3,1536,128]{2,1,0:T(8,128)(2,1)S(1)}, bf16[3,1536,128]{2,1,0:T(8,128)(2,1)}, u32[]{:S(2)}, u32[]{:S(2)}) collective-permute-start(bf16[3,1536,128]{2,1,0:T(8,128)(2,1)S(1)} %pad_maximum_fusion.1.refs_4_), channel_id=1, source_target_pairs={{0,2},{2,0},{1,3},{3,1},{4,6},{6,4},{5,7},{7,5},{8,10},{10,8},{9,1... | collective-permute-start | bytes 3538952 | tf_op jit(solution)/shard_map/ppermute | solution.py:481
  279.7 22.9 %collective-permute-start.33 = (bf16[160,1536]{1,0:T(8,128)(2,1)S(1)}, bf16[160,1536]{1,0:T(8,128)(2,1)S(1)}, u32[]{:S(2)}, u32[]{:S(2)}) collective-permute-start(bf16[160,1536]{1,0:T(8,128)(2,1)S(1)} %add_convert_fusion.19), channel_id=1, source_target_pairs={{0,8},{8,16},{16,24},{24,28},{28,20},{20,12},{12,4},{4,0},{1,9},{9... | collective-permute-start | bytes 1474568 | tf_op jit(solution)/shard_map/ppermute | solution.py:539
  280.1 22.6 %collective-permute-start.34 = (bf16[160,1536]{1,0:T(8,128)(2,1)S(1)}, bf16[160,1536]{1,0:T(8,128)(2,1)S(1)}, u32[]{:S(2)}, u32[]{:S(2)}) collective-permute-start(bf16[160,1536]{1,0:T(8,128)(2,1)S(1)} %add_convert_fusion.18), channel_id=1, source_target_pairs={{0,4},{8,0},{16,8},{24,16},{28,24},{20,28},{12,20},{4,12},{1,5},{9... | collective-permute-start | bytes 1474568 | tf_op jit(solution)/shard_map/ppermute | solution.py:539
  328.4 25.5 %collective-permute-start.41 = (bf16[320,1536]{1,0:T(8,128)(2,1)S(1)}, bf16[320,1536]{1,0:T(8,128)(2,1)S(1)}, u32[]{:S(2)}, u32[]{:S(2)}) collective-permute-start(bf16[320,1536]{1,0:T(8,128)(2,1)S(1)} %get-tuple-element.407), channel_id=1, source_target_pairs={{0,2},{2,0},{1,3},{3,1},{4,6},{6,4},{5,7},{7,5},{8,10},{10,8},{9,1... | collective-permute-start | bytes 2949128 | tf_op jit(solution)/shard_map/ppermute | solution.py:481
  329.9 27.8 %collective-permute-start.44 = (bf16[320,1536]{1,0:T(8,128)(2,1)S(1)}, bf16[320,1536]{1,0:T(8,128)(2,1)S(1)}, u32[]{:S(2)}, u32[]{:S(2)}) collective-permute-start(bf16[320,1536]{1,0:T(8,128)(2,1)S(1)} %get-tuple-element.407), channel_id=1, source_target_pairs={{0,1},{1,0},{2,3},{3,2},{4,5},{5,4},{6,7},{7,6},{8,9},{9,8},{10,11... | collective-permute-start | bytes 2949128 | tf_op jit(solution)/shard_map/ppermute | solution.py:482
  369.7 28.9 %collective-permute-start.50 = (bf16[160,1536]{1,0:T(8,128)(2,1)S(1)}, bf16[160,1536]{1,0:T(8,128)(2,1)S(1)}, u32[]{:S(2)}, u32[]{:S(2)}) collective-permute-start(bf16[160,1536]{1,0:T(8,128)(2,1)S(1)} %add_convert_fusion.11), channel_id=1, source_target_pairs={{0,8},{8,16},{16,24},{24,28},{28,20},{20,12},{12,4},{4,0},{1,9},{9... | collective-permute-start | bytes 1474568 | tf_op jit(solution)/shard_map/ppermute | solution.py:539
  371.2 27.4 %collective-permute-start.51 = (bf16[160,1536]{1,0:T(8,128)(2,1)S(1)}, bf16[160,1536]{1,0:T(8,128)(2,1)S(1)}, u32[]{:S(2)}, u32[]{:S(2)}) collective-permute-start(bf16[160,1536]{1,0:T(8,128)(2,1)S(1)} %add_convert_fusion.10), channel_id=1, source_target_pairs={{0,4},{8,0},{16,8},{24,16},{28,24},{20,28},{12,20},{4,12},{1,5},{9... | collective-permute-start | bytes 1474568 | tf_op jit(solution)/shard_map/ppermute | solution.py:539
  372.1 26.5 %collective-permute-start.49 = (bf16[3,1536,128]{2,1,0:T(8,128)(2,1)S(1)}, bf16[3,1536,128]{2,1,0:T(8,128)(2,1)S(1)}, u32[]{:S(2)}, u32[]{:S(2)}) collective-permute-start(bf16[3,1536,128]{2,1,0:T(8,128)(2,1)S(1)} %fusion.31), channel_id=1, source_target_pairs={{0,2},{2,0},{1,3},{3,1},{4,6},{6,4},{5,7},{7,5},{8,10},{10,8},{9,1... | collective-permute-start | bytes 3538952 | tf_op jit(solution)/shard_map/ppermute | solution.py:494
  421.5 29.3 %collective-permute-start.60 = (bf16[160,1536]{1,0:T(8,128)(2,1)}, bf16[160,1536]{1,0:T(8,128)(2,1)}, u32[]{:S(2)}, u32[]{:S(2)}) collective-permute-start(bf16[160,1536]{1,0:T(8,128)(2,1)} %add_convert_fusion.7), channel_id=1, source_target_pairs={{0,8},{8,16},{16,24},{24,28},{28,20},{20,12},{12,4},{4,0},{1,9},{9... | collective-permute-start | bytes 1474568 | tf_op jit(solution)/shard_map/ppermute | solution.py:539
  421.5 29.3 %collective-permute-start.61 = (bf16[160,1536]{1,0:T(8,128)(2,1)}, bf16[160,1536]{1,0:T(8,128)(2,1)}, u32[]{:S(2)}, u32[]{:S(2)}) collective-permute-start(bf16[160,1536]{1,0:T(8,128)(2,1)} %add_convert_fusion.6), channel_id=1, source_target_pairs={{0,4},{8,0},{16,8},{24,16},{28,24},{20,28},{12,20},{4,12},{1,5},{9... | collective-permute-start | bytes 1474568 | tf_op jit(solution)/shard_map/ppermute | solution.py:539
  424.6 24.2 %collective-permute-start.56 = (bf16[384,1024]{1,0:T(8,128)(2,1)}, bf16[384,1024]{1,0:T(8,128)(2,1)}, u32[]{:S(2)}, u32[]{:S(2)}) collective-permute-start(bf16[384,1024]{1,0:T(8,128)(2,1)} %fusion.40), channel_id=1, source_target_pairs={{0,4},{4,12},{12,8},{8,0},{24,28},{28,20},{20,16},{16,24},{1,5},{5... | collective-permute-start | bytes 2359304 | tf_op jit(solution)/shard_map/ppermute | solution.py:574
  426.2 22.6 %collective-permute-start.57 = (bf16[384,1024]{1,0:T(8,128)(2,1)}, bf16[384,1024]{1,0:T(8,128)(2,1)}, u32[]{:S(2)}, u32[]{:S(2)}) collective-permute-start(bf16[384,1024]{1,0:T(8,128)(2,1)} %pad_maximum_fusion.3), channel_id=1, source_target_pairs={{0,8},{4,0},{12,4},{8,12},{24,16},{28,24},{20,28},{16,20},{1,9},{5... | collective-permute-start | bytes 2359304 | tf_op jit(solution)/shard_map/ppermute | solution.py:574
  452.8 22.3 %collective-permute-start.66 = (bf16[384,1024]{1,0:T(8,128)(2,1)S(1)}, bf16[384,1024]{1,0:T(8,128)(2,1)S(1)}, u32[]{:S(2)}, u32[]{:S(2)}) collective-permute-start(bf16[384,1024]{1,0:T(8,128)(2,1)S(1)} %add_add_fusion), channel_id=1, source_target_pairs={{0,24},{4,28},{8,16},{12,20},{16,8},{20,12},{24,0},{28,4},{1,25},{... | collective-permute-start | bytes 2359304 | tf_op jit(solution)/shard_map/ppermute | solution.py:664
  456.4 27.7 %collective-permute-start.63 = (bf16[3,1536,128]{2,1,0:T(8,128)(2,1)S(1)}, bf16[3,1536,128]{2,1,0:T(8,128)(2,1)S(1)}, u32[]{:S(2)}, u32[]{:S(2)}) collective-permute-start(bf16[3,1536,128]{2,1,0:T(8,128)(2,1)S(1)} %fusion.32), channel_id=1, source_target_pairs={{0,2},{2,0},{1,3},{3,1},{4,6},{6,4},{5,7},{7,5},{8,10},{10,8},{9,1... | collective-permute-start | bytes 3538952 | tf_op jit(solution)/shard_map/ppermute | solution.py:494
  458.5 25.6 %collective-permute-start.67 = (bf16[160,1536]{1,0:T(8,128)(2,1)S(1)}, bf16[160,1536]{1,0:T(8,128)(2,1)S(1)}, u32[]{:S(2)}, u32[]{:S(2)}) collective-permute-start(bf16[160,1536]{1,0:T(8,128)(2,1)S(1)} %add_convert_fusion.5), channel_id=1, source_target_pairs={{0,8},{8,16},{16,24},{24,28},{28,20},{20,12},{12,4},{4,0},{1,9},{9... | collective-permute-start | bytes 1474568 | tf_op jit(solution)/shard_map/ppermute | solution.py:539
  459.1 25.8 %collective-permute-start.68 = (bf16[160,1536]{1,0:T(8,128)(2,1)S(1)}, bf16[160,1536]{1,0:T(8,128)(2,1)S(1)}, u32[]{:S(2)}, u32[]{:S(2)}) collective-permute-start(bf16[160,1536]{1,0:T(8,128)(2,1)S(1)} %add_convert_fusion.4), channel_id=1, source_target_pairs={{0,4},{8,0},{16,8},{24,16},{28,24},{20,28},{12,20},{4,12},{1,5},{9... | collective-permute-start | bytes 1474568 | tf_op jit(solution)/shard_map/ppermute | solution.py:539
  485.2 34.1 %collective-permute-start.71 = (bf16[384,1024]{1,0:T(8,128)(2,1)S(1)}, bf16[384,1024]{1,0:T(8,128)(2,1)S(1)}, u32[]{:S(2)}, u32[]{:S(2)}) collective-permute-start(bf16[384,1024]{1,0:T(8,128)(2,1)S(1)} %add_convert_fusion.3.refs_0_), channel_id=1, source_target_pairs={{0,4},{4,12},{12,8},{8,0},{24,28},{28,20},{20,16},{16,24},{1,5},{5... | collective-permute-start | bytes 2359304 | tf_op jit(solution)/shard_map/ppermute | solution.py:574
  486.2 33.1 %collective-permute-start.72 = (bf16[384,1024]{1,0:T(8,128)(2,1)S(1)}, bf16[384,1024]{1,0:T(8,128)(2,1)S(1)}, u32[]{:S(2)}, u32[]{:S(2)}) collective-permute-start(bf16[384,1024]{1,0:T(8,128)(2,1)S(1)} %add_convert_fusion.3.refs_0_), channel_id=1, source_target_pairs={{0,8},{4,0},{12,4},{8,12},{24,16},{28,24},{20,28},{16,20},{1,9},{5... | collective-permute-start | bytes 2359304 | tf_op jit(solution)/shard_map/ppermute | solution.py:574
  (160 other events, 1627.3 us)
Sparse Core Ops, SparseCore 0:
  12.4 137.4 all-gather.1
